TPU v7x, 32 devices: a whole 2x2x4 slice. The times are simulated.
32 devices in a mesh: dp: 2 (over core), row: 4 (over z), col: 4 (over y, x).
Axes of the slice: x: 2, y: 2, z: 4, core: 2. Of those that a mesh axis runs over, the one named last changes fastest.
Arguments:
- tokens: bfloat16 [16384, 1024], P(('dp', 'row', 'col')), may hold values from -6 to 6
- segment_ids: int32 [16, 1024], P(('dp', 'row')), may hold values from 0 to 2, never falling along the last dimension, each value on 1 to 512 neighbouring positions
- in_weight: bfloat16 [1024, 3072], P('row', 'col'), may hold values from -0.1875 to 0.1875
- in_bias: float32 [2048], P('col'), may hold values from -3 to 3
- out_weight: bfloat16 [1024, 1024], P('col', 'row'), may hold values from -3 to 3
- out_bias: float32 [1024], replicated, may hold values from -3 to 3
- gain_one: float32 [1024], replicated, may hold values from 0.25 to 1.75
- shift_one: float32 [1024], replicated, may hold values from -3 to 3
- up_weight: bfloat16 [1024, 4096], P('row', 'col'), may hold values from -0.1875 to 0.1875
- up_bias: float32 [4096], P('col'), may hold values from -3 to 3
- down_weight: bfloat16 [4096, 1024], P('col', 'row'), may hold values from -0.09375 to 0.09375
- down_bias: float32 [1024], replicated, may hold values from -3 to 3
- gain_two: float32 [1024], replicated, may hold values from 0.25 to 1.75
- shift_two: float32 [1024], replicated, may hold values from -3 to 3
- cotangent: bfloat16 [16384, 1024], P(('dp', 'row', 'col')), may hold values from -6 to 6
Outputs:
- output: bfloat16 [16384, 1024], P(('dp', 'row', 'col'))
- grad_tokens: float32 [16384, 1024], P(('dp', 'row', 'col'))
- grad_in_weight: float32 [1024, 3072], P('row', 'col')
- grad_in_bias: float32 [2048], P('col')
- grad_out_weight: float32 [1024, 1024], P('col', 'row')
- grad_out_bias: float32 [1024], replicated
- grad_gain_one: float32 [1024], replicated
- grad_shift_one: float32 [1024], replicated
- grad_up_weight: float32 [1024, 4096], P('row', 'col')
- grad_up_bias: float32 [4096], P('col')
- grad_down_weight: float32 [4096, 1024], P('col', 'row')
- grad_down_bias: float32 [1024], replicated
- grad_gain_two: float32 [1024], replicated
- grad_shift_two: float32 [1024], replicated
Inputs may be any that keep to these rules, and one draw needn't show every extreme that they name: `segment_ids`: along each sequence the ids never fall; each sequence holds 3 documents of 1 to 512 tokens, one of exactly 512.
All inputs are finite; a program needn't handle non-finite values.
Results may differ from a plain program's by a relative error of at most 0.02.
Values may be sent and summed in bfloat16 or wider, within the bound.
No kernel may reach another device: no remote copies, remote signals or barrier semaphores. Data moves between devices by JAX's collectives and lax.ppermute only.
A program may use at most 128 MiB of HBM per device.

v0:
```python
from functools import partial

import jax
import jax.numpy as jnp
from jax import lax
from jax.sharding import PartitionSpec as P

HD = 64


NORM_EPSILON = 1e-12


def col_tokens(value):
    return lax.all_gather(value, "col", axis=0, tiled=True)


def col_total(value):
    return lax.psum_scatter(
        value.astype(jnp.bfloat16), "col", scatter_dimension=0, tiled=True
    ).astype(jnp.float32)


def norm_forward(hidden, gain, shift):
    row_mean = jnp.mean(hidden, axis=1, keepdims=True)
    variance = jnp.mean(hidden * hidden, axis=1, keepdims=True) - row_mean * row_mean
    inverse = lax.rsqrt(variance + NORM_EPSILON)
    normed = (hidden - row_mean) * inverse
    return (normed * gain + shift, normed, inverse)


def norm_backward(grad_after, normed, inverse, gain):
    grad_normed = grad_after * gain
    mean_one = jnp.mean(grad_normed, axis=1, keepdims=True)
    mean_two = jnp.mean(grad_normed * normed, axis=1, keepdims=True)
    return inverse * (grad_normed - mean_one - normed * mean_two)


def score_block(queries, key_rows, query_ids, key_ids):
    scores = jnp.einsum(
        "qhe,khe->hqk", queries, key_rows, preferred_element_type=jnp.float32
    ) * HD ** (-0.5)
    same_doc = query_ids[:, None] == key_ids[None, :]
    return jnp.where(same_doc[None], scores, -1000000000.0)


def attend_forward(packed):
    queries, key_rows, value_rows, doc_ids = packed
    length, heads_here = (queries.shape[0], queries.shape[1])
    block_rows = min(512, length)
    block_count = length // block_rows

    def one_block(piece):
        block_queries, block_ids = piece
        scores = score_block(block_queries, key_rows, block_ids, doc_ids)
        row_top = jnp.max(scores, axis=2, keepdims=True)
        exp_terms = jnp.exp(scores - row_top)
        row_total = jnp.sum(exp_terms, axis=2, keepdims=True)
        attn_probs = (exp_terms / row_total).astype(jnp.bfloat16)
        result = jnp.einsum(
            "hqk,khe->qhe", attn_probs, value_rows, preferred_element_type=jnp.float32
        )
        return (result.astype(jnp.bfloat16), (row_top + jnp.log(row_total))[:, :, 0])

    results, log_totals = lax.map(
        one_block,
        (
            queries.reshape(block_count, block_rows, heads_here, HD),
            doc_ids.reshape(block_count, block_rows),
        ),
    )
    return (results.reshape(length, heads_here, HD), log_totals)


def attend_backward(packed):
    queries, key_rows, value_rows, doc_ids, grad_rows, log_totals = packed
    length, heads_here = (queries.shape[0], queries.shape[1])
    block_count = log_totals.shape[0]
    block_rows = length // block_count
    factor = HD ** (-0.5)

    def one_block(running, piece):
        key_grad, value_grad = running
        block_queries, block_ids, block_grads, block_logs = piece
        scores = score_block(block_queries, key_rows, block_ids, doc_ids)
        attn_probs = jnp.exp(scores - block_logs[:, :, None])
        rounded = attn_probs.astype(jnp.bfloat16)
        prob_grads = jnp.einsum(
            "qhe,khe->hqk", block_grads, value_rows, preferred_element_type=jnp.float32
        )
        inner = jnp.sum(attn_probs * prob_grads, axis=2, keepdims=True)
        score_grads = (attn_probs * (prob_grads - inner)).astype(jnp.bfloat16)
        query_grad = (
            jnp.einsum("hqk,khe->qhe", score_grads, key_rows, preferred_element_type=jnp.float32)
            * factor
        )
        key_grad = (
            key_grad
            + jnp.einsum(
                "hqk,qhe->khe", score_grads, block_queries, preferred_element_type=jnp.float32
            )
            * factor
        )
        value_grad = value_grad + jnp.einsum(
            "hqk,qhe->khe", rounded, block_grads, preferred_element_type=jnp.float32
        )
        return ((key_grad, value_grad), query_grad)

    empty = jnp.zeros((length, heads_here, HD), jnp.float32)
    pieces = (
        queries.reshape(block_count, block_rows, heads_here, HD),
        doc_ids.reshape(block_count, block_rows),
        grad_rows.reshape(block_count, block_rows, heads_here, HD),
        log_totals,
    )
    (key_grad, value_grad), query_grad = lax.scan(one_block, (empty, empty), pieces)
    return (query_grad.reshape(length, heads_here, HD), key_grad, value_grad)


def on_device(
    tokens,
    segment_ids,
    in_weight,
    in_bias,
    out_weight,
    out_bias,
    gain_one,
    shift_one,
    up_weight,
    up_bias,
    down_weight,
    down_bias,
    gain_two,
    shift_two,
    cotangent,
):
    seq_here, length = segment_ids.shape
    heads_here = in_weight.shape[1] // (3 * HD)
    in_full, out_rows, up_full, down_rows = (
        lax.all_gather(in_weight, "row", axis=0, tiled=True),
        lax.all_gather(out_weight, "row", axis=1, tiled=True),
        lax.all_gather(up_weight, "row", axis=0, tiled=True),
        lax.all_gather(down_weight, "row", axis=1, tiled=True),
    )
    token_full = col_tokens(tokens)
    row_count = token_full.shape[0]
    projected = jnp.dot(token_full, in_full, preferred_element_type=jnp.float32).reshape(
        row_count, heads_here, 3, HD
    )
    bias_rows = in_bias.reshape(heads_here, 2, HD)
    no_bias = jnp.zeros((heads_here, 1, HD), jnp.float32)
    projected = projected + jnp.concatenate([bias_rows[:, :1], no_bias, bias_rows[:, 1:]], axis=1)
    projected = projected.astype(jnp.bfloat16).reshape(seq_here, length, heads_here, 3, HD)
    queries = projected[:, :, :, 0]
    key_rows = projected[:, :, :, 1]
    value_rows = projected[:, :, :, 2]
    attended, log_totals = lax.map(attend_forward, (queries, key_rows, value_rows, segment_ids))
    attended = attended.reshape(row_count, heads_here * HD)
    branch = lax.psum_scatter(
        jnp.dot(attended, out_rows, preferred_element_type=jnp.float32).astype(jnp.bfloat16),
        "col",
        scatter_dimension=0,
        tiled=True,
    ).astype(jnp.float32)
    residual_one = tokens.astype(jnp.float32) + (branch + out_bias)
    normed_one, unit_one, inverse_one = norm_forward(residual_one, gain_one, shift_one)
    mid_full = col_tokens(normed_one.astype(jnp.bfloat16))
    hidden_pre = jnp.dot(mid_full, up_full, preferred_element_type=jnp.float32) + up_bias
    hidden, gelu_back = jax.vjp(partial(jax.nn.gelu, approximate=False), hidden_pre)
    hidden = hidden.astype(jnp.bfloat16)
    residual_two = normed_one + (
        col_total(jnp.dot(hidden, down_rows, preferred_element_type=jnp.float32)) + down_bias
    )
    normed_two, unit_two, inverse_two = norm_forward(residual_two, gain_two, shift_two)
    output = normed_two.astype(jnp.bfloat16)
    grad_top = cotangent.astype(jnp.float32)
    grad_gain_two = jnp.sum(grad_top * unit_two, axis=0)
    grad_shift_two = jnp.sum(grad_top, axis=0)
    grad_two = norm_backward(grad_top, unit_two, inverse_two, gain_two)
    grad_two_low = grad_two.astype(jnp.bfloat16)
    grad_down_bias = jnp.sum(grad_two_low.astype(jnp.float32), axis=0)
    grad_two_full = col_tokens(grad_two_low)
    grad_down = jnp.dot(hidden.T, grad_two_full, preferred_element_type=jnp.float32)
    grad_hidden = jnp.dot(grad_two_full, down_rows.T, preferred_element_type=jnp.float32)
    grad_pre = gelu_back(grad_hidden)[0].astype(jnp.bfloat16)
    grad_up_bias = jnp.sum(grad_pre.astype(jnp.float32), axis=0)
    grad_up = jnp.dot(mid_full.T, grad_pre, preferred_element_type=jnp.float32)
    grad_one = grad_two + col_total(
        jnp.dot(grad_pre, up_full.T, preferred_element_type=jnp.float32)
    )
    grad_gain_one = jnp.sum(grad_one * unit_one, axis=0)
    grad_shift_one = jnp.sum(grad_one, axis=0)
    grad_first = norm_backward(grad_one, unit_one, inverse_one, gain_one)
    grad_first_low = grad_first.astype(jnp.bfloat16)
    grad_out_bias = jnp.sum(grad_first_low.astype(jnp.float32), axis=0)
    grad_first_full = col_tokens(grad_first_low)
    grad_out = jnp.dot(attended.T, grad_first_full, preferred_element_type=jnp.float32)
    grad_attended = jnp.dot(grad_first_full, out_rows.T, preferred_element_type=jnp.float32).astype(
        jnp.bfloat16
    )
    grad_attended = grad_attended.reshape(seq_here, length, heads_here, HD)
    query_grad, key_grad, value_grad = lax.map(
        attend_backward, (queries, key_rows, value_rows, segment_ids, grad_attended, log_totals)
    )
    grad_projected = (
        jnp.stack([query_grad, key_grad, value_grad], axis=3)
        .reshape(row_count, 3 * heads_here * HD)
        .astype(jnp.bfloat16)
    )
    bias_terms = jnp.sum(grad_projected.astype(jnp.float32), axis=0).reshape(heads_here, 3, HD)
    grad_in_bias = jnp.stack([bias_terms[:, 0], bias_terms[:, 2]], axis=1).reshape(
        2 * heads_here * HD
    )
    grad_in = jnp.dot(token_full.T, grad_projected, preferred_element_type=jnp.float32)
    grad_tokens = grad_first + col_total(
        jnp.dot(grad_projected, in_full.T, preferred_element_type=jnp.float32)
    )
    grad_in, grad_out, grad_up, grad_down = (
        lax.psum_scatter(
            grad_in.astype(jnp.bfloat16), "row", scatter_dimension=0, tiled=True
        ).astype(jnp.float32),
        lax.psum_scatter(
            grad_out.astype(jnp.bfloat16), "row", scatter_dimension=1, tiled=True
        ).astype(jnp.float32),
        lax.psum_scatter(
            grad_up.astype(jnp.bfloat16), "row", scatter_dimension=0, tiled=True
        ).astype(jnp.float32),
        lax.psum_scatter(
            grad_down.astype(jnp.bfloat16), "row", scatter_dimension=1, tiled=True
        ).astype(jnp.float32),
    )
    grad_in, grad_out, grad_up, grad_down = (
        lax.psum(grad_in.astype(jnp.bfloat16), "dp").astype(jnp.float32),
        lax.psum(grad_out.astype(jnp.bfloat16), "dp").astype(jnp.float32),
        lax.psum(grad_up.astype(jnp.bfloat16), "dp").astype(jnp.float32),
        lax.psum(grad_down.astype(jnp.bfloat16), "dp").astype(jnp.float32),
    )
    grad_in_bias, grad_up_bias = lax.psum((grad_in_bias, grad_up_bias), ("dp", "row"))
    full_sums = lax.psum(
        (
            grad_out_bias,
            grad_gain_one,
            grad_shift_one,
            grad_down_bias,
            grad_gain_two,
            grad_shift_two,
        ),
        ("dp", "row", "col"),
    )
    return (
        output,
        grad_tokens,
        grad_in,
        grad_in_bias,
        grad_out,
        full_sums[0],
        full_sums[1],
        full_sums[2],
        grad_up,
        grad_up_bias,
        grad_down,
        full_sums[3],
        full_sums[4],
        full_sums[5],
    )


def solution(mesh):
    return jax.shard_map(
        on_device,
        mesh=mesh,
        in_specs=(
            P(("dp", "row", "col"), None),
            P(("dp", "row"), None),
            P("row", "col"),
            P("col"),
            P("col", "row"),
            P(),
            P(),
            P(),
            P("row", "col"),
            P("col"),
            P("col", "row"),
            P(),
            P(),
            P(),
            P(("dp", "row", "col"), None),
        ),
        out_specs=(
            P(("dp", "row", "col"), None),
            P(("dp", "row", "col"), None),
            P("row", "col"),
            P("col"),
            P("col", "row"),
            P(),
            P(),
            P(),
            P("row", "col"),
            P("col"),
            P("col", "row"),
            P(),
            P(),
            P(),
        ),
        check_vma=False,
    )
```

profile of v0, /device:TPU:11, one launch (start us, length us, event | category | flops | bytes accessed | tf_op | source)
XLA Modules:
  0.0 911.1 jit_solution(13218852222439128557)
XLA Ops:
  9.6 16.5 %all_gather.26 = bf16[256,1024]{1,0:T(8,128)(2,1)} all-gather(bf16[256,256]{1,0:T(8,128)(2,1)} %param.27), channel_id=1, replica_groups=mesh['dp'=2,'row'=4,'col'=4] {'row'}, dimensions={1}, use_global_device_ids=true | all-gather | bytes 655360 | tf_op jit(solution)/shard_map/all_gather | solution.py:141
  26.1 24.4 %all-gather.10.cloned.1.call-done = bf16[1024,768]{1,0:T(8,128)(2,1)} async-done(((bf16[256,768]{1,0:T(8,128)(2,1)}), bf16[1024,768]{1,0:T(8,128)(2,1)}) %all-gather.10.cloned.1.call-update) | async-done | bytes 1572880 | tf_op jit(solution)/shard_map/all_gather | solution.py:140
  50.5 54.5 %all-gather.8.cloned.1.call-done = bf16[2048,1024]{1,0:T(8,128)(2,1)} async-done(((bf16[512,1024]{1,0:T(8,128)(2,1)}), bf16[2048,1024]{1,0:T(8,128)(2,1)}) %all-gather.8.cloned.1.call-update) | async-done | bytes 4194320 | tf_op jit(solution)/shard_map/all_gather | solution.py:15
  105.0 8.8 fusion.66
  113.8 9.3 %reshape.220 = f32[2,1024,4,3,64]{1,0,4,3,2:T(2,128)} reshape(f32[2048,768]{0,1:T(8,128)} %fusion.66) | data formatting | bytes 12582912 | tf_op jit(solution)/shard_map/reshape | solution.py:147
  123.2 5.1 add_convert_fusion.1
  133.3 41.8 %while.54 = (s32[]{:T(128)}, bf16[2,1024,4,64]{3,2,1,0:T(4,128)(2,1)}, f32[2,2,4,512]{3,2,1,0:T(4,128)S(1)}, bf16[2,1024,4,64]{1,3,2,0:T(8,128)(2,1)}, s32[2,102...) while((s32[]{:T(128)}, ...), condition=%wide.region_5.6_spmd, body=%wide.region_0.5_spmd.sunk | while | flops 562690048 | bytes 36830012 | solution.py:157
  137.2 15.0 %while.57 = (s32[]{:T(128)}, bf16[2,512,4,64]{1,3,2,0:T(8,128)(2,1)S(1)}, f32[2,4,512]{2,1,0:T(4,128)S(1)}, s32[2,512]{1,0:T(2,128)S(1)}, s32[1024]{0:T(1024)S(1...) while((s32[]{:T(128)}, ...), condition=%wide.region_4.4_spmd, body=%wide.region_1.3_spmd.sunk | while | flops 562690048 | bytes 28911724 | solution.py:65
  158.1 15.0 %while.57 = (s32[]{:T(128)}, bf16[2,512,4,64]{1,3,2,0:T(8,128)(2,1)S(1)}, f32[2,4,512]{2,1,0:T(4,128)S(1)}, s32[2,512]{1,0:T(2,128)S(1)}, s32[1024]{0:T(1024)S(1...) while((s32[]{:T(128)}, ...), condition=%wide.region_4.4_spmd, body=%wide.region_1.3_spmd.sunk | while | flops 562690048 | bytes 28911724 | solution.py:65
  184.8 52.1 %reduce-scatter.9.cloned.1.call-done = bf16[512,1024]{1,0:T(8,128)(2,1)} async-done(((bf16[2048,1024]{1,0:T(8,128)(2,1)}), bf16[512,1024]{1,0:T(8,128)(2,1)}) %reduce-scatter.9.cloned.1.call-update) | async-done | bytes 1048592 | tf_op jit(solution)/shard_map/reduce_scatter | solution.py:159
  242.2 40.4 %all-gather.14.cloned.1.call-done = bf16[1024,1024]{1,0:T(8,128)(2,1)} async-done(((bf16[256,1024]{1,0:T(8,128)(2,1)}), bf16[1024,1024]{1,0:T(8,128)(2,1)}) %all-gather.14.cloned.1.call-update) | async-done | bytes 2097168 | tf_op jit(solution)/shard_map/all_gather | solution.py:142
  282.6 55.7 %all-gather.12.cloned.1.call-done = bf16[2048,1024]{1,0:T(8,128)(2,1)} async-done(((bf16[512,1024]{1,0:T(8,128)(2,1)}), bf16[2048,1024]{1,0:T(8,128)(2,1)}) %all-gather.12.cloned.1.call-update) | async-done | bytes 4194320 | tf_op jit(solution)/shard_map/all_gather | solution.py:15
  338.3 26.2 %multiply_convert_fusion.1 = (bf16[2048,1024]{1,0:T(8,128)(2,1)}, f32[2048,1024]{1,0:T(8,128)}, f32[2048,1024]{1,0:T(8,128)}) fusion(f32[1024]{0:T(1024)S(1)} %copy-done.36, bf16[2048,1024]{1,0:T(8,128)(2,1)} %all-gather.12.cloned.1.call-done, bf16[1024,1024]{1,0:T(8,128)(2,1)} %all-gather.14.cloned.1.call-done), kind=kOutput, calls=%fused_computation.70 | convolution fusion | flops 4433379328 | bytes 27267072 | tf_op jit(solution)/shard_map/dot_general | solution.py:168
  364.6 18.8 %all-gather.16.cloned.1.call-done = bf16[1024,1024]{1,0:T(8,128)(2,1)} async-done(((bf16[1024,256]{1,0:T(8,128)(2,1)}), bf16[1024,1024]{1,0:T(8,128)(2,1)}) %all-gather.16.cloned.1.call-update) | async-done | bytes 2097168 | tf_op jit(solution)/shard_map/all_gather | solution.py:143
  383.4 9.3 %convolution_convert_fusion.3 = bf16[2048,1024]{1,0:T(8,128)(2,1)} fusion(bf16[2048,1024]{1,0:T(8,128)(2,1)} %get-tuple-element.534, bf16[1024,1024]{1,0:T(8,128)(2,1)} %all-gather.16.cloned.1.call-done), kind=kOutput, calls=%fused_computation.90 | convolution fusion | flops 4297064448 | bytes 10485760 | tf_op jit(solution)/shard_map/dot_general | solution.py:172
  393.2 53.2 %reduce-scatter.11.cloned.1.call-done = bf16[512,1024]{1,0:T(8,128)(2,1)} async-done(((bf16[2048,1024]{1,0:T(8,128)(2,1)}), bf16[512,1024]{1,0:T(8,128)(2,1)}) %reduce-scatter.11.cloned.1.call-update) | async-done | bytes 1048592 | tf_op jit(solution)/shard_map/reduce_scatter | solution.py:19
  454.1 52.9 %all-gather.18.cloned.1.call-done = bf16[2048,1024]{1,0:T(8,128)(2,1)} async-done(((bf16[512,1024]{1,0:T(8,128)(2,1)}), bf16[2048,1024]{1,0:T(8,128)(2,1)}) %all-gather.18.cloned.1.call-update) | async-done | bytes 4194320 | tf_op jit(solution)/shard_map/all_gather | solution.py:15
  507.0 14.0 %convert_reduce_fusion = (f32[1024]{0:T(1024)}, bf16[2048,1024]{1,0:T(8,128)(2,1)S(1)}) fusion(f32[2048,1024]{1,0:T(8,128)} %get-tuple-element.535, f32[2048,1024]{1,0:T(8,128)} %get-tuple-element.556, f32[1024]{0:T(1024)S(1)} %copy-done.36, bf16[2048,1024]{1,0:T(8,128)(2,1)} %all-gather.18.cloned.1.call-done, ...), kind=kOutput, calls=%fused_computation.68 | convolution fusion | flops 4330617856 | bytes 27271168 | tf_op jit(solution)/shard_map/dot_general | solution.py:184
  523.0 6.3 convolution_convert_fusion.2
  529.3 52.7 %reduce-scatter.13.cloned.1.call-done = bf16[512,1024]{1,0:T(8,128)(2,1)} async-done(((bf16[2048,1024]{1,0:T(8,128)(2,1)}), bf16[512,1024]{1,0:T(8,128)(2,1)}) %reduce-scatter.13.cloned.1.call-update) | async-done | bytes 1048592 | tf_op jit(solution)/shard_map/reduce_scatter | solution.py:19
  589.4 9.4 %convolution_convert_fusion.5 = bf16[1024,1024]{1,0:T(8,128)(2,1)} fusion(bf16[2048,1024]{1,0:T(8,128)(2,1)} %get-tuple-element.534, bf16[2048,1024]{1,0:T(8,128)(2,1)} %all-gather.18.cloned.1.call-done), kind=kOutput, calls=%fused_computation.117 | convolution fusion | flops 4296015872 | bytes 10485760 | tf_op jit(solution)/shard_map/dot_general | solution.py:183
  598.9 9.7 %convolution_convert_fusion.6 = bf16[1024,1024]{1,0:T(8,128)(2,1)} fusion(bf16[2048,1024]{1,0:T(8,128)(2,1)} %all-gather.12.cloned.1.call-done, bf16[2048,1024]{1,0:T(8,128)(2,1)} %copy-done.37), kind=kOutput, calls=%fused_computation.118 | convolution fusion | flops 4296015872 | bytes 10485760 | tf_op jit(solution)/shard_map/dot_general | solution.py:187
  608.6 33.5 %all-gather.20.cloned.1.call-done = bf16[2048,1024]{1,0:T(8,128)(2,1)} async-done(((bf16[512,1024]{1,0:T(8,128)(2,1)}), bf16[2048,1024]{1,0:T(8,128)(2,1)}) %all-gather.20.cloned.1.call-update) | async-done | bytes 4194320 | tf_op jit(solution)/shard_map/all_gather | solution.py:15
  652.5 106.9 %while.56 = (s32[]{:T(128)}, bf16[2,1024,4,64]{1,3,2,0:T(8,128)(2,1)}, bf16[2,1024,4,64]{1,3,2,0:T(8,128)(2,1)}, bf16[2,1024,4,64]{1,3,2,0:T(8,128)(2,1)}, bf16[...) while((s32[]{:T(128)}, ...), condition=%wide.region_21.22_spmd, body=%wide.region_17.21_spmd.sunk | while | flops 1375598592 | bytes 167895136 | solution.py:202
  658.8 41.5 %while.58 = (s32[]{:T(128)}, f32[1024,4,64]{0,2,1:T(8,128)S(1)}, f32[1024,4,64]{0,2,1:T(8,128)}, bf16[2,512,4,64]{1,3,2,0:T(8,128)(2,1)}, bf16[2,512,4,64]{1,3,2...) while((s32[]{:T(128)}, f32[1024,4,64]{0,2,1:T(8,128)S(1)}, ...), condition=%wide.region_20.20_spmd.clone, body=%wide.region_18.19_spmd.clone.sunk | while | flops 1375598592 | bytes 143723280 | solution.py:116
  712.2 41.4 %while.58 = (s32[]{:T(128)}, f32[1024,4,64]{0,2,1:T(8,128)S(1)}, f32[1024,4,64]{0,2,1:T(8,128)}, bf16[2,512,4,64]{1,3,2,0:T(8,128)(2,1)}, bf16[2,512,4,64]{1,3,2...) while((s32[]{:T(128)}, f32[1024,4,64]{0,2,1:T(8,128)S(1)}, ...), condition=%wide.region_20.20_spmd.clone, body=%wide.region_18.19_spmd.clone.sunk | while | flops 1375598592 | bytes 143723280 | solution.py:116
  775.7 6.4 reduce-scatter.19.cloned.1.call-done
  782.1 37.9 %reduce-scatter.17.cloned.1.call-done = bf16[256,768]{0,1:T(8,128)(2,1)} async-done(((bf16[1024,768]{0,1:T(8,128)(2,1)}), bf16[256,768]{0,1:T(8,128)(2,1)}) %reduce-scatter.17.cloned.1.call-update) | async-done | bytes 393232 | tf_op jit(solution)/shard_map/reduce_scatter | solution.py:219
  820.1 7.0 convolution_convert_fusion.1
  827.9 41.5 %all-reduce = (f32[1024]{0:T(1024)}, f32[1024]{0:T(1024)}, f32[1024]{0:T(1024)}, f32[1024]{0:T(1024)}, f32[1024]{0:T(1024)}, /*index=5*/f32[1024]{0:T(1024)}) all-reduce(f32[1024]{0:T(1024)S(1)} %copy-done.29, f32[1024]{0:T(1024)S(1)} %copy-done.27, ...), channel_id=1, replica_groups=mesh['dp'=2,'row'=4,'col'=4] {'dp','row','col'}, use_global_device_ids=true, to_apply=%region_30.31 | all-reduce | flops 6144 | bytes 49152 | tf_op jit(solution)/shard_map/psum | solution.py:239
  869.5 15.7 %all-reduce.1 = (f32[512]{0:T(512)}, f32[1024]{0:T(1024)}) all-reduce(f32[512]{0:T(512)S(1)} %reshape.224, f32[1024]{0:T(1024)S(1)} %copy-done.32), channel_id=1, replica_groups=mesh['dp'=2,'row'=4,'col'=4] {'dp','row'}, use_global_device_ids=true, to_apply=%region_26.27 | all-reduce | flops 1536 | bytes 12288 | tf_op jit(solution)/shard_map/psum | solution.py:238
  892.2 9.1 reduce-scatter.15.cloned.1.call-done
  (305 shorter events, 224.6 us)
Async XLA Ops:
  7.2 43.3 %all-gather.10.cloned.1.call-start = ((), (), s32[]{:S(2)}) async-start(), calls=%async_computation.9 | async-start | bytes 1966080 | tf_op jit(solution)/shard_map/all_gather | solution.py:140
  7.9 97.1 %all-gather.8.cloned.1.call-start = ((), (), s32[]{:S(2)}) async-start(), calls=%async_computation.8 | async-start | bytes 5242880 | tf_op jit(solution)/shard_map/all_gather | solution.py:15
  8.7 228.2 %reduce-scatter.9.cloned.1.call-start = ((), (), s32[]{:S(2)}) async-start(), calls=%async_computation.10 | async-start | bytes 5242880 | tf_op jit(solution)/shard_map/reduce_scatter | solution.py:159
  184.1 52.8 %copy-start.4 = (bf16[512,1024]{1,0:T(8,128)(2,1)S(1)}, bf16[512,1024]{1,0:T(8,128)(2,1)}, u32[]{:S(2)}) copy-start(bf16[512,1024]{1,0:T(8,128)(2,1)} %param.23) | copy-start | bytes 3145732
  184.1 52.8 %copy-start.20 = (f32[1024]{0:T(1024)S(1)}, f32[1024]{0:T(1024)}, u32[]{:S(2)}) copy-start(f32[1024]{0:T(1024)} %param.28) | copy-start | bytes 12292
  184.1 54.6 %copy-start.21 = (f32[1024]{0:T(1024)S(1)}, f32[1024]{0:T(1024)}, u32[]{:S(2)}) copy-start(f32[1024]{0:T(1024)} %param.29) | copy-start | bytes 12292
  184.1 54.6 %copy-start.22 = (f32[1024]{0:T(1024)S(1)}, f32[1024]{0:T(1024)}, u32[]{:S(2)}) copy-start(f32[1024]{0:T(1024)} %param.30) | copy-start | bytes 12292
  184.2 154.2 %copy-start.36 = (f32[1024]{0:T(1024)S(1)}, f32[1024]{0:T(1024)}, u32[]{:S(2)}) copy-start(f32[1024]{0:T(1024)} %param.32) | copy-start | bytes 12292
  184.2 98.4 %all-gather.14.cloned.1.call-start = ((), (), s32[]{:S(2)}) async-start(), calls=%async_computation.12 | async-start | bytes 2621440 | tf_op jit(solution)/shard_map/all_gather | solution.py:142
  184.7 153.6 %all-gather.12.cloned.1.call-start = ((), (), s32[]{:S(2)}) async-start(), calls=%async_computation.11 | async-start | bytes 5242880 | tf_op jit(solution)/shard_map/all_gather | solution.py:15
  241.5 141.8 %all-gather.16.cloned.1.call-start = ((), (), s32[]{:S(2)}) async-start(), calls=%async_computation.13 | async-start | bytes 2621440 | tf_op jit(solution)/shard_map/all_gather | solution.py:143
  242.1 204.3 %reduce-scatter.11.cloned.1.call-start = ((), (), s32[]{:S(2)}) async-start(), calls=%async_computation.14 | async-start | bytes 5242880 | tf_op jit(solution)/shard_map/reduce_scatter | solution.py:19
  392.7 53.7 %copy-start.7 = (bf16[512,1024]{1,0:T(8,128)(2,1)S(1)}, bf16[512,1024]{1,0:T(8,128)(2,1)}, u32[]{:S(2)}) copy-start(bf16[512,1024]{1,0:T(8,128)(2,1)} %reduce-scatter.9.cloned.1.call-done) | copy-start | bytes 3145732
  392.7 53.7 %copy-start.30 = (f32[1024]{0:T(1024)S(1)}, f32[1024]{0:T(1024)}, u32[]{:S(2)}) copy-start(f32[1024]{0:T(1024)} %param.34) | copy-start | bytes 12292
  392.7 56.2 %copy-start.23 = (f32[1024]{0:T(1024)S(1)}, f32[1024]{0:T(1024)}, u32[]{:S(2)}) copy-start(f32[1024]{0:T(1024)} %param.35) | copy-start | bytes 12292
  392.8 57.7 %copy-start.31 = (f32[1024]{0:T(1024)S(1)}, f32[1024]{0:T(1024)}, u32[]{:S(2)}) copy-start(f32[1024]{0:T(1024)} %param.36) | copy-start | bytes 12292
  392.8 114.2 %all-gather.18.cloned.1.call-start = ((), (), s32[]{:S(2)}) async-start(), calls=%async_computation.15 | async-start | bytes 5242880 | tf_op jit(solution)/shard_map/all_gather | solution.py:15
  454.0 128.0 %reduce-scatter.13.cloned.1.call-start = ((), (), s32[]{:S(2)}) async-start(), calls=%async_computation.16 | async-start | bytes 5242880 | tf_op jit(solution)/shard_map/reduce_scatter | solution.py:19
  507.0 16.0 %copy-start.34 = (bf16[1024,1024]{1,0:T(8,128)(2,1)S(1)}, bf16[1024,1024]{1,0:T(8,128)(2,1)}, u32[]{:S(2)}) copy-start(bf16[1024,1024]{1,0:T(8,128)(2,1)} %all-gather.14.cloned.1.call-done) | copy-start | bytes 6291460
  529.3 112.9 %all-gather.20.cloned.1.call-start = ((), (), s32[]{:S(2)}) async-start(), calls=%async_computation.17 | async-start | bytes 5242880 | tf_op jit(solution)/shard_map/all_gather | solution.py:15
  589.2 186.4 %reduce-scatter.23.cloned.1.call-start = ((), (), s32[]{:S(2)}) async-start(), calls=%async_computation.22 | async-start | bytes 2621440 | tf_op jit(solution)/shard_map/reduce_scatter | solution.py:228
  598.8 176.8 %reduce-scatter.21.cloned.1.call-start = ((), (), s32[]{:S(2)}) async-start(), calls=%async_computation.21 | async-start | bytes 2621440 | tf_op jit(solution)/shard_map/reduce_scatter | solution.py:225
  598.9 43.3 %copy-start.14 = (bf16[256,1024]{1,0:T(8,128)(2,1)S(1)}, bf16[256,1024]{1,0:T(8,128)(2,1)}, u32[]{:S(2)}) copy-start(bf16[256,1024]{1,0:T(8,128)(2,1)} %all_gather.26) | copy-start | bytes 1572868
  608.6 173.5 %reduce-scatter.19.cloned.1.call-start = ((), (), s32[]{:S(2)}) async-start(), calls=%async_computation.20 | async-start | bytes 655360 | tf_op jit(solution)/shard_map/reduce_scatter | solution.py:222
  667.4 8.1 copy-start.1
  720.8 8.0 copy-start.1
  764.2 55.8 %reduce-scatter.17.cloned.1.call-start = ((), (), s32[]{:S(2)}) async-start(), calls=%async_computation.19 | async-start | bytes 1966080 | tf_op jit(solution)/shard_map/reduce_scatter | solution.py:219
  770.9 49.2 %copy-start.35 = (bf16[1024,768]{1,0:T(8,128)(2,1)S(1)}, bf16[1024,768]{1,0:T(8,128)(2,1)}, u32[]{:S(2)}) copy-start(bf16[1024,768]{1,0:T(8,128)(2,1)} %all-gather.10.cloned.1.call-done) | copy-start | bytes 4718596
  775.6 109.5 %all-reduce.5.cloned.1.call-start = ((), (), s32[]{:S(2)}) async-start(), calls=%async_computation.23 | async-start | bytes 3145728 | tf_op jit(solution)/shard_map/psum | solution.py:233
  820.0 81.2 %reduce-scatter.15.cloned.1.call-start = ((), (), s32[]{:S(2)}) async-start(), calls=%async_computation.18 | async-start | bytes 5242880 | tf_op jit(solution)/shard_map/reduce_scatter | solution.py:19
  827.1 42.3 %copy-start.32 = (f32[1024]{0:T(1024)S(1)}, f32[1024]{0:T(1024)}, u32[]{:S(2)}) copy-start(f32[1024]{0:T(1024)} %get-tuple-element.529) | copy-start | bytes 12292
  827.2 74.1 %copy-start.9 = (f32[512,1024]{1,0:T(8,128)S(1)}, f32[512,1024]{1,0:T(8,128)}, u32[]{:S(2)}) copy-start(f32[512,1024]{1,0:T(8,128)} %get-tuple-element.528) | copy-start | bytes 6291460
  (36 other events, 123.1 us)
Sparse Core Ops, SparseCore 0:
  9.6 40.8 all-gather.9
  52.3 52.6 all-gather.7
  184.3 52.5 reduce-scatter.8
  238.4 44.1 all-gather.13
  285.0 53.2 all-gather.11
  339.8 43.5 all-gather.15
  392.9 53.5 reduce-scatter.10
  454.2 52.7 all-gather.17
  529.4 52.5 reduce-scatter.12
  589.3 52.7 all-gather.19
  644.5 41.4 reduce-scatter.22
  688.2 43.3 reduce-scatter.20
  764.3 17.7 reduce-scatter.18
  784.3 35.6 reduce-scatter.16
  822.6 22.1 all-reduce.4
  847.6 53.6 reduce-scatter.14
where the time goes:
time: 918 us; the launch traced here: 911 us
  waiting for transfers between devices  494 us (54%)
  matrix products  194 us (21%)
  blocking collectives  73.6 us (8%)
  local copies, waits for them, and re-layouts  72.1 us (8%)
  other arithmetic  60 us (7%)
  between operations  14.8 us (2%)
    all_gather x4, waiting for transfers between devices, col_tokens(): return lax.all_gather(value, 'col', axis=0, tiled=True)  197 us
    reduce_scatter x3, waiting for transfers between devices, col_total(): lax.psum_scatter(value.astype(jnp.bfloat16), 'col', scatter_dimension=0,...  115 us
    reduce_scatter x1, waiting for transfers between devices, on_device(): lax.psum_scatter(jnp.dot(attended, out_rows, preferred_element_type=jnp.f...  52.1 us
    psum x1, blocking collectives, on_device(): lax.psum((grad_out_bias, grad_gain_one, grad_shift_one, grad_down_bias, g...  41.5 us
    all_gather x1, waiting for transfers between devices, on_device(): lax.all_gather(up_weight, 'row', axis=0, tiled=True)  40.4 us
    reduce_scatter x1, waiting for transfers between devices, on_device(): lax.psum_scatter(grad_in.astype(jnp.bfloat16), 'row', scatter_dimension=0...  37.9 us
    dot_general x1, matrix products, on_device(): jnp.dot(mid_full, up_full, preferred_element_type=jnp.float32) + up_bias  26.2 us
    all_gather x1, waiting for transfers between devices, on_device(): lax.all_gather(in_weight, 'row', axis=0, tiled=True)  24.4 us
  transfers between devices with their start and end apart: 16, of which 13 were waited for; matrix products, arithmetic and copies ran while one was open for 21% of the time, Pallas kernels for 0%

commit v1 on v0

v1 whole, which is shorter than its diff:
```python
from functools import partial
import math

import jax
import jax.numpy as jnp
from jax import lax
from jax.experimental import pallas as pl
from jax.experimental.pallas import tpu as pltpu
from jax.sharding import PartitionSpec as P

HD = 64
NORM_EPSILON = 1e-12
ALL = ("dp", "row", "col")
BF = jnp.bfloat16
F32 = jnp.float32
HIDDEN_SCORE = -1e30
SCALE = HD ** (-0.5)
EXP2_SCALE = SCALE * math.log2(math.e)


class Grid:
    def __init__(self, dp, row, outer, inner):
        self.shape = (dp, row, outer, inner)

    def pairs(self, target):
        n_d, n_r, n_o, n_i = self.shape

        def flat(d, r, o, i):
            return ((d * n_r + r) * n_o + o) * n_i + i

        result = []
        for d in range(n_d):
            for r in range(n_r):
                for o in range(n_o):
                    for i in range(n_i):
                        there = target(d, r, o, i)
                        if there is not None:
                            result.append((flat(d, r, o, i), flat(*there)))
        return result

    def shift(self, value, axis, by):
        size = self.shape[axis]

        def target(*at):
            at = list(at)
            at[axis] = (at[axis] + by) % size
            return tuple(at)

        return lax.ppermute(value, ALL, self.pairs(target))

    def flip(self, value, axis, bit):
        def target(*at):
            at = list(at)
            at[axis] = at[axis] ^ bit
            return tuple(at)

        return lax.ppermute(value, ALL, self.pairs(target))

    def total(self, value):
        for axis, size in enumerate(self.shape):
            bit = 1
            while bit < size:
                value = value + self.flip(value, axis, bit)
                bit *= 2
        return value

    def send_home(self, value):
        def target(d, r, o, i):
            return None if o == d else (d, r, d, i)

        return lax.ppermute(value, ALL, self.pairs(target))

    def send_away(self, value):
        def target(d, r, o, i):
            return (d, r, 1 - d, i) if o == d else None

        return lax.ppermute(value, ALL, self.pairs(target))


def dot(left, right):
    return jnp.dot(left, right, preferred_element_type=F32)


def dot_t(left, right):
    return lax.dot_general(left, right, (((1,), (1,)), ((), ())), preferred_element_type=F32)


def t_dot(left, right):
    return lax.dot_general(left, right, (((0,), (0,)), ((), ())), preferred_element_type=F32)


def norm_forward(hidden, gain, shift):
    row_mean = jnp.mean(hidden, axis=1, keepdims=True)
    variance = jnp.mean(hidden * hidden, axis=1, keepdims=True) - row_mean * row_mean
    inverse = lax.rsqrt(variance + NORM_EPSILON)
    normed = (hidden - row_mean) * inverse
    return (normed * gain + shift, normed, inverse)


def norm_backward(grad_after, normed, inverse, gain):
    grad_normed = grad_after * gain
    mean_one = jnp.mean(grad_normed, axis=1, keepdims=True)
    mean_two = jnp.mean(grad_normed * normed, axis=1, keepdims=True)
    return inverse * (grad_normed - mean_one - normed * mean_two)


def head_groups(width):
    columns = min(128, width)
    return columns, columns // HD, width // columns


def attend_forward_kernel(width, block, qkv, ids_row, ids_col, out):
    length = qkv.shape[1]
    columns, per_group, groups = head_groups(width)
    lane = lax.broadcasted_iota(jnp.int32, (block, columns), 1) // HD

    @pl.loop(0, length // block)
    def _(step):
        rows = pl.ds(pl.multiple_of(step * block, block), block)
        same = ids_col[0, rows, :] == ids_row[0]
        for group in range(groups):
            first = group * columns
            queries = qkv[0, rows, first : first + columns]
            keys = qkv[0, :, width + first : width + first + columns]
            values = qkv[0, :, 2 * width + first : 2 * width + first + columns]
            result = None
            for head in range(per_group):
                masked = jnp.where(lane == head, queries, jnp.zeros_like(queries))
                scores = jnp.where(same, dot_t(masked, keys), HIDDEN_SCORE)
                top = jnp.max(scores, axis=1, keepdims=True)
                terms = jnp.exp2((scores - top) * EXP2_SCALE)
                total = jnp.sum(terms, axis=1, keepdims=True)
                part = dot(terms.astype(BF), values) / total
                result = part if result is None else jnp.where(lane == head, part, result)
            out[0, rows, first : first + columns] = result.astype(BF)


def attend_backward_kernel(width, block, qkv, grads, ids_row, ids_col, out, key_total, value_total):
    length = qkv.shape[1]
    columns, per_group, groups = head_groups(width)
    lane = lax.broadcasted_iota(jnp.int32, (block, columns), 1) // HD
    key_lane = lax.broadcasted_iota(jnp.int32, (length, columns), 1) // HD
    for group in range(groups):
        first = group * columns
        keys = qkv[0, :, width + first : width + first + columns]
        values = qkv[0, :, 2 * width + first : 2 * width + first + columns]
        key_total[...] = jnp.zeros_like(key_total)
        value_total[...] = jnp.zeros_like(value_total)

        @pl.loop(0, length // block)
        def _(step):
            rows = pl.ds(pl.multiple_of(step * block, block), block)
            same = ids_col[0] == ids_row[0, :, rows]
            queries = qkv[0, rows, first : first + columns]
            tops = grads[0, rows, first : first + columns]
            query_grad = None
            for head in range(per_group):
                own = lane == head
                head_queries = jnp.where(own, queries, jnp.zeros_like(queries))
                head_grads = jnp.where(own, tops, jnp.zeros_like(tops))
                head_keys = jnp.where(key_lane == head, keys, jnp.zeros_like(keys))
                scores = jnp.where(same, dot_t(keys, head_queries), HIDDEN_SCORE)
                top = jnp.max(scores, axis=0, keepdims=True)
                terms = jnp.exp2((scores - top) * EXP2_SCALE)
                probs = terms * (1.0 / jnp.sum(terms, axis=0, keepdims=True))
                prob_grads = dot_t(values, head_grads)
                inner = jnp.sum(probs * prob_grads, axis=0, keepdims=True)
                score_grads = (probs * (prob_grads - inner)).astype(BF)
                value_total[...] += dot(probs.astype(BF), head_grads)
                key_total[...] += dot(score_grads, head_queries)
                part = t_dot(score_grads, head_keys)
                query_grad = part if query_grad is None else query_grad + part
            out[0, rows, first : first + columns] = (query_grad * SCALE).astype(BF)

        out[0, :, width + first : width + first + columns] = (key_total[...] * SCALE).astype(BF)
        out[0, :, 2 * width + first : 2 * width + first + columns] = value_total[...].astype(BF)


def whole_block(shape):
    return pl.BlockSpec((1,) + shape[1:], lambda s: (s, 0, 0))


def attend_forward(qkv, ids):
    count, length, columns = qkv.shape
    width = columns // 3
    ids_row, ids_col = ids[:, None, :], ids[:, :, None]
    return pl.pallas_call(
        partial(attend_forward_kernel, width, min(256, length)),
        grid=(count,),
        in_specs=[whole_block(v.shape) for v in (qkv, ids_row, ids_col)],
        out_specs=whole_block((count, length, width)),
        out_shape=jax.ShapeDtypeStruct((count, length, width), BF),
        compiler_params=pltpu.CompilerParams(vmem_limit_bytes=48 * 1024 * 1024),
        cost_estimate=pl.CostEstimate(
            flops=4 * count * length * length * 2 * width,
            bytes_accessed=count * length * width * 8,
            transcendentals=count * length * length * (width // HD),
        ),
    )(qkv, ids_row, ids_col)


def attend_backward(qkv, grads, ids):
    count, length, columns = qkv.shape
    width = columns // 3
    group = head_groups(width)[0]
    ids_row, ids_col = ids[:, None, :], ids[:, :, None]
    return pl.pallas_call(
        partial(attend_backward_kernel, width, min(256, length)),
        grid=(count,),
        in_specs=[whole_block(v.shape) for v in (qkv, grads, ids_row, ids_col)],
        out_specs=whole_block((count, length, columns)),
        out_shape=jax.ShapeDtypeStruct((count, length, columns), BF),
        scratch_shapes=[pltpu.VMEM((length, group), F32)] * 2,
        compiler_params=pltpu.CompilerParams(vmem_limit_bytes=48 * 1024 * 1024),
        cost_estimate=pl.CostEstimate(
            flops=10 * count * length * length * 2 * width,
            bytes_accessed=count * length * width * 14,
            transcendentals=count * length * length * (width // HD),
        ),
    )(qkv, grads, ids_row, ids_col)


D_AX, R_AX, O_AX, I_AX = 0, 1, 2, 3


def gelu_pair(value):
    cdf = 0.5 * (1.0 + lax.erf(value * (0.5**0.5)))
    density = jnp.exp(-0.5 * value * value) * (1.0 / math.sqrt(2.0 * math.pi))
    return value * cdf, cdf + value * density


def on_device(
    sizes,
    tokens,
    segment_ids,
    in_weight,
    in_bias,
    out_weight,
    out_bias,
    gain_one,
    shift_one,
    up_weight,
    up_bias,
    down_weight,
    down_bias,
    gain_two,
    shift_two,
    cotangent,
):
    n_dp, n_row, n_col = sizes
    rows_here, model = tokens.shape
    n_outer, length = segment_ids.shape
    n_inner = length // rows_here
    assert n_dp == 2 and n_outer == 2 and n_outer * n_inner == n_col
    net = Grid(n_dp, n_row, n_outer, n_inner)
    d, r, c = (lax.axis_index(name) for name in ALL)
    o, i = c // n_inner, c % n_inner
    at_home = o == d
    width = in_weight.shape[1] // 3
    heads = width // HD
    part = model // n_row
    units = up_weight.shape[1]
    half = units // 2

    def place(value):
        return lax.rem(r - value + n_row, n_row)

    def gather_row(value, axis):
        shape = list(value.shape)
        step = shape[axis]
        shape[axis] = step * n_row
        result = jnp.zeros(shape, value.dtype)
        for k in range(n_row):
            block = value if k == 0 else net.shift(value, R_AX, k)
            result = lax.dynamic_update_slice_in_dim(result, block, place(k) * step, axis)
        return result

    def scatter_row(value, axis):
        step = value.shape[axis] // n_row
        own = lax.dynamic_slice_in_dim(value, r * step, step, axis).astype(F32)
        for k in range(1, n_row):
            block = lax.dynamic_slice_in_dim(value, place(k) * step, step, axis)
            own = own + net.shift(block.astype(BF), R_AX, -k).astype(F32)
        return own

    def gather_units(value):
        blocks = [value] + [net.shift(value, I_AX, k) for k in range(1, n_inner)]
        blocks = jnp.stack(blocks)
        return jnp.stack([blocks] + [net.shift(blocks, O_AX, k) for k in range(1, n_outer)])

    def scatter_units(value, kind):
        own = value[0].astype(F32)
        for k in range(1, n_outer):
            own = own + net.shift(value[k].astype(kind), O_AX, -k).astype(F32)
        result = own[0]
        for k in range(1, n_inner):
            result = result + net.shift(own[k].astype(kind), I_AX, -k).astype(F32)
        return result

    def other(value):
        return net.shift(value, D_AX, 1)

    def at_block(value):
        return jnp.where(at_home, value, net.send_away(value))

    def from_block(value, kind):
        summed = value + net.send_home(value.astype(kind)).astype(F32)
        return jnp.where(at_home, summed, other(summed))

    in_mine = in_weight.reshape(part, heads, 3, HD).transpose(0, 2, 1, 3).reshape(part, 3 * width)
    in_full = gather_row(at_block(in_mine), 0)
    out_full = gather_row(at_block(out_weight), 1)
    bias_rows = at_block(in_bias).reshape(heads, 2, HD)
    in_bias_row = jnp.concatenate(
        [bias_rows[:, 0].reshape(width), jnp.zeros((width,), F32), bias_rows[:, 1].reshape(width)]
    )
    up_blocks = gather_units(
        gather_row(lax.dynamic_slice_in_dim(up_weight, d * half, half, 1), 0)
    ).reshape(n_col, model, half)
    down_blocks = gather_units(
        gather_row(lax.dynamic_slice_in_dim(down_weight, d * half, half, 0), 1)
    ).reshape(n_col, half, model)
    up_full = jnp.concatenate([up_blocks[k] for k in range(n_col)], axis=1)
    down_full = down_blocks.reshape(n_col * half, model)
    up_bias_row = gather_units(lax.dynamic_slice_in_dim(up_bias, d * half, half, 0)).reshape(
        n_col * half
    )

    def spread(value):
        parts = [value] + [net.shift(value, I_AX, k) for k in range(1, n_inner)]
        return jnp.concatenate(parts + [other(v) for v in parts], axis=0)

    def collect(value, weights_of):
        pieces = value.reshape(2, n_inner, rows_here, value.shape[-1])
        arrived = [
            other(weights_of(pieces[1, k]).astype(BF)) for k in reversed(range(n_inner))
        ][::-1]
        result = None
        for k in range(1, n_inner):
            one = weights_of(pieces[0, k]) + arrived[k].astype(F32)
            moved = net.shift(one.astype(BF), I_AX, -k).astype(F32)
            result = moved if result is None else result + moved
        own = weights_of(pieces[0, 0]) + arrived[0].astype(F32)
        return own if result is None else own + result

    own_ids = lax.dynamic_index_in_dim(segment_ids, o, 0, keepdims=False)
    own_ids = jnp.concatenate(
        [
            lax.dynamic_slice_in_dim(
                own_ids, lax.rem(i - k + n_inner, n_inner) * rows_here, rows_here, 0
            )
            for k in range(n_inner)
        ]
    )
    ids = jnp.stack([own_ids, other(own_ids)])

    token_full = spread(tokens)
    projected = (dot(token_full, in_full) + in_bias_row).astype(BF)
    projected = projected.reshape(2, length, 3 * width)
    attended = attend_forward(projected, ids).reshape(2 * length, width)
    branch = collect(attended, lambda v: dot(v, out_full))
    residual_one = tokens.astype(F32) + (branch + out_bias)
    normed_one, unit_one, inverse_one = norm_forward(residual_one, gain_one, shift_one)

    def both(value):
        return jnp.concatenate([value, other(value)], axis=0)

    def across(value, weights_of):
        away = other(weights_of(value[rows_here:]).astype(BF))
        return weights_of(value[:rows_here]) + away.astype(F32)

    mid = both(normed_one.astype(BF))
    hidden, slope = gelu_pair(dot(mid, up_full) + up_bias_row)
    hidden, slope = hidden.astype(BF), slope.astype(BF)
    residual_two = normed_one + (across(hidden, lambda v: dot(v, down_full)) + down_bias)
    normed_two, unit_two, inverse_two = norm_forward(residual_two, gain_two, shift_two)
    output = normed_two.astype(BF)

    grad_top = cotangent.astype(F32)
    grad_gain_two = jnp.sum(grad_top * unit_two, axis=0)
    grad_shift_two = jnp.sum(grad_top, axis=0)
    grad_two = norm_backward(grad_top, unit_two, inverse_two, gain_two)
    grad_two_low = grad_two.astype(BF)
    grad_down_bias = jnp.sum(grad_two_low.astype(F32), axis=0)
    grad_two_both = both(grad_two_low)
    grad_pre = (dot_t(grad_two_both, down_full) * slope.astype(F32)).astype(BF)
    grad_one = grad_two + across(grad_pre, lambda v: dot_t(v, up_full))
    grad_down = t_dot(hidden, grad_two_both).reshape(n_outer, n_inner, half, model)
    grad_up = jnp.stack(
        [t_dot(mid, grad_pre[:, k * half : (k + 1) * half]) for k in range(n_col)]
    ).reshape(n_outer, n_inner, model, half)
    grad_up_bias = jnp.sum(grad_pre.astype(F32), axis=0).reshape(n_outer, n_inner, half)

    grad_gain_one = jnp.sum(grad_one * unit_one, axis=0)
    grad_shift_one = jnp.sum(grad_one, axis=0)
    grad_first = norm_backward(grad_one, unit_one, inverse_one, gain_one)
    grad_first_low = grad_first.astype(BF)
    grad_out_bias = jnp.sum(grad_first_low.astype(F32), axis=0)
    full_sums = net.total(
        jnp.stack(
            [
                grad_out_bias,
                grad_gain_one,
                grad_shift_one,
                grad_down_bias,
                grad_gain_two,
                grad_shift_two,
            ]
        )
    )

    grad_first_full = spread(grad_first_low)
    grad_attended = dot_t(grad_first_full, out_full).astype(BF).reshape(2, length, width)
    grad_projected = attend_backward(projected, grad_attended, ids).reshape(
        2 * length, 3 * width
    )
    grad_tokens = grad_first + collect(grad_projected, lambda v: dot_t(v, in_full))
    grad_out = t_dot(attended, grad_first_full)
    grad_in = t_dot(token_full, grad_projected)
    bias_terms = jnp.sum(grad_projected.astype(F32), axis=0).reshape(3, heads, HD)
    grad_in_bias = jnp.stack([bias_terms[0], bias_terms[2]], axis=1).reshape(2 * width)

    def row_total(value):
        bit = 1
        while bit < n_row:
            value = value + net.flip(value, R_AX, bit)
            bit *= 2
        return value

    def join_halves(value, axis):
        there = other(value)
        first = jnp.where(d == 0, value, there)
        second = jnp.where(d == 0, there, value)
        return jnp.concatenate([first, second], axis=axis)

    grad_down = join_halves(scatter_row(scatter_units(grad_down, BF), 1), 0)
    grad_up = join_halves(scatter_row(scatter_units(grad_up, BF), 0), 1)
    grad_up_bias = join_halves(row_total(scatter_units(grad_up_bias, F32)), 0)
    grad_out = from_block(scatter_row(grad_out, 1), BF)
    grad_in = from_block(scatter_row(grad_in, 0), BF)
    grad_in = grad_in.reshape(part, 3, heads, HD).transpose(0, 2, 1, 3).reshape(part, 3 * width)
    grad_in_bias = from_block(row_total(grad_in_bias), F32)
    return (
        output,
        grad_tokens,
        grad_in,
        grad_in_bias,
        grad_out,
        full_sums[0],
        full_sums[1],
        full_sums[2],
        grad_up,
        grad_up_bias,
        grad_down,
        full_sums[3],
        full_sums[4],
        full_sums[5],
    )


def solution(mesh):
    return jax.shard_map(
        partial(on_device, tuple(mesh.shape[name] for name in ALL)),
        mesh=mesh,
        in_specs=(
            P(("dp", "row", "col"), None),
            P(("dp", "row"), None),
            P("row", "col"),
            P("col"),
            P("col", "row"),
            P(),
            P(),
            P(),
            P("row", "col"),
            P("col"),
            P("col", "row"),
            P(),
            P(),
            P(),
            P(("dp", "row", "col"), None),
        ),
        out_specs=(
            P(("dp", "row", "col"), None),
            P(("dp", "row", "col"), None),
            P("row", "col"),
            P("col"),
            P("col", "row"),
            P(),
            P(),
            P(),
            P("row", "col"),
            P("col"),
            P("col", "row"),
            P(),
            P(),
            P(),
        ),
        check_vma=False,
    )
```

time: 918 us -> 604 us (0.66)
  waiting for transfers between devices: 494 us -> 261 us
  starting transfers between devices: 1.22 us -> 135 us
  matrix products: 194 us -> 74 us
  blocking collectives: 73.6 us -> 0 us
  Pallas kernels: 0 us -> 63.6 us
  local copies, waits for them, and re-layouts: 72.1 us -> 26.5 us
  other arithmetic: 60 us -> 34 us
  between operations: 14.8 us -> 2.45 us
    all_gather x7 -> x0, waiting for transfers between devices: 280 us -> none  [the longest x4 197 us: col_tokens(): return lax.all_gather(value, 'col', axis=0, tiled=True)]
    ppermute x0 -> x74, waiting for transfers between devices: none -> 261 us  [the longest x59 183 us: shift(): return lax.ppermute(value, ALL, self.pairs(target))]
    reduce_scatter x8 -> x0, waiting for transfers between devices: 212 us -> none  [the longest x3 115 us: col_total(): lax.psum_scatter(value.astype(jnp.bfloat16), 'col', scatter_dimension=0,...]
    ppermute x0 -> x74, starting transfers between devices: none -> 135 us  [the longest x59 116 us: shift(): return lax.ppermute(value, ALL, self.pairs(target))]
    dot_general x40 -> x23, matrix products: 194 us -> 74 us  [the longest x8 33.5 us: dot_t(): lax.dot_general(left, right, (((1,), (1,)), ((), ())), preferred_element_...]
    pallas_call x0 -> x2, Pallas kernels: none -> 63.6 us  [the longest x1 46 us: attend_backward(): pl.pallas_call(partial(attend_backward_kernel, width, min(256, length)),...]
    psum x2 -> x0, blocking collectives: 57.1 us -> none  [the longest x1 41.5 us: on_device(): lax.psum((grad_out_bias, grad_gain_one, grad_shift_one, grad_down_bias, g...]
    convert_element_type x9 -> x3, other arithmetic: 27.7 us -> 0.69 us  [the longest x1 0.4 us: on_device(): mid = both(normed_one.astype(BF))]
  transfers between devices with their start and end apart: 16 -> 74, of which waited for: 13 -> 23; matrix products, arithmetic and copies ran while one was open for 21% -> 16% of each run, Pallas kernels for 0% -> 11%
where the time goes in v1:
time: 604 us; the launch traced here: 596 us
  waiting for transfers between devices  261 us (43%)
  starting transfers between devices  135 us (22%)
  matrix products  74 us (12%)
  Pallas kernels  63.6 us (11%)
  other arithmetic  34 us (6%)
  local copies, waits for them, and re-layouts  26.5 us (4%)
    ppermute x59, waiting for transfers between devices, shift(): return lax.ppermute(value, ALL, self.pairs(target))  183 us
    ppermute x59, starting transfers between devices, shift(): return lax.ppermute(value, ALL, self.pairs(target))  116 us
    ppermute x9, waiting for transfers between devices, flip(): return lax.ppermute(value, ALL, self.pairs(target))  71.7 us
    pallas_call x1, Pallas kernels, attend_backward(): pl.pallas_call(partial(attend_backward_kernel, width, min(256, length)),...  46 us
    dot_general x8, matrix products, dot_t(): lax.dot_general(left, right, (((1,), (1,)), ((), ())), preferred_element_...  33.5 us
    dot_general x7, matrix products, t_dot(): lax.dot_general(left, right, (((0,), (0,)), ((), ())), preferred_element_...  21.6 us
    dot_general x8, matrix products, dot(): return jnp.dot(left, right, preferred_element_type=F32)  18.8 us
    pallas_call x1, Pallas kernels, attend_forward(): pl.pallas_call(partial(attend_forward_kernel, width, min(256, length)), g...  17.6 us
  transfers between devices with their start and end apart: 74, of which 23 were waited for; matrix products, arithmetic and copies ran while one was open for 16% of the time, Pallas kernels for 11%

profile of v1, /device:TPU:11, one launch (start us, length us, event | category | flops | bytes accessed | tf_op | source)
XLA Modules:
  0.0 595.9 jit_solution(15684289588663640915)
XLA Ops:
  23.3 6.1 %collective-permute-start.12 = (bf16[256,256]{1,0:T(8,128)(2,1)}, bf16[256,256]{1,0:T(8,128)(2,1)S(1)}, u32[]{:S(2)}, u32[]{:S(2)}) collective-permute-start(bf16[256,256]{1,0:T(8,128)(2,1)} %get-tuple-element.65), channel_id=1, source_target_pairs={{0,12},{1,13},{2,14},{3,15},{4,0},{5,1},{6,2},{7,3},{8,4},{9,5},{1... | collective-permute-start | bytes 393224 | tf_op jit(solution)/shard_map/ppermute | solution.py:49
  32.8 3.9 collective-permute-start.2
  36.7 4.8 collective-permute-start.5
  45.1 25.1 %collective-permute-done.5 = bf16[256,768]{0,1:T(8,128)(2,1)S(1)} collective-permute-done((bf16[256,768]{0,1:T(8,128)(2,1)S(1)}, bf16[256,768]{0,1:T(8,128)(2,1)S(1)}, u32[]{:S(2)}, u32[]{:S(2)}) %collective-permute-start.5) | collective-permute-done | bytes 393248 | tf_op jit(solution)/shard_map/ppermute | solution.py:49
  70.3 10.7 %collective-permute-done.6 = bf16[256,768]{0,1:T(8,128)(2,1)S(1)} collective-permute-done((bf16[256,768]{0,1:T(8,128)(2,1)S(1)}, bf16[256,768]{0,1:T(8,128)(2,1)S(1)}, u32[]{:S(2)}, u32[]{:S(2)}) %collective-permute-start.6) | collective-permute-done | bytes 393248 | tf_op jit(solution)/shard_map/ppermute | solution.py:49
  91.0 17.6 %shard_map.254 = bf16[2,1024,256]{2,1,0:T(8,128)(2,1)S(1)} custom-call(bf16[2,1024,768]{2,1,0:T(8,128)(2,1)S(1)} %bitcast.137, s32[2,1,1024]{2,1,0:T(1,128)S(1)} %broadcast_in_dim.16.ids_row, s32[2,1024,1]{2,1,0:T(8,128)S(1)} %copy.38.ids_col), custom_call_target="tpu_custom_call" | custom-call | flops 4294967296 | bytes 4194304 | tf_op jit(solution)/shard_map/pallas_call | solution.py:187
  117.9 20.5 %collective-permute-done.20 = bf16[1024,512]{1,0:T(8,128)(2,1)S(1)} collective-permute-done((bf16[1024,512]{1,0:T(8,128)(2,1)}, bf16[1024,512]{1,0:T(8,128)(2,1)S(1)}, u32[]{:S(2)}, u32[]{:S(2)}) %collective-permute-start.20) | collective-permute-done | bytes 1048608 | tf_op jit(solution)/shard_map/ppermute | solution.py:49
  139.9 4.2 collective-permute-start.21
  144.1 16.8 %collective-permute-done.27 = bf16[512,1024]{1,0:T(8,128)(2,1)S(1)} collective-permute-done((bf16[512,1024]{1,0:T(8,128)(2,1)S(1)}, bf16[512,1024]{1,0:T(8,128)(2,1)S(1)}, u32[]{:S(2)}, u32[]{:S(2)}) %collective-permute-start.27) | collective-permute-done | bytes 1048608 | tf_op jit(solution)/shard_map/ppermute | solution.py:49
  161.2 4.2 collective-permute-start.28
  165.9 17.5 %collective-permute-done.15 = bf16[512,1024]{1,0:T(8,128)(2,1)S(1)} collective-permute-done((bf16[512,1024]{1,0:T(8,128)(2,1)S(1)}, bf16[512,1024]{1,0:T(8,128)(2,1)S(1)}, u32[]{:S(2)}, u32[]{:S(2)}) %collective-permute-start.15) | collective-permute-done | bytes 1048608 | tf_op jit(solution)/shard_map/ppermute | solution.py:49
  188.3 4.0 collective-permute-start.23
  192.3 42.0 %collective-permute-done.23 = f32[2,512]{1,0:T(2,128)S(1)} collective-permute-done((f32[2,512]{1,0:T(2,128)S(1)}, f32[2,512]{1,0:T(2,128)S(1)}, u32[]{:S(2)}, u32[]{:S(2)}) %collective-permute-start.23) | collective-permute-done | bytes 4128 | tf_op jit(solution)/shard_map/ppermute | solution.py:49
  235.5 8.1 %multiply_convert_fusion.1 = (bf16[1024,2048]{1,0:T(8,128)(2,1)S(1)}, f32[1024,2048]{1,0:T(8,128)}) fusion(f32[2048]{0:T(1024)S(1)} %bitcast.159, bf16[1024,512]{1,0:T(8,128)(2,1)S(1)} %get-tuple-element.69, bf16[1024,512]{1,0:T(8,128)(2,1)S(1)} %get-tuple-element.70, bf16[1024,512]{1,0:T(8,128)(2,1)S(1)} %get-tuple-element.71, ...), kind=kOutput, calls=%fused_computation.8 | convolution fusion | flops 4328521728 | bytes 18882560 | tf_op jit(solution)/shard_map/dot_general | solution.py:81
  258.4 12.3 %convert_reduce_fusion = (f32[2048]{0:T(1024)S(1)}, bf16[1024,2048]{1,0:T(8,128)(2,1)}) fusion(f32[1024,2048]{1,0:T(8,128)} %get-tuple-element.120, f32[2048]{0:T(1024)S(1)} %bitcast.160, bf16[2048,1024]{1,0:T(8,128)(2,1)S(1)} %bitcast.144, bf16[512,1024]{1,0:T(8,128)(2,1)S(1)} %collective-permute-done.30, bf16[512,1024]{1,0:T(8,128)(2,1)S(1)} %get-tuple-element.57), kind=kOutput, calls=%fused_computation.6 | convolution fusion | flops 4330616832 | bytes 18890752 | tf_op jit(solution)/shard_map/dot_general | solution.py:85
  272.2 5.3 fusion.28
  278.3 4.6 fusion.33
  316.8 61.0 %collective-permute-done.55 = f32[6,1024]{1,0:T(8,128)S(1)} collective-permute-done((f32[6,1024]{1,0:T(8,128)S(1)}, f32[6,1024]{1,0:T(8,128)S(1)}, u32[]{:S(2)}, u32[]{:S(2)}) %collective-permute-start.55) | collective-permute-done | bytes 24608 | tf_op jit(solution)/shard_map/ppermute | solution.py:57
  392.7 5.0 convolution_convert_fusion
  397.7 46.0 %shard_map.255 = bf16[2,1024,768]{2,1,0:T(8,128)(2,1)S(1)} custom-call(bf16[2,1024,768]{2,1,0:T(8,128)(2,1)} %bitcast.138, bf16[2,1024,256]{2,1,0:T(8,128)(2,1)S(1)} %bitcast.139, s32[2,1,1024]{2,1,0:T(1,128)S(1)} %broadcast_in_dim.16.ids_row, s32[2,1024,1]{2,1,0:T(8,128)S(1)} %copy-done.1), custom_call_target="tpu_custom_call" | custom-call | flops 10737418240 | bytes 7340032 | tf_op jit(solution)/shard_map/pallas_call | solution.py:207
  444.2 5.3 fusion.65
  468.9 8.5 %collective-permute-done.44 = f32[512]{0:T(512)S(1)} collective-permute-done((f32[512]{0:T(512)S(1)}, f32[512]{0:T(512)S(1)}, u32[]{:S(2)}, u32[]{:S(2)}) %collective-permute-start.44) | collective-permute-done | bytes 2080 | tf_op jit(solution)/shard_map/ppermute | solution.py:57
  482.4 3.9 collective-permute-start.71
  486.4 4.3 collective-permute-start.46
  495.0 21.6 %collective-permute-start.36 = (bf16[512,1024]{1,0:T(8,128)(2,1)S(1)}, bf16[512,1024]{1,0:T(8,128)(2,1)S(1)}, u32[]{:S(2)}, u32[]{:S(2)}) collective-permute-start(bf16[512,1024]{1,0:T(8,128)(2,1)S(1)} %convolution_convert_fusion.1), channel_id=1, source_target_pairs={{0,16},{1,17},{2,18},{3,19},{4,20},{5,21},{6,22},{7,23},{8,24},{9,... | collective-permute-start | bytes 3145736 | tf_op jit(solution)/shard_map/ppermute | solution.py:49
  519.0 4.4 collective-permute-start.60
  523.4 16.7 %collective-permute-done.39 = bf16[256,768]{0,1:T(8,128)(2,1)S(1)} collective-permute-done((bf16[256,768]{0,1:T(8,128)(2,1)S(1)}, bf16[256,768]{0,1:T(8,128)(2,1)S(1)}, u32[]{:S(2)}, u32[]{:S(2)}) %collective-permute-start.39) | collective-permute-done | bytes 393248 | tf_op jit(solution)/shard_map/ppermute | solution.py:49
  540.1 4.1 collective-permute-start.51
  545.8 5.7 collective-permute-start.35
  556.0 3.7 collective-permute-done.41
  573.4 18.1 %collective-permute-done.37 = bf16[512,1024]{1,0:T(8,128)(2,1)} collective-permute-done((bf16[512,1024]{1,0:T(8,128)(2,1)}, bf16[512,1024]{1,0:T(8,128)(2,1)}, u32[]{:S(2)}, u32[]{:S(2)}) %collective-permute-start.37) | collective-permute-done | bytes 1048608 | tf_op jit(solution)/shard_map/ppermute | solution.py:49
  591.5 4.1 add_add_fusion
  (377 shorter events, 173.4 us)
Async XLA Ops:
  0.7 32.2 %collective-permute-start = (bf16[512,1024]{1,0:T(8,128)(2,1)}, bf16[512,1024]{1,0:T(8,128)(2,1)}, u32[]{:S(2)}, u32[]{:S(2)}) collective-permute-start(bf16[512,1024]{1,0:T(8,128)(2,1)} %param.15), channel_id=1, source_target_pairs={{0,1},{1,0},{2,3},{3,2},{4,5},{5,4},{6,7},{7,6},{8,9},{9,8},{10,11... | collective-permute-start | bytes 3145736 | tf_op jit(solution)/shard_map/ppermute | solution.py:49
  1.0 82.0 %collective-permute-start.1 = (bf16[512,1024]{1,0:T(8,128)(2,1)}, bf16[512,1024]{1,0:T(8,128)(2,1)}, u32[]{:S(2)}, u32[]{:S(2)}) collective-permute-start(bf16[512,1024]{1,0:T(8,128)(2,1)} %param.15), channel_id=1, source_target_pairs={{0,16},{1,17},{2,18},{3,19},{4,20},{5,21},{6,22},{7,23},{8,24},{9,... | collective-permute-start | bytes 3145736 | tf_op jit(solution)/shard_map/ppermute | solution.py:49
  32.8 51.9 %collective-permute-start.2 = (bf16[512,1024]{1,0:T(8,128)(2,1)}, bf16[512,1024]{1,0:T(8,128)(2,1)S(1)}, u32[]{:S(2)}, u32[]{:S(2)}) collective-permute-start(bf16[512,1024]{1,0:T(8,128)(2,1)} %collective-permute-done), channel_id=1, source_target_pairs={{0,16},{1,17},{2,18},{3,19},{4,20},{5,21},{6,22},{7,23},{8,24},{9,... | collective-permute-start | bytes 3145736 | tf_op jit(solution)/shard_map/ppermute | solution.py:49
  36.7 33.5 %collective-permute-start.5 = (bf16[256,768]{0,1:T(8,128)(2,1)S(1)}, bf16[256,768]{0,1:T(8,128)(2,1)S(1)}, u32[]{:S(2)}, u32[]{:S(2)}) collective-permute-start(bf16[256,768]{0,1:T(8,128)(2,1)S(1)} %get-tuple-element.118), channel_id=1, source_target_pairs={{0,8},{1,9},{2,10},{3,11},{4,12},{5,13},{6,14},{7,15},{8,0},{9,1},... | collective-permute-start | bytes 1179656 | tf_op jit(solution)/shard_map/ppermute | solution.py:49
  41.6 39.4 %collective-permute-start.6 = (bf16[256,768]{0,1:T(8,128)(2,1)S(1)}, bf16[256,768]{0,1:T(8,128)(2,1)S(1)}, u32[]{:S(2)}, u32[]{:S(2)}) collective-permute-start(bf16[256,768]{0,1:T(8,128)(2,1)S(1)} %get-tuple-element.118), channel_id=1, source_target_pairs={{0,12},{1,13},{2,14},{3,15},{4,0},{5,1},{6,2},{7,3},{8,4},{9,5},{1... | collective-permute-start | bytes 1179656 | tf_op jit(solution)/shard_map/ppermute | solution.py:49
  43.8 70.9 %collective-permute-start.25 = (bf16[512,256]{1,0:T(8,128)(2,1)S(1)}, bf16[512,256]{1,0:T(8,128)(2,1)S(1)}, u32[]{:S(2)}, u32[]{:S(2)}) collective-permute-start(bf16[512,256]{1,0:T(8,128)(2,1)S(1)} %copy-done.36), channel_id=1, source_target_pairs={{0,8},{1,9},{2,10},{3,11},{4,12},{5,13},{6,14},{7,15},{8,0},{9,1},... | collective-permute-start | bytes 786440 | tf_op jit(solution)/shard_map/ppermute | solution.py:49
  70.2 44.4 %collective-permute-start.24 = (bf16[512,256]{1,0:T(8,128)(2,1)S(1)}, bf16[512,256]{1,0:T(8,128)(2,1)S(1)}, u32[]{:S(2)}, u32[]{:S(2)}) collective-permute-start(bf16[512,256]{1,0:T(8,128)(2,1)S(1)} %copy-done.36), channel_id=1, source_target_pairs={{0,4},{1,5},{2,6},{3,7},{4,8},{5,9},{6,10},{7,11},{8,12},{9,13},{1... | collective-permute-start | bytes 786440 | tf_op jit(solution)/shard_map/ppermute | solution.py:49
  81.0 33.8 %collective-permute-start.26 = (bf16[512,256]{1,0:T(8,128)(2,1)S(1)}, bf16[512,256]{1,0:T(8,128)(2,1)S(1)}, u32[]{:S(2)}, u32[]{:S(2)}) collective-permute-start(bf16[512,256]{1,0:T(8,128)(2,1)S(1)} %copy-done.36), channel_id=1, source_target_pairs={{0,12},{1,13},{2,14},{3,15},{4,0},{5,1},{6,2},{7,3},{8,4},{9,5},{1... | collective-permute-start | bytes 786440 | tf_op jit(solution)/shard_map/ppermute | solution.py:49
  84.8 28.0 %collective-permute-start.19 = (bf16[256,512]{1,0:T(8,128)(2,1)}, bf16[256,512]{1,0:T(8,128)(2,1)S(1)}, u32[]{:S(2)}, u32[]{:S(2)}) collective-permute-start(bf16[256,512]{1,0:T(8,128)(2,1)} %get-tuple-element.62), channel_id=1, source_target_pairs={{0,12},{1,13},{2,14},{3,15},{4,0},{5,1},{6,2},{7,3},{8,4},{9,5},{1... | collective-permute-start | bytes 786440 | tf_op jit(solution)/shard_map/ppermute | solution.py:49
  114.8 46.1 %collective-permute-start.27 = (bf16[512,1024]{1,0:T(8,128)(2,1)S(1)}, bf16[512,1024]{1,0:T(8,128)(2,1)S(1)}, u32[]{:S(2)}, u32[]{:S(2)}) collective-permute-start(bf16[512,1024]{1,0:T(8,128)(2,1)S(1)} %constant_dynamic-update-slice_fusion.4), channel_id=1, source_target_pairs={{0,1},{1,0},{2,3},{3,2},{4,5},{5,4},{6,7},{7,6},{8,9},{9,8},{10,11... | collective-permute-start | bytes 3145736 | tf_op jit(solution)/shard_map/ppermute | solution.py:49
  115.6 50.3 %collective-permute-start.13 = (bf16[512,1024]{1,0:T(8,128)(2,1)S(1)}, bf16[512,1024]{1,0:T(8,128)(2,1)S(1)}, u32[]{:S(2)}, u32[]{:S(2)}) collective-permute-start(bf16[512,1024]{1,0:T(8,128)(2,1)S(1)} %convolution_convert_fusion.6), channel_id=1, source_target_pairs={{0,16},{1,17},{2,18},{3,19},{4,20},{5,21},{6,22},{7,23},{8,24},{9,... | collective-permute-start | bytes 3145736 | tf_op jit(solution)/shard_map/ppermute | solution.py:49
  116.7 66.7 %collective-permute-start.15 = (bf16[512,1024]{1,0:T(8,128)(2,1)S(1)}, bf16[512,1024]{1,0:T(8,128)(2,1)S(1)}, u32[]{:S(2)}, u32[]{:S(2)}) collective-permute-start(bf16[512,1024]{1,0:T(8,128)(2,1)S(1)} %add_convert_fusion.3), channel_id=1, source_target_pairs={{0,1},{1,0},{2,3},{3,2},{4,5},{5,4},{6,7},{7,6},{8,9},{9,8},{10,11... | collective-permute-start | bytes 3145736 | tf_op jit(solution)/shard_map/ppermute | solution.py:49
  139.9 94.4 %collective-permute-start.21 = (bf16[2,1024,512]{2,1,0:T(8,128)(2,1)S(1)}, bf16[2,1024,512]{2,1,0:T(8,128)(2,1)S(1)}, u32[]{:S(2)}, u32[]{:S(2)}) collective-permute-start(bf16[2,1024,512]{2,1,0:T(8,128)(2,1)S(1)} %get-tuple-element.83), channel_id=1, source_target_pairs={{0,2},{1,3},{2,0},{3,1},{4,6},{5,7},{6,4},{7,5},{8,10},{9,11},{10,... | collective-permute-start | bytes 6291464 | tf_op jit(solution)/shard_map/ppermute | solution.py:49
  161.2 73.6 %collective-permute-start.28 = (bf16[2,512,1024]{2,1,0:T(8,128)(2,1)S(1)}, bf16[2,512,1024]{2,1,0:T(8,128)(2,1)S(1)}, u32[]{:S(2)}, u32[]{:S(2)}) collective-permute-start(bf16[2,512,1024]{2,1,0:T(8,128)(2,1)S(1)} %get-tuple-element.85), channel_id=1, source_target_pairs={{0,2},{1,3},{2,0},{3,1},{4,6},{5,7},{6,4},{7,5},{8,10},{9,11},{10,... | collective-permute-start | bytes 6291464 | tf_op jit(solution)/shard_map/ppermute | solution.py:49
  184.7 50.8 %collective-permute-start.16 = (bf16[512,1024]{1,0:T(8,128)(2,1)S(1)}, bf16[512,1024]{1,0:T(8,128)(2,1)S(1)}, u32[]{:S(2)}, u32[]{:S(2)}) collective-permute-start(bf16[512,1024]{1,0:T(8,128)(2,1)S(1)} %fusion.22), channel_id=1, source_target_pairs={{0,16},{1,17},{2,18},{3,19},{4,20},{5,21},{6,22},{7,23},{8,24},{9,... | collective-permute-start | bytes 3145736 | tf_op jit(solution)/shard_map/ppermute | solution.py:49
  188.3 46.0 %collective-permute-start.23 = (f32[2,512]{1,0:T(2,128)S(1)}, f32[2,512]{1,0:T(2,128)S(1)}, u32[]{:S(2)}, u32[]{:S(2)}) collective-permute-start(f32[2,512]{1,0:T(2,128)S(1)} %get-tuple-element.112), channel_id=1, source_target_pairs={{0,2},{1,3},{2,0},{3,1},{4,6},{5,7},{6,4},{7,5},{8,10},{9,11},{10,... | collective-permute-start | bytes 12296 | tf_op jit(solution)/shard_map/ppermute | solution.py:49
  284.6 98.5 %collective-permute-start.68 = (bf16[2,512,1024]{2,1,0:T(8,128)(2,1)}, bf16[2,512,1024]{2,1,0:T(8,128)(2,1)}, u32[]{:S(2)}, u32[]{:S(2)}) collective-permute-start(bf16[2,512,1024]{2,1,0:T(8,128)(2,1)} %bitcast.61), channel_id=1, source_target_pairs={{0,2},{1,3},{2,0},{3,1},{4,6},{5,7},{6,4},{7,5},{8,10},{9,11},{10,... | collective-permute-start | bytes 6291464 | tf_op jit(solution)/shard_map/ppermute | solution.py:49
  290.2 98.2 %collective-permute-start.57 = (bf16[2,1024,512]{1,2,0:T(8,128)(2,1)}, bf16[2,1024,512]{1,2,0:T(8,128)(2,1)}, u32[]{:S(2)}, u32[]{:S(2)}) collective-permute-start(bf16[2,1024,512]{1,2,0:T(8,128)(2,1)} %pad_maximum_fusion.8), channel_id=1, source_target_pairs={{0,2},{1,3},{2,0},{3,1},{4,6},{5,7},{6,4},{7,5},{8,10},{9,11},{10,... | collective-permute-start | bytes 6291464 | tf_op jit(solution)/shard_map/ppermute | solution.py:49
  303.6 77.7 %collective-permute-start.32 = (bf16[512,1024]{1,0:T(8,128)(2,1)}, bf16[512,1024]{1,0:T(8,128)(2,1)S(1)}, u32[]{:S(2)}, u32[]{:S(2)}) collective-permute-start(bf16[512,1024]{1,0:T(8,128)(2,1)} %get-tuple-element.59), channel_id=1, source_target_pairs={{0,1},{1,0},{2,3},{3,2},{4,5},{5,4},{6,7},{7,6},{8,9},{9,8},{10,11... | collective-permute-start | bytes 3145736 | tf_op jit(solution)/shard_map/ppermute | solution.py:49
  316.6 61.2 %collective-permute-start.55 = (f32[6,1024]{1,0:T(8,128)S(1)}, f32[6,1024]{1,0:T(8,128)S(1)}, u32[]{:S(2)}, u32[]{:S(2)}) collective-permute-start(f32[6,1024]{1,0:T(8,128)S(1)} %add.380), channel_id=1, source_target_pairs={{0,2},{1,3},{2,0},{3,1},{4,6},{5,7},{6,4},{7,5},{8,10},{9,11},{10,... | collective-permute-start | bytes 73736 | tf_op jit(solution)/shard_map/ppermute | solution.py:57
  387.1 75.0 %collective-permute-start.69 = (bf16[512,1024]{1,0:T(8,128)(2,1)}, bf16[512,1024]{1,0:T(8,128)(2,1)}, u32[]{:S(2)}, u32[]{:S(2)}) collective-permute-start(bf16[512,1024]{1,0:T(8,128)(2,1)} %fusion.35), channel_id=1, source_target_pairs={{0,1},{1,0},{2,3},{3,2},{4,5},{5,4},{6,7},{7,6},{8,9},{9,8},{10,11... | collective-permute-start | bytes 3145736 | tf_op jit(solution)/shard_map/ppermute | solution.py:49
  392.2 73.2 %collective-permute-start.58 = (bf16[1024,512]{0,1:T(8,128)(2,1)}, bf16[1024,512]{0,1:T(8,128)(2,1)}, u32[]{:S(2)}, u32[]{:S(2)}) collective-permute-start(bf16[1024,512]{0,1:T(8,128)(2,1)} %fusion.34), channel_id=1, source_target_pairs={{0,1},{1,0},{2,3},{3,2},{4,5},{5,4},{6,7},{7,6},{8,9},{9,8},{10,11... | collective-permute-start | bytes 3145736 | tf_op jit(solution)/shard_map/ppermute | solution.py:49
  454.0 28.5 %collective-permute-start.47 = (bf16[256,256]{1,0:T(8,128)(2,1)S(1)}, bf16[256,256]{1,0:T(8,128)(2,1)S(1)}, u32[]{:S(2)}, u32[]{:S(2)}) collective-permute-start(bf16[256,256]{1,0:T(8,128)(2,1)S(1)} %get-tuple-element.90), channel_id=1, source_target_pairs={{0,12},{1,13},{2,14},{3,15},{4,0},{5,1},{6,2},{7,3},{8,4},{9,5},{1... | collective-permute-start | bytes 393224 | tf_op jit(solution)/shard_map/ppermute | solution.py:49
  454.9 27.6 %collective-permute-start.49 = (bf16[256,256]{1,0:T(8,128)(2,1)S(1)}, bf16[256,256]{1,0:T(8,128)(2,1)S(1)}, u32[]{:S(2)}, u32[]{:S(2)}) collective-permute-start(bf16[256,256]{1,0:T(8,128)(2,1)S(1)} %get-tuple-element.91), channel_id=1, source_target_pairs={{0,4},{1,5},{2,6},{3,7},{4,8},{5,9},{6,10},{7,11},{8,12},{9,13},{1... | collective-permute-start | bytes 393224 | tf_op jit(solution)/shard_map/ppermute | solution.py:49
  465.3 53.1 %collective-permute-start.38 = (bf16[256,768]{0,1:T(8,128)(2,1)S(1)}, bf16[256,768]{0,1:T(8,128)(2,1)S(1)}, u32[]{:S(2)}, u32[]{:S(2)}) collective-permute-start(bf16[256,768]{0,1:T(8,128)(2,1)S(1)} %get-tuple-element.72), channel_id=1, source_target_pairs={{0,12},{1,13},{2,14},{3,15},{4,0},{5,1},{6,2},{7,3},{8,4},{9,5},{1... | collective-permute-start | bytes 1179656 | tf_op jit(solution)/shard_map/ppermute | solution.py:49
  482.4 34.1 %collective-permute-start.71 = (bf16[512,256]{1,0:T(8,128)(2,1)S(1)}, bf16[512,256]{1,0:T(8,128)(2,1)S(1)}, u32[]{:S(2)}, u32[]{:S(2)}) collective-permute-start(bf16[512,256]{1,0:T(8,128)(2,1)S(1)} %get-tuple-element.78), channel_id=1, source_target_pairs={{0,8},{1,9},{2,10},{3,11},{4,12},{5,13},{6,14},{7,15},{8,0},{9,1},... | collective-permute-start | bytes 786440 | tf_op jit(solution)/shard_map/ppermute | solution.py:49
  494.8 45.3 %collective-permute-start.39 = (bf16[256,768]{0,1:T(8,128)(2,1)S(1)}, bf16[256,768]{0,1:T(8,128)(2,1)S(1)}, u32[]{:S(2)}, u32[]{:S(2)}) collective-permute-start(bf16[256,768]{0,1:T(8,128)(2,1)S(1)} %get-tuple-element.74), channel_id=1, source_target_pairs={{0,8},{1,9},{2,10},{3,11},{4,12},{5,13},{6,14},{7,15},{8,0},{9,1},... | collective-permute-start | bytes 1179656 | tf_op jit(solution)/shard_map/ppermute | solution.py:49
  495.0 69.4 %collective-permute-start.36 = (bf16[512,1024]{1,0:T(8,128)(2,1)S(1)}, bf16[512,1024]{1,0:T(8,128)(2,1)S(1)}, u32[]{:S(2)}, u32[]{:S(2)}) collective-permute-start(bf16[512,1024]{1,0:T(8,128)(2,1)S(1)} %convolution_convert_fusion.1), channel_id=1, source_target_pairs={{0,16},{1,17},{2,18},{3,19},{4,20},{5,21},{6,22},{7,23},{8,24},{9,... | collective-permute-start | bytes 3145736 | tf_op jit(solution)/shard_map/ppermute | solution.py:49
  516.6 29.2 %collective-permute-start.59 = (bf16[256,512]{0,1:T(8,128)(2,1)S(1)}, bf16[256,512]{0,1:T(8,128)(2,1)S(1)}, u32[]{:S(2)}, u32[]{:S(2)}) collective-permute-start(bf16[256,512]{0,1:T(8,128)(2,1)S(1)} %get-tuple-element.79), channel_id=1, source_target_pairs={{0,12},{1,13},{2,14},{3,15},{4,0},{5,1},{6,2},{7,3},{8,4},{9,5},{1... | collective-permute-start | bytes 786440 | tf_op jit(solution)/shard_map/ppermute | solution.py:49
  518.4 33.1 %collective-permute-start.61 = (bf16[256,512]{0,1:T(8,128)(2,1)S(1)}, bf16[256,512]{0,1:T(8,128)(2,1)S(1)}, u32[]{:S(2)}, u32[]{:S(2)}) collective-permute-start(bf16[256,512]{0,1:T(8,128)(2,1)S(1)} %get-tuple-element.80), channel_id=1, source_target_pairs={{0,4},{1,5},{2,6},{3,7},{4,8},{5,9},{6,10},{7,11},{8,12},{9,13},{1... | collective-permute-start | bytes 786440 | tf_op jit(solution)/shard_map/ppermute | solution.py:49
  519.0 32.5 %collective-permute-start.60 = (bf16[256,512]{0,1:T(8,128)(2,1)S(1)}, bf16[256,512]{0,1:T(8,128)(2,1)S(1)}, u32[]{:S(2)}, u32[]{:S(2)}) collective-permute-start(bf16[256,512]{0,1:T(8,128)(2,1)S(1)} %get-tuple-element.81), channel_id=1, source_target_pairs={{0,8},{1,9},{2,10},{3,11},{4,12},{5,13},{6,14},{7,15},{8,0},{9,1},... | collective-permute-start | bytes 786440 | tf_op jit(solution)/shard_map/ppermute | solution.py:49
  545.8 27.6 %collective-permute-start.35 = (bf16[512,1024]{1,0:T(8,128)(2,1)}, bf16[512,1024]{1,0:T(8,128)(2,1)}, u32[]{:S(2)}, u32[]{:S(2)}) collective-permute-start(bf16[512,1024]{1,0:T(8,128)(2,1)} %convolution_convert_fusion.2), channel_id=1, source_target_pairs={{0,16},{1,17},{2,18},{3,19},{4,20},{5,21},{6,22},{7,23},{8,24},{9,... | collective-permute-start | bytes 3145736 | tf_op jit(solution)/shard_map/ppermute | solution.py:49
  (104 other events, 1285.1 us)

commit v2 on v1

v2 whole, which is shorter than its diff:
```python
from functools import partial
import math

import jax
import jax.numpy as jnp
from jax import lax
from jax.experimental import pallas as pl
from jax.experimental.pallas import tpu as pltpu
from jax.sharding import PartitionSpec as P

HD = 64
NORM_EPSILON = 1e-12
ALL = ("dp", "row", "col")
BF = jnp.bfloat16
F32 = jnp.float32
HIDDEN_SCORE = -1e30
SCALE = HD ** (-0.5)
EXP2_SCALE = SCALE * math.log2(math.e)


class Grid:
    def __init__(self, dp, row, outer, inner):
        self.shape = (dp, row, outer, inner)

    def pairs(self, target):
        n_d, n_r, n_o, n_i = self.shape

        def flat(d, r, o, i):
            return ((d * n_r + r) * n_o + o) * n_i + i

        result = []
        for d in range(n_d):
            for r in range(n_r):
                for o in range(n_o):
                    for i in range(n_i):
                        there = target(d, r, o, i)
                        if there is not None:
                            result.append((flat(d, r, o, i), flat(*there)))
        return result

    def shift(self, value, axis, by):
        size = self.shape[axis]

        def target(*at):
            at = list(at)
            at[axis] = (at[axis] + by) % size
            return tuple(at)

        return lax.ppermute(value, ALL, self.pairs(target))

    def flip(self, value, axis, bit):
        def target(*at):
            at = list(at)
            at[axis] = at[axis] ^ bit
            return tuple(at)

        return lax.ppermute(value, ALL, self.pairs(target))

    def total(self, value):
        for axis in (0, 3, 2, 1):
            size = self.shape[axis]
            bit = 1
            while bit < size:
                value = value + self.flip(value, axis, bit)
                bit *= 2
        return value


def dot(left, right):
    return jnp.dot(left, right, preferred_element_type=F32)


def dot_t(left, right):
    return lax.dot_general(left, right, (((1,), (1,)), ((), ())), preferred_element_type=F32)


def t_dot(left, right):
    return lax.dot_general(left, right, (((0,), (0,)), ((), ())), preferred_element_type=F32)


def after(value, *earlier):
    return lax.optimization_barrier((value, *earlier))[0]


def norm_forward(hidden, gain, shift):
    row_mean = jnp.mean(hidden, axis=1, keepdims=True)
    variance = jnp.mean(hidden * hidden, axis=1, keepdims=True) - row_mean * row_mean
    inverse = lax.rsqrt(variance + NORM_EPSILON)
    normed = (hidden - row_mean) * inverse
    return (normed * gain + shift, normed, inverse)


def norm_backward(grad_after, normed, inverse, gain):
    grad_normed = grad_after * gain
    mean_one = jnp.mean(grad_normed, axis=1, keepdims=True)
    mean_two = jnp.mean(grad_normed * normed, axis=1, keepdims=True)
    return inverse * (grad_normed - mean_one - normed * mean_two)


def head_groups(width):
    columns = min(128, width)
    return columns, columns // HD, width // columns


def attend_forward_kernel(width, block, qkv, ids_row, ids_col, *rest):
    out = rest[-1]
    length = qkv.shape[1]
    columns, per_group, groups = head_groups(width)
    lane = lax.broadcasted_iota(jnp.int32, (block, columns), 1) // HD

    @pl.loop(0, length // block)
    def _(step):
        rows = pl.ds(pl.multiple_of(step * block, block), block)
        same = ids_col[0, rows, :] == ids_row[0]
        for group in range(groups):
            first = group * columns
            queries = qkv[0, rows, first : first + columns]
            keys = qkv[0, :, width + first : width + first + columns]
            values = qkv[0, :, 2 * width + first : 2 * width + first + columns]
            result = None
            for head in range(per_group):
                masked = jnp.where(lane == head, queries, jnp.zeros_like(queries))
                scores = jnp.where(same, dot_t(masked, keys), HIDDEN_SCORE)
                top = jnp.max(scores, axis=1, keepdims=True)
                terms = jnp.exp2((scores - top) * EXP2_SCALE)
                total = jnp.sum(terms, axis=1, keepdims=True)
                part = dot(terms.astype(BF), values) / total
                result = part if result is None else jnp.where(lane == head, part, result)
            out[0, rows, first : first + columns] = result.astype(BF)


def attend_backward_kernel(width, block, qkv, grads, ids_row, ids_col, *rest):
    out, key_total, value_total = rest[-3:]
    length = qkv.shape[1]
    columns, per_group, groups = head_groups(width)
    lane = lax.broadcasted_iota(jnp.int32, (block, columns), 1) // HD
    key_lane = lax.broadcasted_iota(jnp.int32, (length, columns), 1) // HD
    for group in range(groups):
        first = group * columns
        keys = qkv[0, :, width + first : width + first + columns]
        values = qkv[0, :, 2 * width + first : 2 * width + first + columns]
        key_total[...] = jnp.zeros_like(key_total)
        value_total[...] = jnp.zeros_like(value_total)

        @pl.loop(0, length // block)
        def _(step):
            rows = pl.ds(pl.multiple_of(step * block, block), block)
            same = ids_col[0] == ids_row[0, :, rows]
            queries = qkv[0, rows, first : first + columns]
            tops = grads[rows, first : first + columns]
            query_grad = None
            for head in range(per_group):
                own = lane == head
                head_queries = jnp.where(own, queries, jnp.zeros_like(queries))
                head_grads = jnp.where(own, tops, jnp.zeros_like(tops))
                head_keys = jnp.where(key_lane == head, keys, jnp.zeros_like(keys))
                scores = jnp.where(same, dot_t(keys, head_queries), HIDDEN_SCORE)
                top = jnp.max(scores, axis=0, keepdims=True)
                terms = jnp.exp2((scores - top) * EXP2_SCALE)
                probs = terms * (1.0 / jnp.sum(terms, axis=0, keepdims=True))
                prob_grads = dot_t(values, head_grads)
                inner = jnp.sum(probs * prob_grads, axis=0, keepdims=True)
                score_grads = (probs * (prob_grads - inner)).astype(BF)
                value_total[...] += dot(probs.astype(BF), head_grads)
                key_total[...] += dot(score_grads, head_queries)
                part = t_dot(score_grads, head_keys)
                query_grad = part if query_grad is None else query_grad + part
            out[rows, first : first + columns] = (query_grad * SCALE).astype(BF)

        out[:, width + first : width + first + columns] = (key_total[...] * SCALE).astype(BF)
        out[:, 2 * width + first : 2 * width + first + columns] = value_total[...].astype(BF)


def whole_block(shape):
    return pl.BlockSpec((1,) + shape[1:], lambda s: (s, 0, 0))


def attend_forward(qkv, ids, earlier):
    count, length, columns = qkv.shape
    width = columns // 3
    ids_row, ids_col = ids[:, None, :], ids[:, :, None]
    return pl.pallas_call(
        partial(attend_forward_kernel, width, min(256, length)),
        grid=(count,),
        in_specs=[whole_block(v.shape) for v in (qkv, ids_row, ids_col)]
        + [pl.BlockSpec(memory_space=pl.ANY)] * len(earlier),
        out_specs=whole_block((count, length, width)),
        out_shape=jax.ShapeDtypeStruct((count, length, width), BF),
        compiler_params=pltpu.CompilerParams(vmem_limit_bytes=48 * 1024 * 1024),
        cost_estimate=pl.CostEstimate(flops=1024, bytes_accessed=1024, transcendentals=0),
    )(qkv, ids_row, ids_col, *earlier)


def attend_backward(qkv, grads, ids, which, earlier):
    _, length, columns = qkv.shape
    width = columns // 3
    group = head_groups(width)[0]
    ids_row, ids_col = ids[:, None, :], ids[:, :, None]

    def chosen(value):
        return pl.BlockSpec((1,) + value.shape[1:], lambda s: (which, 0, 0))

    return pl.pallas_call(
        partial(attend_backward_kernel, width, min(256, length)),
        grid=(1,),
        in_specs=[chosen(qkv), pl.BlockSpec((length, width), lambda s: (0, 0))]
        + [chosen(ids_row), chosen(ids_col)]
        + [pl.BlockSpec(memory_space=pl.ANY)] * len(earlier),
        out_specs=pl.BlockSpec((length, columns), lambda s: (0, 0)),
        out_shape=jax.ShapeDtypeStruct((length, columns), BF),
        scratch_shapes=[pltpu.VMEM((length, group), F32)] * 2,
        compiler_params=pltpu.CompilerParams(vmem_limit_bytes=48 * 1024 * 1024),
        cost_estimate=pl.CostEstimate(flops=1024, bytes_accessed=1024, transcendentals=0),
    )(qkv, grads, ids_row, ids_col, *earlier)


D_AX, R_AX, O_AX, I_AX = 0, 1, 2, 3


def gelu_pair(value):
    cdf = 0.5 * (1.0 + lax.erf(value * (0.5**0.5)))
    density = jnp.exp(-0.5 * value * value) * (1.0 / math.sqrt(2.0 * math.pi))
    return value * cdf, cdf + value * density


def on_device(
    sizes,
    tokens,
    segment_ids,
    in_weight,
    in_bias,
    out_weight,
    out_bias,
    gain_one,
    shift_one,
    up_weight,
    up_bias,
    down_weight,
    down_bias,
    gain_two,
    shift_two,
    cotangent,
):
    n_dp, n_row, n_col = sizes
    rows_here, model = tokens.shape
    n_outer, length = segment_ids.shape
    n_inner = length // rows_here
    assert n_dp == 2 and n_outer == 2 and n_outer * n_inner == n_col
    net = Grid(n_dp, n_row, n_outer, n_inner)
    d, r, c = (lax.axis_index(name) for name in ALL)
    o, i = c // n_inner, c % n_inner
    at_home = o == d
    width = in_weight.shape[1] // 3
    heads = width // HD
    part = model // n_row
    units = up_weight.shape[1]
    half = units // 2

    def place(k):
        return lax.rem(r - k + n_row, n_row)

    def other(value):
        return net.shift(value, D_AX, 1)

    def across_outer(value):
        return net.shift(value, O_AX, 1)

    def in_order(mine, theirs, axis):
        first = jnp.where(d == 0, mine, theirs)
        second = jnp.where(d == 0, theirs, mine)
        return jnp.concatenate([first, second], axis=axis)

    def gather_row(value, axis):
        shape = list(value.shape)
        step = shape[axis]
        shape[axis] = step * n_row
        result = jnp.zeros(shape, value.dtype)
        for k in range(n_row):
            block = value if k == 0 else net.shift(value, R_AX, k)
            result = lax.dynamic_update_slice_in_dim(result, block, place(k) * step, axis)
        return result

    def scatter_row(value, axis):
        step = value.shape[axis] // n_row
        own = lax.dynamic_slice_in_dim(value, r * step, step, axis).astype(F32)
        for k in range(1, n_row):
            block = lax.dynamic_slice_in_dim(value, place(k) * step, step, axis)
            own = own + net.shift(block.astype(BF), R_AX, -k).astype(F32)
        return own

    def gather_near(value):
        near = [value] + [net.shift(value, I_AX, k) for k in range(1, n_inner)]
        return near + [across_outer(value)]

    def gather_far(near, outer_share):
        near, away = near[:n_inner], near[n_inner]
        cut = int(away.shape[0] * outer_share)
        far = []
        for k in range(1, n_inner):
            pieces = [across_outer(near[k][:cut])]
            if cut < away.shape[0]:
                pieces.append(net.shift(away[cut:], I_AX, k))
            far.append(jnp.concatenate(pieces, axis=0))
        return near + [away] + far

    def scatter_far(blocks):
        near, far = blocks[:n_inner], blocks[n_inner:]
        cut = near[0].shape[0] // 2
        result, away = [near[0]], far[0]
        top, bottom = away[:cut], away[cut:]
        for k in range(1, n_inner):
            low = far[k].astype(BF)
            passed = across_outer(low[:cut]).astype(F32)
            bottom = bottom + net.shift(low[cut:], I_AX, -k).astype(F32)
            result.append(
                jnp.concatenate([near[k][:cut] + passed, near[k][cut:]], axis=0).astype(BF)
            )
        return result + [jnp.concatenate([top, bottom], axis=0).astype(BF)]

    def scatter_near(blocks):
        own = blocks[0] + across_outer(blocks[n_inner]).astype(F32)
        for k in range(1, n_inner):
            own = own + net.shift(blocks[k], I_AX, -k).astype(F32)
        return own

    def exchange_blocks(value, away):
        keep = jnp.where(at_home, value, away)
        return keep, other(jnp.where(at_home, away, value))

    def return_blocks(mine, theirs):
        received = other(theirs).astype(F32)
        keep = jnp.where(at_home, mine, received)
        away = jnp.where(at_home, received, mine)
        return keep + across_outer(away.astype(BF)).astype(F32)

    def join(value, axis):
        return in_order(value, other(value), axis)

    small = jnp.concatenate([in_bias, up_bias])
    small_near = gather_near(small)
    small_blocks = gather_far(small_near, 1.0)
    in_mine = in_weight.reshape(2, part // 2, heads, 3, HD)
    in_mine = lax.dynamic_index_in_dim(in_mine, d, 0, keepdims=False)
    in_mine = in_mine.transpose(0, 2, 1, 3).reshape(part // 2, 3 * width)
    in_row = gather_row(in_mine, 0)
    token_parts = [tokens]
    for k in range(1, n_inner):
        token_parts.append(net.shift(after(tokens, *small_near), I_AX, k))
    in_row, small_blocks = lax.optimization_barrier((in_row, small_blocks))
    in_away = across_outer(in_row)
    in_row, in_away, token_parts = lax.optimization_barrier((in_row, in_away, token_parts))
    in_halves = exchange_blocks(in_row, in_away)
    out_weight = after(out_weight, in_row)
    bias_rows = jnp.where(
        at_home, small_blocks[0][: 2 * width], small_blocks[n_inner][: 2 * width]
    ).reshape(heads, 2, HD)
    in_bias_row = jnp.concatenate(
        [bias_rows[:, 0].reshape(width), jnp.zeros((width,), F32), bias_rows[:, 1].reshape(width)]
    )
    up_bias_blocks = [
        lax.dynamic_slice_in_dim(v[2 * width :], d * half, half, 0) for v in small_blocks
    ]
    in_full = in_order(
        *(v.reshape(n_row, 1, part // 2, 3 * width) for v in in_halves), 1
    ).reshape(model, 3 * width)
    out_mine = lax.dynamic_slice_in_dim(out_weight, d * (width // 2), width // 2, 0)
    out_row = gather_row(out_mine, 1)
    out_away = across_outer(after(out_row, in_away))
    out_full = in_order(*exchange_blocks(out_row, out_away), 0)
    up_mine = lax.dynamic_slice_in_dim(up_weight, d * half, half, 1)
    up_row = gather_row(after(up_mine, out_row), 0)
    up_near = gather_near(after(up_row, out_away))
    def spread(parts):
        return jnp.concatenate(parts, axis=0), jnp.concatenate([other(v) for v in parts], axis=0)

    def collect(own_rows, other_rows, weights_of):
        own_rows, other_rows = (
            v.reshape(n_inner, rows_here, v.shape[-1]) for v in (own_rows, other_rows)
        )
        arrived = [other(weights_of(v).astype(BF)) for v in other_rows]
        result = None
        for k in range(1, n_inner):
            one = weights_of(own_rows[k]) + arrived[k].astype(F32)
            moved = net.shift(one.astype(BF), I_AX, -k).astype(F32)
            result = moved if result is None else result + moved
        own = weights_of(own_rows[0]) + arrived[0].astype(F32)
        return own if result is None else own + result

    own_ids = lax.dynamic_index_in_dim(segment_ids, o, 0, keepdims=False)
    own_ids = jnp.concatenate(
        [
            lax.dynamic_slice_in_dim(
                own_ids, lax.rem(i - k + n_inner, n_inner) * rows_here, rows_here, 0
            )
            for k in range(n_inner)
        ]
    )
    ids = jnp.stack([own_ids, other(own_ids)])

    token_full = jnp.concatenate(spread(token_parts), axis=0)
    projected = (dot(token_full, in_full) + in_bias_row).astype(BF)
    projected = projected.reshape(2, length, 3 * width)
    down_mine = lax.dynamic_slice_in_dim(down_weight, d * half, half, 0)
    down_row = gather_row(after(down_mine, projected), 1)
    attended = attend_forward(projected, ids, (up_row,))
    attended, up_near, down_row = lax.optimization_barrier((attended, up_near, down_row))
    down_away = across_outer(down_row)
    branch = collect(attended[0], attended[1], lambda v: dot(v, out_full))
    token_late = after(token_full, attended)
    step = part // 2
    halves_of = [
        jnp.concatenate(
            [token_late[:, k * step : (k + 1) * step] for k in range(at, 2 * n_row, 2)], axis=1
        )
        for at in range(2)
    ]
    token_halves = (
        jnp.where(d == 0, halves_of[0], halves_of[1]),
        jnp.where(d == 0, halves_of[1], halves_of[0]),
    )
    branch, down_away, token_halves = lax.optimization_barrier((branch, down_away, token_halves))
    up_blocks = gather_far(up_near, 1.0)
    down_near = gather_near(after(down_row, branch))[:n_inner] + [down_away]
    down_blocks = gather_far(down_near, 0.5)
    residual_one = tokens.astype(F32) + (branch + out_bias)
    normed_one, unit_one, inverse_one = norm_forward(residual_one, gain_one, shift_one)

    def both(value):
        return jnp.concatenate([value, other(value)], axis=0)

    def across(blocks, weights_of):
        def product(start):
            result = None
            for k, value in enumerate(blocks):
                one = weights_of(value[start : start + rows_here], k)
                result = one if result is None else result + one
            return result

        away = other(product(rows_here).astype(BF))
        return product(0) + away.astype(F32)

    mid = both(normed_one.astype(BF))
    hidden, slope = [], []
    for k in range(n_col):
        one = gelu_pair(dot(mid, up_blocks[k]) + up_bias_blocks[k])
        hidden.append(one[0].astype(BF))
        slope.append(one[1].astype(BF))
    residual_two = normed_one + (
        across(hidden, lambda v, k: dot(v, down_blocks[k])) + down_bias
    )
    normed_two, unit_two, inverse_two = norm_forward(residual_two, gain_two, shift_two)
    output = normed_two.astype(BF)

    grad_top = cotangent.astype(F32)
    grad_gain_two = jnp.sum(grad_top * unit_two, axis=0)
    grad_shift_two = jnp.sum(grad_top, axis=0)
    grad_two = norm_backward(grad_top, unit_two, inverse_two, gain_two)
    grad_two_low = grad_two.astype(BF)
    grad_down_bias = jnp.sum(grad_two_low.astype(F32), axis=0)
    grad_two_both = both(grad_two_low)
    grad_down = scatter_far([t_dot(v, grad_two_both) for v in hidden])
    grad_pre = [
        (dot_t(grad_two_both, down_blocks[k]) * slope[k].astype(F32)).astype(BF)
        for k in range(n_col)
    ]
    grad_pre, grad_down = lax.optimization_barrier((grad_pre, grad_down))
    grad_one = grad_two + across(grad_pre, lambda v, k: dot_t(v, up_blocks[k]))
    grad_up_bias = jnp.zeros((2, n_outer, n_inner, half), F32)
    for k in range(n_col):
        there_o = lax.rem(o - k // n_inner + n_outer, n_outer)
        there_i = lax.rem(i - k % n_inner + n_inner, n_inner)
        grad_up_bias = lax.dynamic_update_slice(
            grad_up_bias,
            jnp.sum(grad_pre[k].astype(F32), axis=0)[None, None, None],
            (d, there_o, there_i, 0),
        )

    grad_gain_one = jnp.sum(grad_one * unit_one, axis=0)
    grad_shift_one = jnp.sum(grad_one, axis=0)
    grad_first = norm_backward(grad_one, unit_one, inverse_one, gain_one)
    grad_first_low = grad_first.astype(BF)
    grad_out_bias = jnp.sum(grad_first_low.astype(F32), axis=0)

    first_parts = [grad_first_low]
    first_parts += [net.shift(grad_first_low, I_AX, k) for k in range(1, n_inner)]
    mid_late = after(mid, grad_first_low)
    grad_up = scatter_far([t_dot(mid_late, v) for v in grad_pre])
    grad_first_both = spread(first_parts)
    grad_attended = [dot_t(v, out_full).astype(BF) for v in grad_first_both]

    def halves(value, axis):
        step = value.shape[axis] // 2
        return [
            lax.dynamic_slice_in_dim(value, at * step, step, axis) for at in (d, 1 - d)
        ]

    out_mine, out_theirs = (
        [sum(t_dot(v, w) for v, w in zip(pair, grad_first_both)) for pair in
         zip(*(halves(v, 1) for v in attended))]
    )
    grad_out = return_blocks(out_mine, out_theirs.astype(BF))
    grad_down = scatter_near(grad_down)
    projected_grads = [None, None]
    projected_grads[1] = attend_backward(projected, grad_attended[1], ids, 1, (grad_down,))
    grad_down = scatter_row(grad_down, 1)
    grad_up = scatter_near(lax.optimization_barrier((grad_up, grad_out))[0])
    projected_grads[0] = attend_backward(
        projected, grad_attended[0], ids, 0, (grad_down, grad_out)
    )
    grad_out = scatter_row(grad_out, 1)
    projected_grads[0], grad_up, grad_out = lax.optimization_barrier(
        (projected_grads[0], grad_up, grad_out)
    )
    grad_tokens = grad_first + collect(*projected_grads, lambda v: dot_t(v, in_full))
    in_mine, in_theirs = (
        sum(t_dot(v[k * length : (k + 1) * length], w) for k, w in enumerate(projected_grads))
        for v in token_halves
    )
    grad_in = return_blocks(in_mine, in_theirs.astype(BF))
    grad_up = scatter_row(grad_up, 0)
    grad_in, grad_tokens, grad_up = lax.optimization_barrier((grad_in, grad_tokens, grad_up))
    grad_in_there = grad_in
    grad_in = scatter_row(grad_in, 0)
    bias_terms = sum(jnp.sum(v.astype(F32), axis=0) for v in projected_grads).reshape(3, heads, HD)
    bias_terms = jnp.stack([bias_terms[0], bias_terms[2]], axis=1).reshape(1, 2 * width)
    grad_in_bias = lax.dynamic_update_slice_in_dim(
        jnp.zeros((n_col, 2 * width), F32), bias_terms, d * n_inner + i, 0
    )

    flat = [
        grad_out_bias,
        grad_gain_one,
        grad_shift_one,
        grad_down_bias,
        grad_gain_two,
        grad_shift_two,
        grad_up_bias.reshape(-1),
        grad_in_bias.reshape(-1),
    ]
    flat = after(jnp.concatenate(flat).reshape(-1, 128), grad_in_there)
    sums = net.total(flat).reshape(-1)
    sums = jnp.split(sums, [model * k for k in range(1, 7)] + [6 * model + 2 * n_col * half])
    grad_up_bias = lax.dynamic_index_in_dim(
        sums[6].reshape(2, n_col, half), c, 1, keepdims=False
    ).reshape(2 * half)
    grad_in_bias = lax.dynamic_index_in_dim(
        sums[7].reshape(n_col, 2 * width), c, 0, keepdims=False
    )

    grad_down = join(grad_down, 0)
    grad_up = join(grad_up, 1)
    grad_out = join(grad_out, 0)
    grad_in = join(grad_in, 0)
    grad_in = grad_in.reshape(part, 3, heads, HD).transpose(0, 2, 1, 3).reshape(part, 3 * width)
    return (
        output,
        grad_tokens,
        grad_in,
        grad_in_bias,
        grad_out,
        sums[0],
        sums[1],
        sums[2],
        grad_up,
        grad_up_bias,
        grad_down,
        sums[3],
        sums[4],
        sums[5],
    )


def solution(mesh):
    return jax.shard_map(
        partial(on_device, tuple(mesh.shape[name] for name in ALL)),
        mesh=mesh,
        in_specs=(
            P(("dp", "row", "col"), None),
            P(("dp", "row"), None),
            P("row", "col"),
            P("col"),
            P("col", "row"),
            P(),
            P(),
            P(),
            P("row", "col"),
            P("col"),
            P("col", "row"),
            P(),
            P(),
            P(),
            P(("dp", "row", "col"), None),
        ),
        out_specs=(
            P(("dp", "row", "col"), None),
            P(("dp", "row", "col"), None),
            P("row", "col"),
            P("col"),
            P("col", "row"),
            P(),
            P(),
            P(),
            P("row", "col"),
            P("col"),
            P("col", "row"),
            P(),
            P(),
            P(),
        ),
        check_vma=False,
    )
```

time: 604 us -> 455 us (0.75)
  waiting for transfers between devices: 261 us -> 148 us
  starting transfers between devices: 135 us -> 76.6 us
  matrix products: 74 us -> 91.1 us
  local copies, waits for them, and re-layouts: 26.5 us -> 19.6 us
  other arithmetic: 34 us -> 40.5 us
    ppermute x9 -> x5, waiting for transfers between devices: 71.7 us -> 7.1 us  [flip(): return lax.ppermute(value, ALL, self.pairs(target))]
    ppermute x59 -> x71, starting transfers between devices: 116 us -> 71.8 us  [shift(): return lax.ppermute(value, ALL, self.pairs(target))]
    ppermute x59 -> x71, waiting for transfers between devices: 183 us -> 141 us  [shift(): return lax.ppermute(value, ALL, self.pairs(target))]
    ppermute x6 -> x0, starting transfers between devices: 10.6 us -> none  [the longest x3 6.78 us: send_home(): return lax.ppermute(value, ALL, self.pairs(target))]
    dot_general x8 -> x17, matrix products: 18.8 us -> 26.7 us  [dot(): return jnp.dot(left, right, preferred_element_type=F32)]
    dot_general x7 -> x16, matrix products: 21.6 us -> 28.6 us  [t_dot(): lax.dot_general(left, right, (((0,), (0,)), ((), ())), preferred_element_...]
    concatenate x3 -> x10, other arithmetic: 1.71 us -> 8.69 us  [the longest x5 3 us: in_order(): return jnp.concatenate([first, second], axis=axis)]
    reduce_sum x1 -> x7, other arithmetic: 0.51 us -> 7.37 us  [the longest x1 4.75 us: on_device(): grad_gain_one = jnp.sum(grad_one * unit_one, axis=0)]
  transfers between devices with their start and end apart: 74 -> 76, of which waited for: 23 -> 28; matrix products, arithmetic and copies ran while one was open for 16% -> 27% of each run, Pallas kernels for 11% -> 10%
where the time goes in v2:
time: 455 us; the launch traced here: 446 us
  waiting for transfers between devices  148 us (33%)
  matrix products  91.1 us (20%)
  starting transfers between devices  76.6 us (17%)
  Pallas kernels  66.9 us (15%)
  other arithmetic  40.5 us (9%)
  local copies, waits for them, and re-layouts  19.6 us (4%)
    ppermute x71, waiting for transfers between devices, shift(): return lax.ppermute(value, ALL, self.pairs(target))  141 us
    ppermute x71, starting transfers between devices, shift(): return lax.ppermute(value, ALL, self.pairs(target))  71.8 us
    pallas_call x2, Pallas kernels, attend_backward(): pl.pallas_call(partial(attend_backward_kernel, width, min(256, length)),...  47.9 us
    dot_general x18, matrix products, dot_t(): lax.dot_general(left, right, (((1,), (1,)), ((), ())), preferred_element_...  35.8 us
    dot_general x16, matrix products, t_dot(): lax.dot_general(left, right, (((0,), (0,)), ((), ())), preferred_element_...  28.6 us
    dot_general x17, matrix products, dot(): return jnp.dot(left, right, preferred_element_type=F32)  26.7 us
    pallas_call x1, Pallas kernels, attend_forward(): pl.pallas_call(partial(attend_forward_kernel, width, min(256, length)), g...  19 us
    unnamed x189, local copies, waits for them, and re-layouts  9.32 us
  transfers between devices with their start and end apart: 76, of which 28 were waited for; matrix products, arithmetic and copies ran while one was open for 27% of the time, Pallas kernels for 10%

profile of v2, /device:TPU:11, one launch (start us, length us, event | category | flops | bytes accessed | tf_op | source)
XLA Modules:
  0.0 445.7 jit_solution(12069271075845140910)
XLA Ops:
  13.3 6.9 %collective-permute-done.1 = bf16[128,768]{1,0:T(8,128)(2,1)S(1)} collective-permute-done((bf16[128,768]{1,0:T(8,128)(2,1)S(1)}, bf16[128,768]{1,0:T(8,128)(2,1)S(1)}, u32[]{:S(2)}, u32[]{:S(2)}) %collective-permute-start.1) | collective-permute-done | bytes 196640 | tf_op jit(solution)/shard_map/ppermute | solution.py:49
  26.7 15.3 %collective-permute-done.6 = bf16[512,768]{1,0:T(8,128)(2,1)S(1)} collective-permute-done((bf16[512,768]{1,0:T(8,128)(2,1)S(1)}, bf16[512,768]{1,0:T(8,128)(2,1)S(1)}, u32[]{:S(2)}, u32[]{:S(2)}) %collective-permute-start.6) | collective-permute-done | bytes 786464 | tf_op jit(solution)/shard_map/ppermute | solution.py:49
  49.5 3.2 collective-permute-done.14
  61.4 13.7 %collective-permute-done.16 = bf16[256,512]{1,0:T(8,128)(2,1)S(1)} collective-permute-done((bf16[256,512]{1,0:T(8,128)(2,1)S(1)}, bf16[256,512]{1,0:T(8,128)(2,1)S(1)}, u32[]{:S(2)}, u32[]{:S(2)}) %collective-permute-start.16) | collective-permute-done | bytes 262176 | tf_op jit(solution)/shard_map/ppermute | solution.py:49
  81.5 4.8 %add_convert_fusion = bf16[2048,768]{1,0:T(8,128)(2,1)} fusion(bf16[2048,1024]{1,0:T(8,128)(2,1)S(1)} %constant_dynamic-update-slice_fusion.1, bf16[1024,768]{1,0:T(8,128)(2,1)S(1)} %bitcast.131, f32[768]{0:T(1024)S(1)} %pad_maximum_fusion.18), kind=kOutput, calls=%fused_computation | convolution fusion | flops 3224371200 | bytes 8915968 | tf_op jit(solution)/shard_map/dot_general | solution.py:70
  89.7 19.0 %shard_map.254 = bf16[2,1024,256]{2,1,0:T(8,128)(2,1)S(1)} custom-call(bf16[2,1024,768]{2,1,0:T(8,128)(2,1)} %bitcast.124, s32[2,1,1024]{2,1,0:T(1,128)S(1)} %broadcast_in_dim.28.ids_row, s32[2,1024,1]{2,1,0:T(8,128)S(1)} %copy.55.ids_col, bf16[1024,512]{1,0:T(8,128)(2,1)S(1)} %constant_dynamic-update-slice_fusion.14.rest_0_), custom_call_target="tpu_custom_call" | custom-call | flops 1024 | bytes 1024 | tf_op jit(solution)/shard_map/pallas_call | solution.py:182
  119.9 19.1 %collective-permute-done.27 = bf16[512,1024]{1,0:T(8,128)(2,1)S(1)} collective-permute-done((bf16[512,1024]{1,0:T(8,128)(2,1)S(1)}, bf16[512,1024]{1,0:T(8,128)(2,1)S(1)}, u32[]{:S(2)}, u32[]{:S(2)}) %collective-permute-start.27) | collective-permute-done | bytes 1048608 | tf_op jit(solution)/shard_map/ppermute | solution.py:49
  146.4 3.4 multiply_convert_fusion.5
  150.6 17.6 %collective-permute-done.30 = bf16[512,1024]{1,0:T(8,128)(2,1)S(1)} collective-permute-done((bf16[512,1024]{1,0:T(8,128)(2,1)S(1)}, bf16[512,1024]{1,0:T(8,128)(2,1)S(1)}, u32[]{:S(2)}, u32[]{:S(2)}) %collective-permute-start.30) | collective-permute-done | bytes 1048608 | tf_op jit(solution)/shard_map/ppermute | solution.py:49
  169.3 3.4 multiply_convert_fusion.7
  173.5 3.4 multiply_convert_fusion.6
  177.7 3.9 multiply_convert_fusion.4
  199.7 4.3 fusion.121
  204.0 3.6 multiply_convert_fusion.3
  207.6 3.8 multiply_convert_fusion.2
  211.5 4.0 multiply_convert_fusion.1
  215.5 3.8 multiply_convert_fusion
  219.3 3.2 fusion.120
  244.3 4.8 %multiply_reduce_fusion = (f32[1024]{0:T(1024)S(1)}, f32[512]{0:T(512)S(1)}, f32[512]{0:T(512)S(1)}, f32[1024]{0:T(1024)S(1)}, f32[512,1024]{1,0:T(8,128)S(1)}, /*index=5*/bf16[512,1024]{1,0:T(8,128)(2,1)}) fusion(f32[512,1024]{1,0:T(8,128)S(1)} %copy-done.3, f32[512]{0:T(512)S(1)} %get-tuple-element.210, f32[512]{0:T(512)S(1)} %get-tuple-element.209, ...), kind=kLoop, calls=%fused_computation.47 | loop fusion | flops 13628416 | bytes 17862656 | tf_op jit(solution)/shard_map/reduce_sum | solution.py:478
  255.6 5.6 %collective-permute-done.41 = bf16[512,1024]{1,0:T(8,128)(2,1)} collective-permute-done((bf16[512,1024]{1,0:T(8,128)(2,1)}, bf16[512,1024]{1,0:T(8,128)(2,1)}, u32[]{:S(2)}, u32[]{:S(2)}) %collective-permute-start.41) | collective-permute-done | bytes 1048608 | tf_op jit(solution)/shard_map/ppermute | solution.py:49
  270.5 3.6 collective-permute-start.45
  274.2 11.3 %collective-permute-done.43 = bf16[512,256]{1,0:T(8,128)(2,1)S(1)} collective-permute-done((bf16[512,256]{1,0:T(8,128)(2,1)S(1)}, bf16[512,256]{1,0:T(8,128)(2,1)S(1)}, u32[]{:S(2)}, u32[]{:S(2)}) %collective-permute-start.43) | collective-permute-done | bytes 262176 | tf_op jit(solution)/shard_map/ppermute | solution.py:49
  291.3 5.9 %collective-permute-done.50 = bf16[512,512]{1,0:T(8,128)(2,1)S(1)} collective-permute-done((bf16[512,512]{1,0:T(8,128)(2,1)S(1)}, bf16[512,512]{1,0:T(8,128)(2,1)S(1)}, u32[]{:S(2)}, u32[]{:S(2)}) %collective-permute-start.50) | collective-permute-done | bytes 524320 | tf_op jit(solution)/shard_map/ppermute | solution.py:49
  303.2 24.1 %shard_map.256 = bf16[1024,768]{1,0:T(8,128)(2,1)S(1)} custom-call(bf16[2,1024,768]{2,1,0:T(8,128)(2,1)} %bitcast.125, bf16[1024,256]{1,0:T(8,128)(2,1)S(1)} %convolution_convert_fusion.6.grads, s32[2,1,1024]{2,1,0:T(1,128)S(1)} %broadcast_in_dim.28.ids_row, s32[2,1024,1]{2,1,0:T(8,128)S(1)} %copy.55.ids_col, f32[512,1024]{1,0:T(8,128)S(1)} %convert_add_fusion.1.rest_0_), custom_call_target="tpu_custom_call" | custom-call | flops 1024 | bytes 1024 | tf_op jit(solution)/shard_map/pallas_call | solution.py:203
  336.6 3.6 collective-permute-done.48
  353.3 23.8 %shard_map.255 = bf16[1024,768]{1,0:T(8,128)(2,1)S(1)} custom-call(bf16[2,1024,768]{2,1,0:T(8,128)(2,1)} %bitcast.126, bf16[1024,256]{1,0:T(8,128)(2,1)S(1)} %convolution_convert_fusion.7.grads, s32[2,1,1024]{2,1,0:T(1,128)S(1)} %broadcast_in_dim.28.ids_row, s32[2,1024,1]{2,1,0:T(8,128)S(1)} %copy.55.ids_col, f32[512,256]{1,0:T(8,128)S(1)} %convert_add_fusion.4.rest_0_, ...), custom_call_target="tpu_custom_call" | custom-call | flops 1024 | bytes 1024 | tf_op jit(solution)/shard_map/pallas_call | solution.py:203
  381.6 3.2 add_convert_fusion.1
  386.5 3.5 collective-permute-start.62
  395.3 13.6 %collective-permute-done.62 = bf16[256,512]{1,0:T(8,128)(2,1)} collective-permute-done((bf16[256,512]{1,0:T(8,128)(2,1)}, bf16[256,512]{1,0:T(8,128)(2,1)}, u32[]{:S(2)}, u32[]{:S(2)}) %collective-permute-start.62) | collective-permute-done | bytes 262176 | tf_op jit(solution)/shard_map/ppermute | solution.py:49
  413.4 3.6 add_add_fusion
  431.2 4.6 %collective-permute-done.71 = f32[96,128]{1,0:T(8,128)S(1)} collective-permute-done((f32[96,128]{1,0:T(8,128)S(1)}, f32[96,128]{1,0:T(8,128)S(1)}, u32[]{:S(2)}, u32[]{:S(2)}) %collective-permute-start.71) | collective-permute-done | bytes 49184 | tf_op jit(solution)/shard_map/ppermute | solution.py:57
  437.0 3.1 collective-permute-done.64
  (507 shorter events, 192.0 us)
Async XLA Ops:
  11.8 30.2 %collective-permute-start.7 = (bf16[512,1024]{1,0:T(8,128)(2,1)}, bf16[512,1024]{1,0:T(8,128)(2,1)}, u32[]{:S(2)}, u32[]{:S(2)}) collective-permute-start(bf16[512,1024]{1,0:T(8,128)(2,1)} %param.15), channel_id=1, source_target_pairs={{0,1},{1,0},{2,3},{3,2},{4,5},{5,4},{6,7},{7,6},{8,9},{9,8},{10,11... | collective-permute-start | bytes 3145736 | tf_op jit(solution)/shard_map/ppermute | solution.py:49
  43.6 37.8 %collective-permute-start.8 = (bf16[512,1024]{1,0:T(8,128)(2,1)}, bf16[512,1024]{1,0:T(8,128)(2,1)S(1)}, u32[]{:S(2)}, u32[]{:S(2)}) collective-permute-start(bf16[512,1024]{1,0:T(8,128)(2,1)} %param.15), channel_id=1, source_target_pairs={{0,16},{1,17},{2,18},{3,19},{4,20},{5,21},{6,22},{7,23},{8,24},{9,... | collective-permute-start | bytes 3145736 | tf_op jit(solution)/shard_map/ppermute | solution.py:49
  52.9 27.1 %collective-permute-start.10 = (bf16[512,768]{1,0:T(8,128)(2,1)S(1)}, bf16[512,768]{1,0:T(8,128)(2,1)S(1)}, u32[]{:S(2)}, u32[]{:S(2)}) collective-permute-start(bf16[512,768]{1,0:T(8,128)(2,1)S(1)} %broadcast_select_fusion.2), channel_id=1, source_target_pairs={{0,16},{1,17},{2,18},{3,19},{4,20},{5,21},{6,22},{7,23},{8,24},{9,... | collective-permute-start | bytes 2359304 | tf_op jit(solution)/shard_map/ppermute | solution.py:49
  53.4 21.8 %collective-permute-start.16 = (bf16[256,512]{1,0:T(8,128)(2,1)S(1)}, bf16[256,512]{1,0:T(8,128)(2,1)S(1)}, u32[]{:S(2)}, u32[]{:S(2)}) collective-permute-start(bf16[256,512]{1,0:T(8,128)(2,1)S(1)} %constant_dynamic-slice_fusion.4), channel_id=1, source_target_pairs={{0,8},{1,9},{2,10},{3,11},{4,12},{5,13},{6,14},{7,15},{8,0},{9,1},... | collective-permute-start | bytes 786440 | tf_op jit(solution)/shard_map/ppermute | solution.py:49
  78.4 32.4 %collective-permute-start.19 = (bf16[1024,512]{1,0:T(8,128)(2,1)S(1)}, bf16[1024,512]{1,0:T(8,128)(2,1)S(1)}, u32[]{:S(2)}, u32[]{:S(2)}) collective-permute-start(bf16[1024,512]{1,0:T(8,128)(2,1)S(1)} %constant_dynamic-update-slice_fusion.14.rest_0_), channel_id=1, source_target_pairs={{0,1},{1,0},{2,3},{3,2},{4,5},{5,4},{6,7},{7,6},{8,9},{9,8},{10,11... | collective-permute-start | bytes 3145736 | tf_op jit(solution)/shard_map/ppermute | solution.py:49
  78.7 32.1 %collective-permute-start.20 = (bf16[1024,512]{1,0:T(8,128)(2,1)S(1)}, bf16[1024,512]{1,0:T(8,128)(2,1)S(1)}, u32[]{:S(2)}, u32[]{:S(2)}) collective-permute-start(bf16[1024,512]{1,0:T(8,128)(2,1)S(1)} %constant_dynamic-update-slice_fusion.14.rest_0_), channel_id=1, source_target_pairs={{0,2},{1,3},{2,0},{3,1},{4,6},{5,7},{6,4},{7,5},{8,10},{9,11},{10,... | collective-permute-start | bytes 3145736 | tf_op jit(solution)/shard_map/ppermute | solution.py:49
  86.3 22.4 %collective-permute-start.21 = (bf16[512,256]{1,0:T(8,128)(2,1)}, bf16[512,256]{1,0:T(8,128)(2,1)S(1)}, u32[]{:S(2)}, u32[]{:S(2)}) collective-permute-start(bf16[512,256]{1,0:T(8,128)(2,1)} %constant_dynamic-slice_fusion.2), channel_id=1, source_target_pairs={{0,4},{1,5},{2,6},{3,7},{4,8},{5,9},{6,10},{7,11},{8,12},{9,13},{1... | collective-permute-start | bytes 786440 | tf_op jit(solution)/shard_map/ppermute | solution.py:49
  86.3 23.1 %collective-permute-start.22 = (bf16[512,256]{1,0:T(8,128)(2,1)}, bf16[512,256]{1,0:T(8,128)(2,1)S(1)}, u32[]{:S(2)}, u32[]{:S(2)}) collective-permute-start(bf16[512,256]{1,0:T(8,128)(2,1)} %constant_dynamic-slice_fusion.2), channel_id=1, source_target_pairs={{0,8},{1,9},{2,10},{3,11},{4,12},{5,13},{6,14},{7,15},{8,0},{9,1},... | collective-permute-start | bytes 786440 | tf_op jit(solution)/shard_map/ppermute | solution.py:49
  86.9 23.8 %collective-permute-start.23 = (bf16[512,256]{1,0:T(8,128)(2,1)}, bf16[512,256]{1,0:T(8,128)(2,1)S(1)}, u32[]{:S(2)}, u32[]{:S(2)}) collective-permute-start(bf16[512,256]{1,0:T(8,128)(2,1)} %constant_dynamic-slice_fusion.2), channel_id=1, source_target_pairs={{0,12},{1,13},{2,14},{3,15},{4,0},{5,1},{6,2},{7,3},{8,4},{9,5},{1... | collective-permute-start | bytes 786440 | tf_op jit(solution)/shard_map/ppermute | solution.py:49
  112.3 27.2 %collective-permute-start.28 = (bf16[512,1024]{1,0:T(8,128)(2,1)S(1)}, bf16[512,1024]{1,0:T(8,128)(2,1)S(1)}, u32[]{:S(2)}, u32[]{:S(2)}) collective-permute-start(bf16[512,1024]{1,0:T(8,128)(2,1)S(1)} %constant_dynamic-update-slice_fusion.10), channel_id=1, source_target_pairs={{0,2},{1,3},{2,0},{3,1},{4,6},{5,7},{6,4},{7,5},{8,10},{9,11},{10,... | collective-permute-start | bytes 3145736 | tf_op jit(solution)/shard_map/ppermute | solution.py:49
  114.5 24.4 %collective-permute-start.27 = (bf16[512,1024]{1,0:T(8,128)(2,1)S(1)}, bf16[512,1024]{1,0:T(8,128)(2,1)S(1)}, u32[]{:S(2)}, u32[]{:S(2)}) collective-permute-start(bf16[512,1024]{1,0:T(8,128)(2,1)S(1)} %add_convert_fusion.5), channel_id=1, source_target_pairs={{0,1},{1,0},{2,3},{3,2},{4,5},{5,4},{6,7},{7,6},{8,9},{9,8},{10,11... | collective-permute-start | bytes 3145736 | tf_op jit(solution)/shard_map/ppermute | solution.py:49
  143.5 24.7 %collective-permute-start.30 = (bf16[512,1024]{1,0:T(8,128)(2,1)S(1)}, bf16[512,1024]{1,0:T(8,128)(2,1)S(1)}, u32[]{:S(2)}, u32[]{:S(2)}) collective-permute-start(bf16[512,1024]{1,0:T(8,128)(2,1)S(1)} %constant_dynamic-update-slice_fusion.10), channel_id=1, source_target_pairs={{0,1},{1,0},{2,3},{3,2},{4,5},{5,4},{6,7},{7,6},{8,9},{9,8},{10,11... | collective-permute-start | bytes 3145736 | tf_op jit(solution)/shard_map/ppermute | solution.py:49
  145.0 32.7 %collective-permute-start.31 = (bf16[1024,512]{1,0:T(8,128)(2,1)S(1)}, bf16[1024,512]{1,0:T(8,128)(2,1)S(1)}, u32[]{:S(2)}, u32[]{:S(2)}) collective-permute-start(bf16[1024,512]{1,0:T(8,128)(2,1)S(1)} %collective-permute-done.19), channel_id=1, source_target_pairs={{0,2},{1,3},{2,0},{3,1},{4,6},{5,7},{6,4},{7,5},{8,10},{9,11},{10,... | collective-permute-start | bytes 3145736 | tf_op jit(solution)/shard_map/ppermute | solution.py:49
  145.3 36.4 %collective-permute-start.33 = (bf16[256,1024]{1,0:T(8,128)(2,1)S(1)}, bf16[256,1024]{1,0:T(8,128)(2,1)S(1)}, u32[]{:S(2)}, u32[]{:S(2)}) collective-permute-start(bf16[256,1024]{1,0:T(8,128)(2,1)S(1)} %slice.247), channel_id=1, source_target_pairs={{0,1},{1,0},{2,3},{3,2},{4,5},{5,4},{6,7},{7,6},{8,9},{9,8},{10,11... | collective-permute-start | bytes 1572872 | tf_op jit(solution)/shard_map/ppermute | solution.py:49
  198.0 27.6 %collective-permute-start.36 = (bf16[256,1024]{1,0:T(8,128)(2,1)S(1)}, bf16[256,1024]{1,0:T(8,128)(2,1)S(1)}, u32[]{:S(2)}, u32[]{:S(2)}) collective-permute-start(bf16[256,1024]{1,0:T(8,128)(2,1)S(1)} %get-tuple-element.185), channel_id=1, source_target_pairs={{0,2},{1,3},{2,0},{3,1},{4,6},{5,7},{6,4},{7,5},{8,10},{9,11},{10,... | collective-permute-start | bytes 1572872 | tf_op jit(solution)/shard_map/ppermute | solution.py:49
  198.5 28.3 %collective-permute-start.37 = (bf16[256,1024]{1,0:T(8,128)(2,1)S(1)}, bf16[256,1024]{1,0:T(8,128)(2,1)S(1)}, u32[]{:S(2)}, u32[]{:S(2)}) collective-permute-start(bf16[256,1024]{1,0:T(8,128)(2,1)S(1)} %get-tuple-element.184), channel_id=1, source_target_pairs={{0,1},{1,0},{2,3},{3,2},{4,5},{5,4},{6,7},{7,6},{8,9},{9,8},{10,11... | collective-permute-start | bytes 1572872 | tf_op jit(solution)/shard_map/ppermute | solution.py:49
  236.2 25.1 %collective-permute-start.41 = (bf16[512,1024]{1,0:T(8,128)(2,1)}, bf16[512,1024]{1,0:T(8,128)(2,1)}, u32[]{:S(2)}, u32[]{:S(2)}) collective-permute-start(bf16[512,1024]{1,0:T(8,128)(2,1)} %pad_maximum_fusion.6), channel_id=1, source_target_pairs={{0,1},{1,0},{2,3},{3,2},{4,5},{5,4},{6,7},{7,6},{8,9},{9,8},{10,11... | collective-permute-start | bytes 3145736 | tf_op jit(solution)/shard_map/ppermute | solution.py:49
  236.7 24.8 %collective-permute-start.40 = (bf16[512,1024]{1,0:T(8,128)(2,1)}, bf16[512,1024]{1,0:T(8,128)(2,1)}, u32[]{:S(2)}, u32[]{:S(2)}) collective-permute-start(bf16[512,1024]{1,0:T(8,128)(2,1)} %pad_maximum_fusion.7), channel_id=1, source_target_pairs={{0,2},{1,3},{2,0},{3,1},{4,6},{5,7},{6,4},{7,5},{8,10},{9,11},{10,... | collective-permute-start | bytes 3145736 | tf_op jit(solution)/shard_map/ppermute | solution.py:49
  251.1 40.2 %collective-permute-start.39 = (bf16[512,1024]{1,0:T(8,128)(2,1)S(1)}, bf16[512,1024]{1,0:T(8,128)(2,1)S(1)}, u32[]{:S(2)}, u32[]{:S(2)}) collective-permute-start(bf16[512,1024]{1,0:T(8,128)(2,1)S(1)} %get-tuple-element.147), channel_id=1, source_target_pairs={{0,1},{1,0},{2,3},{3,2},{4,5},{5,4},{6,7},{7,6},{8,9},{9,8},{10,11... | collective-permute-start | bytes 3145736 | tf_op jit(solution)/shard_map/ppermute | solution.py:49
  263.8 21.6 %collective-permute-start.43 = (bf16[512,256]{1,0:T(8,128)(2,1)S(1)}, bf16[512,256]{1,0:T(8,128)(2,1)S(1)}, u32[]{:S(2)}, u32[]{:S(2)}) collective-permute-start(bf16[512,256]{1,0:T(8,128)(2,1)S(1)} %get-tuple-element.172), channel_id=1, source_target_pairs={{0,8},{1,9},{2,10},{3,11},{4,12},{5,13},{6,14},{7,15},{8,0},{9,1},... | collective-permute-start | bytes 786440 | tf_op jit(solution)/shard_map/ppermute | solution.py:49
  265.8 23.6 %collective-permute-start.42 = (bf16[512,256]{1,0:T(8,128)(2,1)S(1)}, bf16[512,256]{1,0:T(8,128)(2,1)S(1)}, u32[]{:S(2)}, u32[]{:S(2)}) collective-permute-start(bf16[512,256]{1,0:T(8,128)(2,1)S(1)} %get-tuple-element.170), channel_id=1, source_target_pairs={{0,12},{1,13},{2,14},{3,15},{4,0},{5,1},{6,2},{7,3},{8,4},{9,5},{1... | collective-permute-start | bytes 786440 | tf_op jit(solution)/shard_map/ppermute | solution.py:49
  267.2 22.9 %collective-permute-start.49 = (bf16[512,512]{1,0:T(8,128)(2,1)S(1)}, bf16[512,512]{1,0:T(8,128)(2,1)S(1)}, u32[]{:S(2)}, u32[]{:S(2)}) collective-permute-start(bf16[512,512]{1,0:T(8,128)(2,1)S(1)} %get-tuple-element.181), channel_id=1, source_target_pairs={{0,2},{1,3},{2,0},{3,1},{4,6},{5,7},{6,4},{7,5},{8,10},{9,11},{10,... | collective-permute-start | bytes 1572872 | tf_op jit(solution)/shard_map/ppermute | solution.py:49
  270.5 29.3 %collective-permute-start.45 = (bf16[512,1024]{1,0:T(8,128)(2,1)S(1)}, bf16[512,1024]{1,0:T(8,128)(2,1)S(1)}, u32[]{:S(2)}, u32[]{:S(2)}) collective-permute-start(bf16[512,1024]{1,0:T(8,128)(2,1)S(1)} %get-tuple-element.147), channel_id=1, source_target_pairs={{0,16},{1,17},{2,18},{3,19},{4,20},{5,21},{6,22},{7,23},{8,24},{9,... | collective-permute-start | bytes 3145736 | tf_op jit(solution)/shard_map/ppermute | solution.py:49
  340.3 37.6 %collective-permute-start.52 = (bf16[1024,512]{1,0:T(8,128)(2,1)S(1)}, bf16[1024,512]{1,0:T(8,128)(2,1)S(1)}, u32[]{:S(2)}, u32[]{:S(2)}) collective-permute-start(bf16[1024,512]{1,0:T(8,128)(2,1)S(1)} %copy-done.58), channel_id=1, source_target_pairs={{0,1},{1,0},{2,3},{3,2},{4,5},{5,4},{6,7},{7,6},{8,9},{9,8},{10,11... | collective-permute-start | bytes 3145736 | tf_op jit(solution)/shard_map/ppermute | solution.py:49
  341.3 36.6 %collective-permute-start.51 = (bf16[1024,512]{1,0:T(8,128)(2,1)S(1)}, bf16[1024,512]{1,0:T(8,128)(2,1)}, u32[]{:S(2)}, u32[]{:S(2)}) collective-permute-start(bf16[1024,512]{1,0:T(8,128)(2,1)S(1)} %copy-done.59), channel_id=1, source_target_pairs={{0,2},{1,3},{2,0},{3,1},{4,6},{5,7},{6,4},{7,5},{8,10},{9,11},{10,... | collective-permute-start | bytes 3145736 | tf_op jit(solution)/shard_map/ppermute | solution.py:49
  345.8 35.8 %collective-permute-start.59 = (bf16[512,1024]{1,0:T(8,128)(2,1)}, bf16[512,1024]{1,0:T(8,128)(2,1)}, u32[]{:S(2)}, u32[]{:S(2)}) collective-permute-start(bf16[512,1024]{1,0:T(8,128)(2,1)} %convolution_convert_fusion), channel_id=1, source_target_pairs={{0,16},{1,17},{2,18},{3,19},{4,20},{5,21},{6,22},{7,23},{8,24},{9,... | collective-permute-start | bytes 3145736 | tf_op jit(solution)/shard_map/ppermute | solution.py:49
  348.3 28.8 %collective-permute-start.54 = (bf16[128,256]{1,0:T(8,128)(2,1)S(1)}, bf16[128,256]{1,0:T(8,128)(2,1)S(1)}, u32[]{:S(2)}, u32[]{:S(2)}) collective-permute-start(bf16[128,256]{1,0:T(8,128)(2,1)S(1)} %get-tuple-element.192), channel_id=1, source_target_pairs={{0,8},{1,9},{2,10},{3,11},{4,12},{5,13},{6,14},{7,15},{8,0},{9,1},... | collective-permute-start | bytes 196616 | tf_op jit(solution)/shard_map/ppermute | solution.py:49
  351.3 26.4 %collective-permute-start.53 = (bf16[128,256]{1,0:T(8,128)(2,1)S(1)}, bf16[128,256]{1,0:T(8,128)(2,1)S(1)}, u32[]{:S(2)}, u32[]{:S(2)}) collective-permute-start(bf16[128,256]{1,0:T(8,128)(2,1)S(1)} %get-tuple-element.190), channel_id=1, source_target_pairs={{0,12},{1,13},{2,14},{3,15},{4,0},{5,1},{6,2},{7,3},{8,4},{9,5},{1... | collective-permute-start | bytes 196616 | tf_op jit(solution)/shard_map/ppermute | solution.py:49
  377.1 36.3 %collective-permute-start.58 = (bf16[512,1024]{1,0:T(8,128)(2,1)}, bf16[512,1024]{1,0:T(8,128)(2,1)}, u32[]{:S(2)}, u32[]{:S(2)}) collective-permute-start(bf16[512,1024]{1,0:T(8,128)(2,1)} %convolution_convert_fusion.1), channel_id=1, source_target_pairs={{0,16},{1,17},{2,18},{3,19},{4,20},{5,21},{6,22},{7,23},{8,24},{9,... | collective-permute-start | bytes 3145736 | tf_op jit(solution)/shard_map/ppermute | solution.py:49
  384.8 28.6 %collective-permute-start.60 = (bf16[512,1024]{1,0:T(8,128)(2,1)}, bf16[512,1024]{1,0:T(8,128)(2,1)}, u32[]{:S(2)}, u32[]{:S(2)}) collective-permute-start(bf16[512,1024]{1,0:T(8,128)(2,1)} %add_convert_fusion.1), channel_id=1, source_target_pairs={{0,1},{1,0},{2,3},{3,2},{4,5},{5,4},{6,7},{7,6},{8,9},{9,8},{10,11... | collective-permute-start | bytes 3145736 | tf_op jit(solution)/shard_map/ppermute | solution.py:49
  386.5 22.4 %collective-permute-start.62 = (bf16[256,512]{1,0:T(8,128)(2,1)}, bf16[256,512]{1,0:T(8,128)(2,1)}, u32[]{:S(2)}, u32[]{:S(2)}) collective-permute-start(bf16[256,512]{1,0:T(8,128)(2,1)} %get-tuple-element.169), channel_id=1, source_target_pairs={{0,8},{1,9},{2,10},{3,11},{4,12},{5,13},{6,14},{7,15},{8,0},{9,1},... | collective-permute-start | bytes 786440 | tf_op jit(solution)/shard_map/ppermute | solution.py:49
  394.5 22.6 %collective-permute-start.57 = (bf16[512,768]{1,0:T(8,128)(2,1)S(1)}, bf16[512,768]{1,0:T(8,128)(2,1)S(1)}, u32[]{:S(2)}, u32[]{:S(2)}) collective-permute-start(bf16[512,768]{1,0:T(8,128)(2,1)S(1)} %get-tuple-element.221), channel_id=1, source_target_pairs={{0,2},{1,3},{2,0},{3,1},{4,6},{5,7},{6,4},{7,5},{8,10},{9,11},{10,... | collective-permute-start | bytes 2359304 | tf_op jit(solution)/shard_map/ppermute | solution.py:49
  (130 other events, 1357.9 us)

commit v3 on v2

v3 whole, which is shorter than its diff:
```python
from functools import partial
import math

import jax
import jax.numpy as jnp
from jax import lax
from jax.experimental import pallas as pl
from jax.experimental.pallas import tpu as pltpu
from jax.sharding import PartitionSpec as P

HD = 64
NORM_EPSILON = 1e-12
ALL = ("dp", "row", "col")
BF = jnp.bfloat16
F32 = jnp.float32
HIDDEN_SCORE = -1e30
SCALE = HD ** (-0.5)
EXP2_SCALE = SCALE * math.log2(math.e)


class Grid:
    def __init__(self, dp, row, outer, inner):
        self.shape = (dp, row, outer, inner)

    def pairs(self, target):
        n_d, n_r, n_o, n_i = self.shape

        def flat(d, r, o, i):
            return ((d * n_r + r) * n_o + o) * n_i + i

        result = []
        for d in range(n_d):
            for r in range(n_r):
                for o in range(n_o):
                    for i in range(n_i):
                        there = target(d, r, o, i)
                        if there is not None:
                            result.append((flat(d, r, o, i), flat(*there)))
        return result

    def shift(self, value, axis, by):
        size = self.shape[axis]

        def target(*at):
            at = list(at)
            at[axis] = (at[axis] + by) % size
            return tuple(at)

        return lax.ppermute(value, ALL, self.pairs(target))

    def flip(self, value, axis, bit):
        def target(*at):
            at = list(at)
            at[axis] = at[axis] ^ bit
            return tuple(at)

        return lax.ppermute(value, ALL, self.pairs(target))

    def total(self, value, axes):
        for axis in axes:
            size = self.shape[axis]
            bit = 1
            while bit < size:
                value = value + self.flip(value, axis, bit)
                bit *= 2
        return value


def dot(left, right):
    return jnp.dot(left, right, preferred_element_type=F32)


def dot_t(left, right):
    return lax.dot_general(left, right, (((1,), (1,)), ((), ())), preferred_element_type=F32)


def t_dot(left, right):
    return lax.dot_general(left, right, (((0,), (0,)), ((), ())), preferred_element_type=F32)


def after(value, *earlier):
    return lax.optimization_barrier((value, *earlier))[0]


def norm_forward(hidden, gain, shift):
    row_mean = jnp.mean(hidden, axis=1, keepdims=True)
    variance = jnp.mean(hidden * hidden, axis=1, keepdims=True) - row_mean * row_mean
    inverse = lax.rsqrt(variance + NORM_EPSILON)
    normed = (hidden - row_mean) * inverse
    return (normed * gain + shift, normed, inverse)


def norm_backward(grad_after, normed, inverse, gain):
    grad_normed = grad_after * gain
    mean_one = jnp.mean(grad_normed, axis=1, keepdims=True)
    mean_two = jnp.mean(grad_normed * normed, axis=1, keepdims=True)
    return inverse * (grad_normed - mean_one - normed * mean_two)


def head_groups(width):
    columns = min(128, width)
    return columns, columns // HD, width // columns


def attend_forward_kernel(width, block, qkv, ids_row, ids_col, *rest):
    out, logs = rest[-2:]
    length = qkv.shape[1]
    columns, per_group, groups = head_groups(width)
    lane = lax.broadcasted_iota(jnp.int32, (block, columns), 1) // HD
    log_lane = lax.broadcasted_iota(jnp.int32, (block, 128), 1)

    @pl.loop(0, length // block)
    def _(step):
        rows = pl.ds(pl.multiple_of(step * block, block), block)
        same = ids_col[0, rows, :] == ids_row[0]
        row_logs = jnp.zeros((block, 128), F32)
        for group in range(groups):
            first = 3 * group * columns
            queries = qkv[0, rows, first : first + columns]
            keys = qkv[0, :, first + columns : first + 2 * columns]
            values = qkv[0, :, first + 2 * columns : first + 3 * columns]
            result = None
            for head in range(per_group):
                masked = jnp.where(lane == head, queries, jnp.zeros_like(queries))
                scores = jnp.where(same, dot_t(masked, keys), HIDDEN_SCORE)
                top = jnp.max(scores, axis=1, keepdims=True)
                terms = jnp.exp2((scores - top) * EXP2_SCALE)
                total = jnp.sum(terms, axis=1, keepdims=True)
                part = dot(terms.astype(BF), values) / total
                result = part if result is None else jnp.where(lane == head, part, result)
                log = top * EXP2_SCALE + jnp.log(total) * math.log2(math.e)
                row_logs = jnp.where(log_lane == group * per_group + head, log, row_logs)
            out[0, rows, group * columns : (group + 1) * columns] = result.astype(BF)
        logs[0, :, rows] = row_logs.T[: logs.shape[1]]


def attend_backward_kernel(
    width, block, group, ranges, qkv, grads, attended, logs, ids_row, ids_col, *rest
):
    out, query_total, key_total, value_total = rest[-4:]
    length = qkv.shape[1]
    columns, per_group, groups = head_groups(width)
    blocks = length // block
    sequence = pl.program_id(0)
    lane = lax.broadcasted_iota(jnp.int32, (block, columns), 1) // HD
    pick = lax.broadcasted_iota(jnp.int32, (8, columns), 0)
    pick = (pick == lax.broadcasted_iota(jnp.int32, (8, columns), 1) // HD).astype(F32)
    def low(at):
        return ranges[sequence, 0, at]

    def high(at):
        return ranges[sequence, 1, at]

    first, outer_first = 3 * group * columns, group * columns
    for total in (query_total, key_total, value_total):
        total[...] = jnp.zeros_like(total)

    @pl.loop(0, blocks)
    def _(step):
        rows = pl.ds(pl.multiple_of(step * block, block), block)
        row_ids = ids_row[0, :, rows]
        queries = qkv[0, rows, first : first + columns]
        tops = grads[0, rows, outer_first : outer_first + columns]
        results = attended[0, rows, outer_first : outer_first + columns]
        inner = lax.dot_general(
            pick,
            tops.astype(F32) * results.astype(F32),
            (((1,), (1,)), ((), ())),
            precision=lax.Precision.HIGHEST,
            preferred_element_type=F32,
        )
        nothing = jnp.zeros_like(queries)
        head_queries = [jnp.where(lane == head, queries, nothing) for head in range(per_group)]
        head_grads = [jnp.where(lane == head, tops, nothing) for head in range(per_group)]
        head_logs = [
            logs[0, pl.ds(group * per_group + head, 1), rows] for head in range(per_group)
        ]

        @pl.loop(0, blocks)
        def _(key_step):
            @pl.when((low(step) <= high(key_step)) & (low(key_step) <= high(step)))
            def _():
                at = pl.ds(pl.multiple_of(key_step * block, block), block)
                keys = qkv[0, at, first + columns : first + 2 * columns]
                values = qkv[0, at, first + 2 * columns : first + 3 * columns]
                same = ids_col[0, at, :] == row_ids
                query_part, key_part, value_part = 0.0, 0.0, 0.0
                for head in range(per_group):
                    scores = dot_t(keys, head_queries[head]) * EXP2_SCALE - head_logs[head]
                    probs = jnp.exp2(jnp.where(same, scores, HIDDEN_SCORE))
                    prob_grads = dot_t(values, head_grads[head])
                    score_grads = (probs * (prob_grads - inner[head : head + 1])).astype(BF)
                    head_keys = jnp.where(lane == head, keys, jnp.zeros_like(keys))
                    value_part += dot(probs.astype(BF), head_grads[head])
                    key_part += dot(score_grads, head_queries[head])
                    query_part += t_dot(score_grads, head_keys)
                value_total[at, :] += value_part
                key_total[at, :] += key_part
                query_total[rows, :] += query_part

    out[0, :, :columns] = (query_total[...] * SCALE).astype(BF)
    out[0, :, columns : 2 * columns] = (key_total[...] * SCALE).astype(BF)
    out[0, :, 2 * columns :] = value_total[...].astype(BF)


def whole_block(shape):
    return pl.BlockSpec((1,) + shape[1:], lambda s, *_: (s, 0, 0))


SMALL_COST = pl.CostEstimate(flops=1024, bytes_accessed=1024, transcendentals=0)


def attend_forward(qkv, ids, earlier):
    count, length, columns = qkv.shape
    width = columns // 3
    ids_row, ids_col = ids[:, None, :], ids[:, :, None]
    log_rows = -(-width // HD // 8) * 8
    return pl.pallas_call(
        partial(attend_forward_kernel, width, min(256, length)),
        grid=(count,),
        in_specs=[whole_block(v.shape) for v in (qkv, ids_row, ids_col)]
        + [pl.BlockSpec(memory_space=pl.ANY)] * len(earlier),
        out_specs=[
            whole_block((count, length, width)),
            whole_block((count, log_rows, length)),
        ],
        out_shape=[
            jax.ShapeDtypeStruct((count, length, width), BF),
            jax.ShapeDtypeStruct((count, log_rows, length), F32),
        ],
        compiler_params=pltpu.CompilerParams(vmem_limit_bytes=48 * 1024 * 1024),
        cost_estimate=SMALL_COST,
    )(qkv, ids_row, ids_col, *earlier)


def attend_backward(qkv, grads, attended, logs, ids, group, others):
    count, length, columns = qkv.shape
    width = columns // 3
    wide = head_groups(width)[0]
    block = min(256, length)
    ids_row, ids_col = ids[:, None, :], ids[:, :, None]
    blocked = ids.reshape(count, length // block, block)
    ranges = jnp.stack([jnp.min(blocked, axis=2), jnp.max(blocked, axis=2)], axis=1)
    operands = (qkv, grads, attended, logs, ids_row, ids_col)
    kept = () if others is None else (others,)
    return pl.pallas_call(
        partial(attend_backward_kernel, width, block, group),
        grid_spec=pltpu.PrefetchScalarGridSpec(
            num_scalar_prefetch=1,
            grid=(count,),
            in_specs=[whole_block(v.shape) for v in operands]
            + [pl.BlockSpec(memory_space=pl.ANY)] * len(kept),
            out_specs=pl.BlockSpec((1, length, 3 * wide), lambda s, *_: (s, 0, group)),
            scratch_shapes=[pltpu.VMEM((length, wide), F32)] * 3,
        ),
        out_shape=jax.ShapeDtypeStruct(qkv.shape, BF),
        input_output_aliases={1 + len(operands): 0} if kept else {},
        compiler_params=pltpu.CompilerParams(vmem_limit_bytes=48 * 1024 * 1024),
        cost_estimate=SMALL_COST,
    )(ranges, *operands, *kept)


D_AX, R_AX, O_AX, I_AX = 0, 1, 2, 3


def gelu_pair(value):
    cdf = 0.5 * (1.0 + lax.erf(value * (0.5**0.5)))
    density = jnp.exp(-0.5 * value * value) * (1.0 / math.sqrt(2.0 * math.pi))
    return value * cdf, cdf + value * density


def on_device(
    sizes,
    tokens,
    segment_ids,
    in_weight,
    in_bias,
    out_weight,
    out_bias,
    gain_one,
    shift_one,
    up_weight,
    up_bias,
    down_weight,
    down_bias,
    gain_two,
    shift_two,
    cotangent,
):
    n_dp, n_row, n_col = sizes
    rows_here, model = tokens.shape
    n_outer, length = segment_ids.shape
    n_inner = length // rows_here
    assert n_dp == 2 and n_outer == 2 and n_outer * n_inner == n_col
    net = Grid(n_dp, n_row, n_outer, n_inner)
    d, r, c = (lax.axis_index(name) for name in ALL)
    o, i = c // n_inner, c % n_inner
    at_home = o == d
    width = in_weight.shape[1] // 3
    heads = width // HD
    wide, per_group, groups = head_groups(width)
    part = model // n_row
    units = up_weight.shape[1]
    half = units // 2

    def place(k):
        return lax.rem(r - k + n_row, n_row)

    def other(value):
        return net.shift(value, D_AX, 1)

    def across_outer(value):
        return net.shift(value, O_AX, 1)

    def in_order(mine, theirs, axis):
        first = jnp.where(d == 0, mine, theirs)
        second = jnp.where(d == 0, theirs, mine)
        return jnp.concatenate([first, second], axis=axis)

    def row_blocks(value):
        return [value] + [net.shift(value, R_AX, k) for k in range(1, n_row)]

    def place_rows(blocks, axis):
        shape = list(blocks[0].shape)
        step = shape[axis]
        shape[axis] = step * n_row
        result = jnp.zeros(shape, blocks[0].dtype)
        for k, block in enumerate(blocks):
            result = lax.dynamic_update_slice_in_dim(result, block, place(k) * step, axis)
        return result

    def scatter_row(value, axis):
        step = value.shape[axis] // n_row
        terms = [lax.dynamic_slice_in_dim(value, r * step, step, axis).astype(F32)]
        for k in range(1, n_row):
            block = lax.dynamic_slice_in_dim(value, place(k) * step, step, axis)
            terms.append(net.shift(block.astype(BF), R_AX, -k))
        return terms

    def add_up(terms):
        return sum(v.astype(F32) for v in terms)

    def gather_near(value):
        near = [value] + [net.shift(value, I_AX, k) for k in range(1, n_inner)]
        return near + [across_outer(value)]

    def gather_far(near, outer_share):
        near, away = near[:n_inner], near[n_inner]
        cut = int(away.shape[0] * outer_share)
        far = []
        for k in range(1, n_inner):
            pieces = [across_outer(near[k][:cut])]
            if cut < away.shape[0]:
                pieces.append(net.shift(away[cut:], I_AX, k))
            far.append(jnp.concatenate(pieces, axis=0))
        return near + [away] + far

    def scatter_far(blocks):
        return blocks[: n_inner + 1], [across_outer(v.astype(BF)) for v in blocks[n_inner + 1 :]]

    def scatter_near(parts, first=None, earlier=()):
        blocks, passed = parts
        if first is None:
            first = across_outer(blocks[n_inner].astype(BF))
        terms = [blocks[0], first]
        for k in range(1, n_inner):
            sent = (blocks[k].astype(F32) + passed[k - 1].astype(F32)).astype(BF)
            terms.append(net.shift(after(sent, *earlier), I_AX, -k))
        return terms

    def exchange_blocks(value, away):
        keep = jnp.where(at_home, value, away)
        return keep, other(jnp.where(at_home, away, value))

    def return_blocks(mine, theirs):
        received = other(theirs).astype(F32)
        keep = jnp.where(at_home, mine, received)
        away = jnp.where(at_home, received, mine)
        return keep, away.astype(BF)

    def join(value, axis):
        return in_order(value, other(value), axis)

    small = jnp.concatenate([in_bias, up_bias])
    small_near = gather_near(small)
    small_blocks = gather_far(small_near, 1.0)
    in_mine = in_weight.reshape(2, part // 2, groups, per_group, 3, HD)
    in_mine = lax.dynamic_index_in_dim(in_mine, d, 0, keepdims=False)
    in_mine = in_mine.transpose(0, 1, 3, 2, 4).reshape(part // 2, 3 * width)
    in_row = place_rows(row_blocks(in_mine), 0)
    token_parts = [tokens]
    for k in range(1, n_inner):
        token_parts.append(net.shift(after(tokens, *small_near), I_AX, k))
    in_row, small_blocks = lax.optimization_barrier((in_row, small_blocks))
    out_weight, up_weight = (after(v, in_row) for v in (out_weight, up_weight))
    in_away = across_outer(in_row)
    in_row, in_away, token_parts = lax.optimization_barrier((in_row, in_away, token_parts))
    in_halves = exchange_blocks(in_row, in_away)
    bias_rows = jnp.where(
        at_home, small_blocks[0][: 2 * width], small_blocks[n_inner][: 2 * width]
    ).reshape(groups, per_group, 2, HD)
    in_bias_row = jnp.stack(
        [bias_rows[:, :, 0], jnp.zeros_like(bias_rows[:, :, 0]), bias_rows[:, :, 1]], axis=1
    ).reshape(3 * width)
    up_bias_blocks = [
        lax.dynamic_slice_in_dim(v[2 * width :], d * half, half, 0) for v in small_blocks
    ]
    in_full = in_order(
        *(v.reshape(n_row, 1, part // 2, 3 * width) for v in in_halves), 1
    ).reshape(model, 3 * width)
    out_mine = lax.dynamic_slice_in_dim(out_weight, d * (width // 2), width // 2, 0)
    out_row = place_rows(row_blocks(out_mine), 1)
    out_away = across_outer(after(out_row, in_away))
    up_mine = lax.dynamic_slice_in_dim(up_weight, d * half, half, 1)
    up_row = row_blocks(up_mine)
    def spread(parts):
        return jnp.concatenate(parts, axis=0), jnp.concatenate([other(v) for v in parts], axis=0)

    def collect_here(product):
        arrived = [other(product(1, k).astype(BF)) for k in range(n_inner)]
        sums = [product(0, k) + arrived[k].astype(F32) for k in range(n_inner)]
        return sums[0], [v.astype(BF) for v in sums[1:]]

    def collect(own, sent):
        for k, value in enumerate(sent):
            own = own + net.shift(value, I_AX, -k - 1).astype(F32)
        return own

    def part_rows(k):
        return slice(k * rows_here, (k + 1) * rows_here)

    own_ids = lax.dynamic_index_in_dim(segment_ids, o, 0, keepdims=False)
    own_ids = jnp.concatenate(
        [
            lax.dynamic_slice_in_dim(
                own_ids, lax.rem(i - k + n_inner, n_inner) * rows_here, rows_here, 0
            )
            for k in range(n_inner)
        ]
    )
    ids = jnp.stack([own_ids, other(own_ids)])

    token_full = jnp.concatenate(spread(token_parts), axis=0)
    projected = (dot(token_full, in_full) + in_bias_row).astype(BF)
    projected = projected.reshape(2, length, 3 * width)
    down_mine = lax.dynamic_slice_in_dim(down_weight, d * half, half, 0)
    projected, up_row, out_away = lax.optimization_barrier((projected, up_row, out_away))
    out_full = in_order(*exchange_blocks(out_row, out_away), 0)
    up_row = place_rows(up_row, 0)
    up_near = gather_near(up_row)
    down_row = place_rows(row_blocks(after(down_mine, projected)), 1)
    attended, logs = attend_forward(projected, ids, (up_row,))
    attended, up_near, down_row = lax.optimization_barrier((attended, up_near, down_row))
    down_away = across_outer(down_row)
    branch = collect(*collect_here(lambda seq, k: dot(attended[seq, part_rows(k)], out_full)))
    token_late = after(token_full, attended)
    step = part // 2
    halves_of = [
        jnp.concatenate(
            [token_late[:, k * step : (k + 1) * step] for k in range(at, 2 * n_row, 2)], axis=1
        )
        for at in range(2)
    ]
    token_halves = (
        jnp.where(d == 0, halves_of[0], halves_of[1]),
        jnp.where(d == 0, halves_of[1], halves_of[0]),
    )
    branch, down_away, token_halves = lax.optimization_barrier((branch, down_away, token_halves))
    up_blocks = gather_far(up_near, 1.0)
    down_near = gather_near(after(down_row, branch))[:n_inner] + [down_away]
    down_blocks = gather_far(down_near, 0.5)

    def lay_out(blocks, axis):
        shape = list(blocks[0].shape)
        step = shape[axis]
        shape[axis] = step * len(blocks)
        result = jnp.zeros(shape, blocks[0].dtype)
        for k, block in enumerate(blocks):
            result = lax.dynamic_update_slice_in_dim(result, block, k * step, axis)
        return result

    up_full, down_full = lay_out(up_blocks, 1), lay_out(down_blocks, 0)
    up_bias_row = jnp.concatenate(up_bias_blocks)
    residual_one = tokens.astype(F32) + (branch + out_bias)
    normed_one, unit_one, inverse_one = norm_forward(residual_one, gain_one, shift_one)

    def both(value):
        return jnp.concatenate([value, other(value)], axis=0)

    def across(value, weights_of):
        away = other(weights_of(value[rows_here:]).astype(BF))
        return weights_of(value[:rows_here]) + away.astype(F32)

    mid = both(normed_one.astype(BF))
    hidden, slope = lax.optimization_barrier(
        [v.astype(BF) for v in gelu_pair(dot(mid, up_full) + up_bias_row)]
    )
    residual_two = normed_one + (across(hidden, lambda v: dot(v, down_full)) + down_bias)
    normed_two, unit_two, inverse_two = norm_forward(residual_two, gain_two, shift_two)
    output = normed_two.astype(BF)

    grad_top = cotangent.astype(F32)
    grad_gain_two = jnp.sum(grad_top * unit_two, axis=0)
    grad_shift_two = jnp.sum(grad_top, axis=0)
    grad_two = norm_backward(grad_top, unit_two, inverse_two, gain_two)
    grad_two_low = grad_two.astype(BF)
    grad_down_bias = jnp.sum(grad_two_low.astype(F32), axis=0)
    grad_two_both = both(grad_two_low)

    def unit_blocks(value):
        return [value[k * half : (k + 1) * half] for k in range(n_col)]

    grad_down = scatter_far(unit_blocks(t_dot(hidden, grad_two_both).astype(BF)))
    grad_pre = (dot_t(grad_two_both, down_full) * slope.astype(F32)).astype(BF)
    grad_one = grad_two + across(grad_pre, lambda v: dot_t(v, up_full))
    unit_sums = unit_blocks(jnp.sum(grad_pre.astype(F32), axis=0))
    grad_up_bias = jnp.zeros((2, n_outer, n_inner, half), F32)
    for k in range(n_col):
        there_o = lax.rem(o - k // n_inner + n_outer, n_outer)
        there_i = lax.rem(i - k % n_inner + n_inner, n_inner)
        grad_up_bias = lax.dynamic_update_slice(
            grad_up_bias,
            unit_sums[k][None, None, None],
            (d, there_o, there_i, 0),
        )

    grad_gain_one = jnp.sum(grad_one * unit_one, axis=0)
    grad_shift_one = jnp.sum(grad_one, axis=0)
    grad_first = norm_backward(grad_one, unit_one, inverse_one, gain_one)
    grad_first_low = grad_first.astype(BF)
    grad_out_bias = jnp.sum(grad_first_low.astype(F32), axis=0)

    flat = [
        grad_out_bias,
        grad_gain_one,
        grad_shift_one,
        grad_down_bias,
        grad_gain_two,
        grad_shift_two,
        grad_up_bias.reshape(-1),
    ]
    first_parts = [grad_first_low]
    first_parts += [net.shift(grad_first_low, I_AX, k) for k in range(1, n_inner)]
    down_first = across_outer(grad_down[0][n_inner].astype(BF))
    mid_late = after(mid, grad_first_low, down_first)
    grad_up = scatter_far(unit_blocks(t_dot(grad_pre, mid_late).astype(BF)))
    grad_first_both = spread(first_parts)
    grad_down = scatter_near(grad_down, down_first, first_parts)
    grad_attended = jnp.stack([dot_t(v, out_full).astype(BF) for v in grad_first_both])

    def halves(value, axis):
        step = value.shape[axis] // 2
        return [
            lax.dynamic_slice_in_dim(value, at * step, step, axis) for at in (d, 1 - d)
        ]

    out_mine, out_theirs = (
        [sum(t_dot(v, w) for v, w in zip(pair, grad_first_both)) for pair in
         zip(*(halves(v, 1) for v in attended))]
    )
    grad_out, out_away = return_blocks(out_mine, out_theirs.astype(BF))
    grad_out = [grad_out, across_outer(out_away)]
    projected_grads = None
    for g in range(groups):
        if g == groups - 1:
            grad_attended, grad_down, grad_up, grad_out, projected_grads = (
                lax.optimization_barrier(
                    (grad_attended, grad_down, grad_up, grad_out, projected_grads)
                )
            )
            grad_up = scatter_near(grad_up)
            grad_down = scatter_row(add_up(grad_down), 1)
            grad_out = scatter_row(add_up(grad_out), 1)
        projected_grads = attend_backward(
            projected, grad_attended, attended, logs, ids, g, projected_grads
        )
    projected_grads, grad_up, grad_down, grad_out = lax.optimization_barrier(
        (projected_grads, grad_up, grad_down, grad_out)
    )
    sent = collect_here(lambda seq, k: dot_t(projected_grads[seq, part_rows(k)], in_full))
    in_mine, in_theirs = (
        sum(t_dot(v[k * length : (k + 1) * length], projected_grads[k]) for k in range(2))
        for v in token_halves
    )
    grad_in, in_away = return_blocks(in_mine, in_theirs.astype(BF))
    sent, grad_in, in_away, grad_up, projected_grads = lax.optimization_barrier(
        (sent, grad_in, in_away, grad_up, projected_grads)
    )
    grad_tokens = grad_first + collect(*sent)
    flat = after(jnp.concatenate(flat).reshape(-1, 128), projected_grads)
    sums = net.total(flat, (R_AX, D_AX, O_AX, I_AX)).reshape(-1)
    grad_in = [grad_in, across_outer(in_away)]
    grad_up = scatter_row(add_up(grad_up), 1)
    bias_terms = jnp.sum(projected_grads.astype(F32), axis=(0, 1))
    bias_terms = bias_terms.reshape(groups, 3, per_group, HD)
    bias_terms = jnp.stack([bias_terms[:, 0], bias_terms[:, 2]], axis=2).reshape(1, 2 * width)
    bias_terms = bias_terms + across_outer(bias_terms)
    grad_up, grad_out, grad_tokens, grad_in, bias_terms, sums = lax.optimization_barrier(
        (grad_up, grad_out, grad_tokens, grad_in, bias_terms, sums)
    )
    grad_in = add_up(scatter_row(add_up(grad_in), 0))
    bias_terms = jnp.sum(place_rows(row_blocks(bias_terms), 0), axis=0)
    grad_in_bias = jnp.where(at_home, bias_terms, other(bias_terms))
    grad_down, grad_up, grad_out = (add_up(v) for v in (grad_down, grad_up, grad_out))

    sums = jnp.split(sums, [model * k for k in range(1, 7)])
    grad_up_bias = lax.dynamic_index_in_dim(
        sums[6].reshape(2, n_col, half), c, 1, keepdims=False
    ).reshape(2 * half)

    grad_down = join(grad_down, 0)
    grad_up = join(grad_up.T, 1)
    grad_out = join(grad_out, 0)
    grad_in = join(grad_in, 0)
    grad_in = grad_in.reshape(part, groups, 3, per_group, HD).transpose(0, 1, 3, 2, 4)
    grad_in = grad_in.reshape(part, 3 * width)
    return (
        output,
        grad_tokens,
        grad_in,
        grad_in_bias,
        grad_out,
        sums[0],
        sums[1],
        sums[2],
        grad_up,
        grad_up_bias,
        grad_down,
        sums[3],
        sums[4],
        sums[5],
    )


def solution(mesh):
    return jax.shard_map(
        partial(on_device, tuple(mesh.shape[name] for name in ALL)),
        mesh=mesh,
        in_specs=(
            P(("dp", "row", "col"), None),
            P(("dp", "row"), None),
            P("row", "col"),
            P("col"),
            P("col", "row"),
            P(),
            P(),
            P(),
            P("row", "col"),
            P("col"),
            P("col", "row"),
            P(),
            P(),
            P(),
            P(("dp", "row", "col"), None),
        ),
        out_specs=(
            P(("dp", "row", "col"), None),
            P(("dp", "row", "col"), None),
            P("row", "col"),
            P("col"),
            P("col", "row"),
            P(),
            P(),
            P(),
            P("row", "col"),
            P("col"),
            P("col", "row"),
            P(),
            P(),
            P(),
        ),
        check_vma=False,
    )
```

time: 455 us -> 413 us (0.908)
  matrix products: 91.1 us -> 69.2 us
  waiting for transfers between devices: 148 us -> 131 us
  local copies, waits for them, and re-layouts: 19.6 us -> 31 us
  Pallas kernels: 66.9 us -> 58.5 us
  other arithmetic: 40.5 us -> 33.5 us
    ppermute x71 -> x74, waiting for transfers between devices: 141 us -> 123 us  [shift(): return lax.ppermute(value, ALL, self.pairs(target))]
    dot_general x16 -> x10, matrix products: 28.6 us -> 19.2 us  [t_dot(): lax.dot_general(left, right, (((0,), (0,)), ((), ())), preferred_element_...]
    pallas_call x2, Pallas kernels: 47.9 us -> 39.1 us  [attend_backward(): pl.pallas_call(partial(attend_backward_kernel, width, block, group), grid...]
    dot_general x18 -> x9, matrix products: 35.8 us -> 28 us  [dot_t(): lax.dot_general(left, right, (((1,), (1,)), ((), ())), preferred_element_...]
    dynamic_update_slice x21 -> x31, local copies, waits for them, and re-layouts: 1.46 us -> 8.33 us  [the longest x7 4.12 us: lay_out(): result = lax.dynamic_update_slice_in_dim(result, block, k * step, axis)]
    reduce_sum x7 -> x2, other arithmetic: 7.37 us -> 0.53 us  [the longest x1 0.51 us: on_device(): bias_terms = jnp.sum(projected_grads.astype(F32), axis=(0, 1))]
    dot_general x17 -> x8, matrix products: 26.7 us -> 22.1 us  [dot(): return jnp.dot(left, right, preferred_element_type=F32)]
    ppermute x71 -> x74, starting transfers between devices: 71.8 us -> 76.4 us  [shift(): return lax.ppermute(value, ALL, self.pairs(target))]
  transfers between devices with their start and end apart: 76 -> 79, of which waited for: 28 -> 29; matrix products, arithmetic and copies ran while one was open for 27% -> 25% of each run, Pallas kernels for 10% -> 14%
where the time goes in v3:
time: 413 us; the launch traced here: 406 us
  waiting for transfers between devices  131 us (32%)
  starting transfers between devices  80.3 us (19%)
  matrix products  69.2 us (17%)
  Pallas kernels  58.5 us (14%)
  other arithmetic  33.5 us (8%)
  local copies, waits for them, and re-layouts  31 us (8%)
    ppermute x74, waiting for transfers between devices, shift(): return lax.ppermute(value, ALL, self.pairs(target))  123 us
    ppermute x74, starting transfers between devices, shift(): return lax.ppermute(value, ALL, self.pairs(target))  76.4 us
    pallas_call x2, Pallas kernels, attend_backward(): pl.pallas_call(partial(attend_backward_kernel, width, block, group), grid...  39.1 us
    dot_general x9, matrix products, dot_t(): lax.dot_general(left, right, (((1,), (1,)), ((), ())), preferred_element_...  28 us
    dot_general x8, matrix products, dot(): return jnp.dot(left, right, preferred_element_type=F32)  22.1 us
    pallas_call x1, Pallas kernels, attend_forward(): pl.pallas_call(partial(attend_forward_kernel, width, min(256, length)), g...  19.4 us
    dot_general x10, matrix products, t_dot(): lax.dot_general(left, right, (((0,), (0,)), ((), ())), preferred_element_...  19.2 us
    unnamed x146, local copies, waits for them, and re-layouts  8.37 us
  transfers between devices with their start and end apart: 79, of which 29 were waited for; matrix products, arithmetic and copies ran while one was open for 25% of the time, Pallas kernels for 14%

profile of v3, /device:TPU:11, one launch (start us, length us, event | category | flops | bytes accessed | tf_op | source)
XLA Modules:
  0.0 406.4 jit_solution(16918615272199627734)
XLA Ops:
  12.2 8.1 %collective-permute-done.1 = bf16[128,768]{1,0:T(8,128)(2,1)S(1)} collective-permute-done((bf16[128,768]{1,0:T(8,128)(2,1)S(1)}, bf16[128,768]{1,0:T(8,128)(2,1)S(1)}, u32[]{:S(2)}, u32[]{:S(2)}) %collective-permute-start.1) | collective-permute-done | bytes 196640 | tf_op jit(solution)/shard_map/ppermute | solution.py:49
  20.3 2.9 collective-permute-done.2
  29.8 12.2 %collective-permute-done.6 = bf16[512,768]{1,0:T(8,128)(2,1)S(1)} collective-permute-done((bf16[512,768]{1,0:T(8,128)(2,1)S(1)}, bf16[512,768]{1,0:T(8,128)(2,1)S(1)}, u32[]{:S(2)}, u32[]{:S(2)}) %collective-permute-start.6) | collective-permute-done | bytes 786464 | tf_op jit(solution)/shard_map/ppermute | solution.py:49
  55.7 4.8 %add_convert_fusion = bf16[2048,768]{1,0:T(8,128)(2,1)} fusion(bf16[2048,1024]{1,0:T(8,128)(2,1)S(1)} %constant_dynamic-update-slice_fusion.1, bf16[1024,768]{1,0:T(8,128)(2,1)S(1)} %bitcast.142, f32[768]{0:T(1024)S(1)} %copy-done.51), kind=kOutput, calls=%fused_computation.11 | convolution fusion | flops 3224371200 | bytes 8915968 | tf_op jit(solution)/shard_map/dot_general | solution.py:70
  60.5 10.4 %collective-permute-done.12 = bf16[256,512]{1,0:T(8,128)(2,1)S(1)} collective-permute-done((bf16[256,512]{1,0:T(8,128)(2,1)S(1)}, bf16[256,512]{1,0:T(8,128)(2,1)S(1)}, u32[]{:S(2)}, u32[]{:S(2)}) %collective-permute-start.12) | collective-permute-done | bytes 262176 | tf_op jit(solution)/shard_map/ppermute | solution.py:49
  70.9 3.1 collective-permute-done.13
  79.0 19.4 %shard_map.254 = (bf16[2,1024,256]{2,1,0:T(8,128)(2,1)S(1)}, f32[2,8,1024]{2,1,0:T(8,128)S(1)}) custom-call(bf16[2,1024,768]{2,1,0:T(8,128)(2,1)} %bitcast.135, s32[2,1,1024]{2,1,0:T(1,128)S(1)} %broadcast_in_dim.26.ids_row, s32[2,1024,1]{2,1,0:T(8,128)S(1)} %copy.89.ids_col, bf16[1024,512]{1,0:T(8,128)(2,1)S(1)} %constant_dynamic-update-slice_fusion.19.rest_0_), custom_call_target="tpu_custom_call" | custom-call | flops 1024 | bytes 1024 | tf_op jit(solution)/shard_map/pallas_call | solution.py:218
  108.1 2.8 broadcast_select_fusion
  111.0 18.6 %collective-permute-done.27 = bf16[512,1024]{1,0:T(8,128)(2,1)S(1)} collective-permute-done((bf16[512,1024]{1,0:T(8,128)(2,1)S(1)}, bf16[512,1024]{1,0:T(8,128)(2,1)S(1)}, u32[]{:S(2)}, u32[]{:S(2)}) %collective-permute-start.27) | collective-permute-done | bytes 1048608 | tf_op jit(solution)/shard_map/ppermute | solution.py:49
  138.2 12.1 %collective-permute-done.30 = bf16[1024,512]{1,0:T(8,128)(2,1)S(1)} collective-permute-done((bf16[1024,512]{1,0:T(8,128)(2,1)}, bf16[1024,512]{1,0:T(8,128)(2,1)S(1)}, u32[]{:S(2)}, u32[]{:S(2)}) %collective-permute-start.30) | collective-permute-done | bytes 1048608 | tf_op jit(solution)/shard_map/ppermute | solution.py:49
  153.7 10.3 %fusion.4 = (bf16[1024,2048]{1,0:T(8,128)(2,1)}, bf16[1024,2048]{1,0:T(8,128)(2,1)S(1)}) fusion(f32[2048]{0:T(1024)S(1)} %pad_maximum_fusion.17, bf16[1024,2048]{1,0:T(8,128)(2,1)S(1)} %constant_dynamic-update-slice_fusion.12, bf16[512,1024]{1,0:T(8,128)(2,1)S(1)} %collective-permute-done.29, bf16[512,1024]{1,0:T(8,128)(2,1)S(1)} %fusion.20), kind=kOutput, calls=%fused_computation.5 | convolution fusion | flops 4324327424 | bytes 14688256 | tf_op jit(solution)/shard_map/dot_general | solution.py:70
  167.6 3.5 collective-permute-start.34
  173.3 2.9 fusion.102
  181.2 3.4 pad_maximum_fusion.2
  184.6 7.3 %convert_reduce_fusion = (f32[2048]{0:T(1024)S(1)}, bf16[1024,2048]{1,0:T(8,128)(2,1)S(1)}) fusion(bf16[1024,2048]{1,0:T(8,128)(2,1)} %get-tuple-element.127, bf16[2048,1024]{1,0:T(8,128)(2,1)S(1)} %copy-done.15, bf16[512,1024]{1,0:T(8,128)(2,1)} %collective-permute-done.35, bf16[512,1024]{1,0:T(8,128)(2,1)} %get-tuple-element.249), kind=kOutput, calls=%fused_computation.6 | convolution fusion | flops 4309645312 | bytes 14688256 | tf_op jit(solution)/shard_map/dot_general | solution.py:74
  192.0 3.4 fusion.40
  196.1 6.8 %convolution_convert_fusion.1 = bf16[2048,1024]{1,0:T(8,128)(2,1)S(1)} fusion(bf16[1024,2048]{1,0:T(8,128)(2,1)S(1)} %copy-done.64, bf16[512,1024]{1,0:T(8,128)(2,1)} %collective-permute-done.35, bf16[512,1024]{1,0:T(8,128)(2,1)} %get-tuple-element.249), kind=kOutput, calls=%fused_computation.13 | convolution fusion | flops 4301258752 | bytes 10485760 | tf_op jit(solution)/shard_map/dot_general | solution.py:78
  207.6 8.2 %multiply_reduce_fusion = (f32[1024]{0:T(1024)S(1)}, f32[512]{0:T(512)S(1)}, f32[512]{0:T(512)S(1)}, f32[1024]{0:T(1024)S(1)}, f32[512,1024]{1,0:T(8,128)S(1)}) fusion(f32[512,1024]{1,0:T(8,128)} %copy-done.3, f32[512]{0:T(512)S(1)} %get-tuple-element.323, f32[512]{0:T(512)S(1)} %get-tuple-element.322, f32[1024]{0:T(1024)S(1)} %copy-done.42, ...), kind=kOutput, calls=%fused_computation.34 | convolution fusion | flops 2157966336 | bytes 14712832 | tf_op jit(solution)/shard_map/dot_general | solution.py:74
  219.8 11.1 %collective-permute-done.40 = bf16[512,1024]{1,0:T(8,128)(2,1)} collective-permute-done((bf16[512,1024]{1,0:T(8,128)(2,1)}, bf16[512,1024]{1,0:T(8,128)(2,1)}, u32[]{:S(2)}, u32[]{:S(2)}) %collective-permute-start.40) | collective-permute-done | bytes 1048608 | tf_op jit(solution)/shard_map/ppermute | solution.py:49
  230.9 5.1 %convolution_convert_fusion = bf16[2048,1024]{1,0:T(8,128)(2,1)S(1)} fusion(bf16[1024,2048]{1,0:T(8,128)(2,1)S(1)} %copy-done.62, bf16[1024,1024]{1,0:T(8,128)(2,1)S(1)} %copy-done.23), kind=kOutput, calls=%fused_computation.12 | convolution fusion | flops 4297064448 | bytes 10485760 | tf_op jit(solution)/shard_map/dot_general | solution.py:78
  238.5 4.9 %collective-permute-done.37 = bf16[512,1024]{1,0:T(8,128)(2,1)S(1)} collective-permute-done((bf16[512,1024]{1,0:T(8,128)(2,1)S(1)}, bf16[512,1024]{1,0:T(8,128)(2,1)S(1)}, u32[]{:S(2)}, u32[]{:S(2)}) %collective-permute-start.37) | collective-permute-done | bytes 1048608 | tf_op jit(solution)/shard_map/ppermute | solution.py:49
  244.2 9.1 %collective-permute-done.41 = bf16[512,1024]{1,0:T(8,128)(2,1)} collective-permute-done((bf16[512,1024]{1,0:T(8,128)(2,1)}, bf16[512,1024]{1,0:T(8,128)(2,1)}, u32[]{:S(2)}, u32[]{:S(2)}) %collective-permute-start.41) | collective-permute-done | bytes 1048608 | tf_op jit(solution)/shard_map/ppermute | solution.py:49
  264.0 19.5 %shard_map.255.rest_0_ = bf16[2,1024,768]{2,1,0:T(8,128)(2,1)} custom-call(s32[2,2,4]{2,1,0:T(2,128)S(1)} %pad_add_fusion.2.ranges, bf16[2,1024,768]{2,1,0:T(8,128)(2,1)} %bitcast.136, bf16[2,1024,256]{2,1,0:T(8,128)(2,1)S(1)} %pad_maximum_fusion.8.grads, bf16[2,1024,256]{2,1,0:T(8,128)(2,1)S(1)} %get-tuple-element.114.attended, ...), custom_call_target="tpu_custom_call" | custom-call | flops 1024 | bytes 1024 | tf_op jit(solution)/shard_map/pallas_call | solution.py:246
  292.4 2.7 collective-permute-start.50
  295.1 19.6 %shard_map.256 = bf16[2,1024,768]{2,1,0:T(8,128)(2,1)} custom-call(s32[2,2,4]{2,1,0:T(2,128)S(1)} %pad_add_fusion.2.ranges, bf16[2,1024,768]{2,1,0:T(8,128)(2,1)} %bitcast.137, bf16[2,1024,256]{2,1,0:T(8,128)(2,1)S(1)} %pad_maximum_fusion.8.grads, bf16[2,1024,256]{2,1,0:T(8,128)(2,1)S(1)} %get-tuple-element.114.attended, ...), custom_call_target="tpu_custom_call", output_to_operand_aliasing={{}: (7, {})} | custom-call | flops 1024 | bytes 1024 | tf_op jit(solution)/shard_map/pallas_call | solution.py:246
  339.3 3.0 collective-permute-done.64
  359.5 3.6 add_add_fusion
  363.1 8.5 %collective-permute-done.58 = bf16[512,256]{1,0:T(8,128)(2,1)S(1)} collective-permute-done((bf16[512,256]{1,0:T(8,128)(2,1)}, bf16[512,256]{1,0:T(8,128)(2,1)S(1)}, u32[]{:S(2)}, u32[]{:S(2)}) %collective-permute-start.58) | collective-permute-done | bytes 262176 | tf_op jit(solution)/shard_map/ppermute | solution.py:49
  371.6 5.5 %collective-permute-done.59 = bf16[512,256]{1,0:T(8,128)(2,1)S(1)} collective-permute-done((bf16[512,256]{1,0:T(8,128)(2,1)S(1)}, bf16[512,256]{1,0:T(8,128)(2,1)S(1)}, u32[]{:S(2)}, u32[]{:S(2)}) %collective-permute-start.59) | collective-permute-done | bytes 262176 | tf_op jit(solution)/shard_map/ppermute | solution.py:49
  381.9 3.3 collective-permute-start.69
  392.6 5.5 %collective-permute-done.69 = bf16[128,768]{1,0:T(8,128)(2,1)S(1)} collective-permute-done((bf16[128,768]{1,0:T(8,128)(2,1)S(1)}, bf16[128,768]{1,0:T(8,128)(2,1)S(1)}, u32[]{:S(2)}, u32[]{:S(2)}) %collective-permute-start.69) | collective-permute-done | bytes 196640 | tf_op jit(solution)/shard_map/ppermute | solution.py:49
  398.1 3.5 collective-permute-done.68
  (451 shorter events, 158.9 us)
Async XLA Ops:
  5.1 18.0 %collective-permute-start.2 = (bf16[128,768]{1,0:T(8,128)(2,1)S(1)}, bf16[128,768]{1,0:T(8,128)(2,1)S(1)}, u32[]{:S(2)}, u32[]{:S(2)}) collective-permute-start(bf16[128,768]{1,0:T(8,128)(2,1)S(1)} %copy.81), channel_id=1, source_target_pairs={{0,12},{1,13},{2,14},{3,15},{4,0},{5,1},{6,2},{7,3},{8,4},{9,5},{1... | collective-permute-start | bytes 589832 | tf_op jit(solution)/shard_map/ppermute | solution.py:49
  9.7 32.3 %collective-permute-start.7 = (bf16[512,1024]{1,0:T(8,128)(2,1)S(1)}, bf16[512,1024]{1,0:T(8,128)(2,1)}, u32[]{:S(2)}, u32[]{:S(2)}) collective-permute-start(bf16[512,1024]{1,0:T(8,128)(2,1)S(1)} %copy-done.12), channel_id=1, source_target_pairs={{0,1},{1,0},{2,3},{3,2},{4,5},{5,4},{6,7},{7,6},{8,9},{9,8},{10,11... | collective-permute-start | bytes 3145736 | tf_op jit(solution)/shard_map/ppermute | solution.py:49
  23.2 18.8 %collective-permute-start.6 = (bf16[512,768]{1,0:T(8,128)(2,1)S(1)}, bf16[512,768]{1,0:T(8,128)(2,1)S(1)}, u32[]{:S(2)}, u32[]{:S(2)}) collective-permute-start(bf16[512,768]{1,0:T(8,128)(2,1)S(1)} %constant_dynamic-update-slice_fusion.27), channel_id=1, source_target_pairs={{0,2},{1,3},{2,0},{3,1},{4,6},{5,7},{6,4},{7,5},{8,10},{9,11},{10,... | collective-permute-start | bytes 2359304 | tf_op jit(solution)/shard_map/ppermute | solution.py:49
  24.5 51.2 %collective-permute-start.18 = (s32[1024]{0:T(1024)S(1)}, s32[1024]{0:T(1024)S(1)}, u32[]{:S(2)}, u32[]{:S(2)}) collective-permute-start(s32[1024]{0:T(1024)S(1)} %pad_add_fusion.1), channel_id=1, source_target_pairs={{0,16},{1,17},{2,18},{3,19},{4,20},{5,21},{6,22},{7,23},{8,24},{9,... | collective-permute-start | bytes 12296 | tf_op jit(solution)/shard_map/ppermute | solution.py:49
  27.5 18.4 %collective-permute-start.15 = (bf16[128,256]{1,0:T(8,128)(2,1)S(1)}, bf16[128,256]{1,0:T(8,128)(2,1)S(1)}, u32[]{:S(2)}, u32[]{:S(2)}) collective-permute-start(bf16[128,256]{1,0:T(8,128)(2,1)S(1)} %get-tuple-element.255), channel_id=1, source_target_pairs={{0,8},{1,9},{2,10},{3,11},{4,12},{5,13},{6,14},{7,15},{8,0},{9,1},... | collective-permute-start | bytes 196616 | tf_op jit(solution)/shard_map/ppermute | solution.py:49
  50.6 20.3 %collective-permute-start.12 = (bf16[256,512]{1,0:T(8,128)(2,1)S(1)}, bf16[256,512]{1,0:T(8,128)(2,1)S(1)}, u32[]{:S(2)}, u32[]{:S(2)}) collective-permute-start(bf16[256,512]{1,0:T(8,128)(2,1)S(1)} %constant_dynamic-slice_fusion.6), channel_id=1, source_target_pairs={{0,8},{1,9},{2,10},{3,11},{4,12},{5,13},{6,14},{7,15},{8,0},{9,1},... | collective-permute-start | bytes 786440 | tf_op jit(solution)/shard_map/ppermute | solution.py:49
  54.1 19.8 %collective-permute-start.13 = (bf16[256,512]{1,0:T(8,128)(2,1)S(1)}, bf16[256,512]{1,0:T(8,128)(2,1)S(1)}, u32[]{:S(2)}, u32[]{:S(2)}) collective-permute-start(bf16[256,512]{1,0:T(8,128)(2,1)S(1)} %constant_dynamic-slice_fusion.6), channel_id=1, source_target_pairs={{0,12},{1,13},{2,14},{3,15},{4,0},{5,1},{6,2},{7,3},{8,4},{9,5},{1... | collective-permute-start | bytes 786440 | tf_op jit(solution)/shard_map/ppermute | solution.py:49
  54.3 19.7 %collective-permute-start.17 = (bf16[128,1024]{1,0:T(8,128)(2,1)S(1)}, bf16[128,1024]{1,0:T(8,128)(2,1)S(1)}, u32[]{:S(2)}, u32[]{:S(2)}) collective-permute-start(bf16[128,1024]{1,0:T(8,128)(2,1)S(1)} %constant_dynamic-update-slice_fusion.23), channel_id=1, source_target_pairs={{0,2},{1,3},{2,0},{3,1},{4,6},{5,7},{6,4},{7,5},{8,10},{9,11},{10,... | collective-permute-start | bytes 786440 | tf_op jit(solution)/shard_map/ppermute | solution.py:49
  74.2 27.8 %collective-permute-start.19 = (bf16[1024,512]{1,0:T(8,128)(2,1)S(1)}, bf16[1024,512]{1,0:T(8,128)(2,1)}, u32[]{:S(2)}, u32[]{:S(2)}) collective-permute-start(bf16[1024,512]{1,0:T(8,128)(2,1)S(1)} %constant_dynamic-update-slice_fusion.19.rest_0_), channel_id=1, source_target_pairs={{0,1},{1,0},{2,3},{3,2},{4,5},{5,4},{6,7},{7,6},{8,9},{9,8},{10,11... | collective-permute-start | bytes 3145736 | tf_op jit(solution)/shard_map/ppermute | solution.py:49
  74.5 27.5 %collective-permute-start.20 = (bf16[1024,512]{1,0:T(8,128)(2,1)S(1)}, bf16[1024,512]{1,0:T(8,128)(2,1)}, u32[]{:S(2)}, u32[]{:S(2)}) collective-permute-start(bf16[1024,512]{1,0:T(8,128)(2,1)S(1)} %constant_dynamic-update-slice_fusion.19.rest_0_), channel_id=1, source_target_pairs={{0,2},{1,3},{2,0},{3,1},{4,6},{5,7},{6,4},{7,5},{8,10},{9,11},{10,... | collective-permute-start | bytes 3145736 | tf_op jit(solution)/shard_map/ppermute | solution.py:49
  76.1 22.3 %collective-permute-start.21 = (bf16[512,256]{1,0:T(8,128)(2,1)}, bf16[512,256]{1,0:T(8,128)(2,1)S(1)}, u32[]{:S(2)}, u32[]{:S(2)}) collective-permute-start(bf16[512,256]{1,0:T(8,128)(2,1)} %constant_dynamic-slice_fusion.4), channel_id=1, source_target_pairs={{0,4},{1,5},{2,6},{3,7},{4,8},{5,9},{6,10},{7,11},{8,12},{9,13},{1... | collective-permute-start | bytes 786440 | tf_op jit(solution)/shard_map/ppermute | solution.py:49
  76.2 24.5 %collective-permute-start.22 = (bf16[512,256]{1,0:T(8,128)(2,1)}, bf16[512,256]{1,0:T(8,128)(2,1)S(1)}, u32[]{:S(2)}, u32[]{:S(2)}) collective-permute-start(bf16[512,256]{1,0:T(8,128)(2,1)} %constant_dynamic-slice_fusion.4), channel_id=1, source_target_pairs={{0,8},{1,9},{2,10},{3,11},{4,12},{5,13},{6,14},{7,15},{8,0},{9,1},... | collective-permute-start | bytes 786440 | tf_op jit(solution)/shard_map/ppermute | solution.py:49
  76.3 24.5 %collective-permute-start.23 = (bf16[512,256]{1,0:T(8,128)(2,1)}, bf16[512,256]{1,0:T(8,128)(2,1)S(1)}, u32[]{:S(2)}, u32[]{:S(2)}) collective-permute-start(bf16[512,256]{1,0:T(8,128)(2,1)} %constant_dynamic-slice_fusion.4), channel_id=1, source_target_pairs={{0,12},{1,13},{2,14},{3,15},{4,0},{5,1},{6,2},{7,3},{8,4},{9,5},{1... | collective-permute-start | bytes 786440 | tf_op jit(solution)/shard_map/ppermute | solution.py:49
  103.5 26.7 %collective-permute-start.28 = (bf16[512,1024]{1,0:T(8,128)(2,1)S(1)}, bf16[512,1024]{1,0:T(8,128)(2,1)S(1)}, u32[]{:S(2)}, u32[]{:S(2)}) collective-permute-start(bf16[512,1024]{1,0:T(8,128)(2,1)S(1)} %constant_dynamic-update-slice_fusion.15), channel_id=1, source_target_pairs={{0,2},{1,3},{2,0},{3,1},{4,6},{5,7},{6,4},{7,5},{8,10},{9,11},{10,... | collective-permute-start | bytes 3145736 | tf_op jit(solution)/shard_map/ppermute | solution.py:49
  103.7 46.6 %collective-permute-start.30 = (bf16[1024,512]{1,0:T(8,128)(2,1)}, bf16[1024,512]{1,0:T(8,128)(2,1)S(1)}, u32[]{:S(2)}, u32[]{:S(2)}) collective-permute-start(bf16[1024,512]{1,0:T(8,128)(2,1)} %collective-permute-done.19), channel_id=1, source_target_pairs={{0,2},{1,3},{2,0},{3,1},{4,6},{5,7},{6,4},{7,5},{8,10},{9,11},{10,... | collective-permute-start | bytes 3145736 | tf_op jit(solution)/shard_map/ppermute | solution.py:49
  105.6 23.9 %collective-permute-start.27 = (bf16[512,1024]{1,0:T(8,128)(2,1)S(1)}, bf16[512,1024]{1,0:T(8,128)(2,1)S(1)}, u32[]{:S(2)}, u32[]{:S(2)}) collective-permute-start(bf16[512,1024]{1,0:T(8,128)(2,1)S(1)} %add_convert_fusion.5), channel_id=1, source_target_pairs={{0,1},{1,0},{2,3},{3,2},{4,5},{5,4},{6,7},{7,6},{8,9},{9,8},{10,11... | collective-permute-start | bytes 3145736 | tf_op jit(solution)/shard_map/ppermute | solution.py:49
  130.2 23.0 %collective-permute-start.31 = (bf16[512,1024]{1,0:T(8,128)(2,1)S(1)}, bf16[512,1024]{1,0:T(8,128)(2,1)S(1)}, u32[]{:S(2)}, u32[]{:S(2)}) collective-permute-start(bf16[512,1024]{1,0:T(8,128)(2,1)S(1)} %constant_dynamic-update-slice_fusion.15), channel_id=1, source_target_pairs={{0,1},{1,0},{2,3},{3,2},{4,5},{5,4},{6,7},{7,6},{8,9},{9,8},{10,11... | collective-permute-start | bytes 3145736 | tf_op jit(solution)/shard_map/ppermute | solution.py:49
  132.5 21.2 %collective-permute-start.29 = (bf16[512,1024]{1,0:T(8,128)(2,1)S(1)}, bf16[512,1024]{1,0:T(8,128)(2,1)S(1)}, u32[]{:S(2)}, u32[]{:S(2)}) collective-permute-start(bf16[512,1024]{1,0:T(8,128)(2,1)S(1)} %fusion.20), channel_id=1, source_target_pairs={{0,16},{1,17},{2,18},{3,19},{4,20},{5,21},{6,22},{7,23},{8,24},{9,... | collective-permute-start | bytes 3145736 | tf_op jit(solution)/shard_map/ppermute | solution.py:49
  205.9 24.9 %collective-permute-start.40 = (bf16[512,1024]{1,0:T(8,128)(2,1)}, bf16[512,1024]{1,0:T(8,128)(2,1)}, u32[]{:S(2)}, u32[]{:S(2)}) collective-permute-start(bf16[512,1024]{1,0:T(8,128)(2,1)} %get-tuple-element.263), channel_id=1, source_target_pairs={{0,2},{1,3},{2,0},{3,1},{4,6},{5,7},{6,4},{7,5},{8,10},{9,11},{10,... | collective-permute-start | bytes 3145736 | tf_op jit(solution)/shard_map/ppermute | solution.py:49
  207.1 46.2 %collective-permute-start.41 = (bf16[512,1024]{1,0:T(8,128)(2,1)}, bf16[512,1024]{1,0:T(8,128)(2,1)}, u32[]{:S(2)}, u32[]{:S(2)}) collective-permute-start(bf16[512,1024]{1,0:T(8,128)(2,1)} %get-tuple-element.262), channel_id=1, source_target_pairs={{0,2},{1,3},{2,0},{3,1},{4,6},{5,7},{6,4},{7,5},{8,10},{9,11},{10,... | collective-permute-start | bytes 3145736 | tf_op jit(solution)/shard_map/ppermute | solution.py:49
  217.9 39.1 %collective-permute-start.38 = (bf16[512,1024]{1,0:T(8,128)(2,1)S(1)}, bf16[512,1024]{1,0:T(8,128)(2,1)S(1)}, u32[]{:S(2)}, u32[]{:S(2)}) collective-permute-start(bf16[512,1024]{1,0:T(8,128)(2,1)S(1)} %get-tuple-element.251), channel_id=1, source_target_pairs={{0,16},{1,17},{2,18},{3,19},{4,20},{5,21},{6,22},{7,23},{8,24},{9,... | collective-permute-start | bytes 3145736 | tf_op jit(solution)/shard_map/ppermute | solution.py:49
  218.6 24.9 %collective-permute-start.37 = (bf16[512,1024]{1,0:T(8,128)(2,1)S(1)}, bf16[512,1024]{1,0:T(8,128)(2,1)S(1)}, u32[]{:S(2)}, u32[]{:S(2)}) collective-permute-start(bf16[512,1024]{1,0:T(8,128)(2,1)S(1)} %get-tuple-element.251), channel_id=1, source_target_pairs={{0,1},{1,0},{2,3},{3,2},{4,5},{5,4},{6,7},{7,6},{8,9},{9,8},{10,11... | collective-permute-start | bytes 3145736 | tf_op jit(solution)/shard_map/ppermute | solution.py:49
  237.4 46.2 %collective-permute-start.43 = (bf16[512,1024]{1,0:T(8,128)(2,1)S(1)}, bf16[512,1024]{1,0:T(8,128)(2,1)S(1)}, u32[]{:S(2)}, u32[]{:S(2)}) collective-permute-start(bf16[512,1024]{1,0:T(8,128)(2,1)S(1)} %get-tuple-element.258), channel_id=1, source_target_pairs={{0,2},{1,3},{2,0},{3,1},{4,6},{5,7},{6,4},{7,5},{8,10},{9,11},{10,... | collective-permute-start | bytes 3145736 | tf_op jit(solution)/shard_map/ppermute | solution.py:49
  255.3 28.3 %collective-permute-start.42 = (bf16[512,1024]{1,0:T(8,128)(2,1)S(1)}, bf16[512,1024]{1,0:T(8,128)(2,1)S(1)}, u32[]{:S(2)}, u32[]{:S(2)}) collective-permute-start(bf16[512,1024]{1,0:T(8,128)(2,1)S(1)} %add_convert_fusion.3), channel_id=1, source_target_pairs={{0,1},{1,0},{2,3},{3,2},{4,5},{5,4},{6,7},{7,6},{8,9},{9,8},{10,11... | collective-permute-start | bytes 3145736 | tf_op jit(solution)/shard_map/ppermute | solution.py:49
  261.9 21.6 %collective-permute-start.45 = (bf16[128,1024]{1,0:T(8,128)(2,1)S(1)}, bf16[128,1024]{1,0:T(8,128)(2,1)S(1)}, u32[]{:S(2)}, u32[]{:S(2)}) collective-permute-start(bf16[128,1024]{1,0:T(8,128)(2,1)S(1)} %fusion.72), channel_id=1, source_target_pairs={{0,2},{1,3},{2,0},{3,1},{4,6},{5,7},{6,4},{7,5},{8,10},{9,11},{10,... | collective-permute-start | bytes 786440 | tf_op jit(solution)/shard_map/ppermute | solution.py:49
  283.5 31.5 %collective-permute-start.46 = (bf16[512,1024]{1,0:T(8,128)(2,1)}, bf16[512,1024]{1,0:T(8,128)(2,1)S(1)}, u32[]{:S(2)}, u32[]{:S(2)}) collective-permute-start(bf16[512,1024]{1,0:T(8,128)(2,1)} %get-tuple-element.134), channel_id=1, source_target_pairs={{0,2},{1,3},{2,0},{3,1},{4,6},{5,7},{6,4},{7,5},{8,10},{9,11},{10,... | collective-permute-start | bytes 3145736 | tf_op jit(solution)/shard_map/ppermute | solution.py:49
  284.0 31.0 %collective-permute-start.47 = (bf16[512,1024]{1,0:T(8,128)(2,1)S(1)}, bf16[512,1024]{1,0:T(8,128)(2,1)S(1)}, u32[]{:S(2)}, u32[]{:S(2)}) collective-permute-start(bf16[512,1024]{1,0:T(8,128)(2,1)S(1)} %add_convert_fusion.2), channel_id=1, source_target_pairs={{0,1},{1,0},{2,3},{3,2},{4,5},{5,4},{6,7},{7,6},{8,9},{9,8},{10,11... | collective-permute-start | bytes 3145736 | tf_op jit(solution)/shard_map/ppermute | solution.py:49
  291.1 23.8 %collective-permute-start.48 = (bf16[512,256]{1,0:T(8,128)(2,1)S(1)}, bf16[512,256]{1,0:T(8,128)(2,1)S(1)}, u32[]{:S(2)}, u32[]{:S(2)}) collective-permute-start(bf16[512,256]{1,0:T(8,128)(2,1)S(1)} %get-tuple-element.283), channel_id=1, source_target_pairs={{0,12},{1,13},{2,14},{3,15},{4,0},{5,1},{6,2},{7,3},{8,4},{9,5},{1... | collective-permute-start | bytes 786440 | tf_op jit(solution)/shard_map/ppermute | solution.py:49
  291.2 23.7 %collective-permute-start.49 = (bf16[512,256]{1,0:T(8,128)(2,1)S(1)}, bf16[512,256]{1,0:T(8,128)(2,1)S(1)}, u32[]{:S(2)}, u32[]{:S(2)}) collective-permute-start(bf16[512,256]{1,0:T(8,128)(2,1)S(1)} %get-tuple-element.282), channel_id=1, source_target_pairs={{0,8},{1,9},{2,10},{3,11},{4,12},{5,13},{6,14},{7,15},{8,0},{9,1},... | collective-permute-start | bytes 786440 | tf_op jit(solution)/shard_map/ppermute | solution.py:49
  292.4 22.6 %collective-permute-start.50 = (bf16[512,256]{1,0:T(8,128)(2,1)S(1)}, bf16[512,256]{1,0:T(8,128)(2,1)S(1)}, u32[]{:S(2)}, u32[]{:S(2)}) collective-permute-start(bf16[512,256]{1,0:T(8,128)(2,1)S(1)} %get-tuple-element.281), channel_id=1, source_target_pairs={{0,4},{1,5},{2,6},{3,7},{4,8},{5,9},{6,10},{7,11},{8,12},{9,13},{1... | collective-permute-start | bytes 786440 | tf_op jit(solution)/shard_map/ppermute | solution.py:49
  334.0 25.4 %collective-permute-start.60 = (bf16[512,1024]{1,0:T(8,128)(2,1)}, bf16[512,1024]{1,0:T(8,128)(2,1)S(1)}, u32[]{:S(2)}, u32[]{:S(2)}) collective-permute-start(bf16[512,1024]{1,0:T(8,128)(2,1)} %add_convert_fusion.1), channel_id=1, source_target_pairs={{0,1},{1,0},{2,3},{3,2},{4,5},{5,4},{6,7},{7,6},{8,9},{9,8},{10,11... | collective-permute-start | bytes 3145736 | tf_op jit(solution)/shard_map/ppermute | solution.py:49
  354.7 22.4 %collective-permute-start.59 = (bf16[512,256]{1,0:T(8,128)(2,1)S(1)}, bf16[512,256]{1,0:T(8,128)(2,1)S(1)}, u32[]{:S(2)}, u32[]{:S(2)}) collective-permute-start(bf16[512,256]{1,0:T(8,128)(2,1)S(1)} %get-tuple-element.278), channel_id=1, source_target_pairs={{0,4},{1,5},{2,6},{3,7},{4,8},{5,9},{6,10},{7,11},{8,12},{9,13},{1... | collective-permute-start | bytes 786440 | tf_op jit(solution)/shard_map/ppermute | solution.py:49
  (112 other events, 1185.3 us)
